TPU v7x, 32 devices: a whole 2x2x4 slice. The times are simulated.
32 devices in a mesh: dp: 8 (over z, y), seq: 4 (over x, core).
Axes of the slice: x: 2, y: 2, z: 4, core: 2. Of those that a mesh axis runs over, the one named last changes fastest.
Arguments:
- tokens: bfloat16 [24, 640, 1024], P('dp', 'seq'), may hold values from -6 to 6
- cotangent: bfloat16 [24, 640, 1024], P('dp', 'seq'), may hold values from -6 to 6
- token_mask: int32 [24, 640], P('dp'), may hold values from 0 to 1, as said below
- w_qkv: bfloat16 [1024, 3072], P(('dp', 'seq')), may hold values from -0.1875 to 0.1875
- w_out: bfloat16 [1024, 1024], P(('dp', 'seq')), may hold values from -1.5 to 1.5
- w_fc1: bfloat16 [1024, 4096], P(('dp', 'seq')), may hold values from -0.1875 to 0.1875
- w_fc2: bfloat16 [4096, 1024], P(('dp', 'seq')), may hold values from -0.09375 to 0.09375
- b_q: bfloat16 [1024], P(('dp', 'seq')), may hold values from -3 to 3
- b_v: bfloat16 [1024], P(('dp', 'seq')), may hold values from -3 to 3
- b_out: bfloat16 [1024], P(('dp', 'seq')), may hold values from -3 to 3
- b_fc1: bfloat16 [4096], P(('dp', 'seq')), may hold values from -3 to 3
- b_fc2: bfloat16 [1024], P(('dp', 'seq')), may hold values from -3 to 3
- ln1_gain: bfloat16 [1024], P(('dp', 'seq')), may hold values from 0.5 to 1.5
- ln1_shift: bfloat16 [1024], P(('dp', 'seq')), may hold values from -3 to 3
- ln2_gain: bfloat16 [1024], P(('dp', 'seq')), may hold values from 0.5 to 1.5
- ln2_shift: bfloat16 [1024], P(('dp', 'seq')), may hold values from -3 to 3
Outputs:
- out_tokens: bfloat16 [24, 640, 1024], P('dp', 'seq')
- grad_tokens: float32 [24, 640, 1024], P('dp', 'seq')
- grad_w_qkv: float32 [1024, 3072], P(('dp', 'seq'))
- grad_w_out: float32 [1024, 1024], P(('dp', 'seq'))
- grad_w_fc1: float32 [1024, 4096], P(('dp', 'seq'))
- grad_w_fc2: float32 [4096, 1024], P(('dp', 'seq'))
- grad_b_q: float32 [1024], P(('dp', 'seq'))
- grad_b_v: float32 [1024], P(('dp', 'seq'))
- grad_b_out: float32 [1024], P(('dp', 'seq'))
- grad_b_fc1: float32 [4096], P(('dp', 'seq'))
- grad_b_fc2: float32 [1024], P(('dp', 'seq'))
- grad_ln1_gain: float32 [1024], P(('dp', 'seq'))
- grad_ln1_shift: float32 [1024], P(('dp', 'seq'))
- grad_ln2_gain: float32 [1024], P(('dp', 'seq'))
- grad_ln2_shift: float32 [1024], P(('dp', 'seq'))
Inputs may be any that keep to these rules, and one draw needn't show every extreme that they name: `token_mask`: every row is either all zeros (an empty slot) or holds exactly 577 ones at positions drawn anew for each image; each aligned block of 3 rows (the slots of one dp group) holds between (3 + 1) // 2 and 3 images, and some block holds 3.
All inputs are finite; a program needn't handle non-finite values.
Results may differ from a plain program's by a relative error of at most 0.013.
Values may be sent and summed in bfloat16 or wider, within the bound.
No kernel may reach another device: no remote copies, remote signals or barrier semaphores. Data moves between devices by JAX's collectives and lax.ppermute only.
A program may use at most 192 MiB of HBM per device.

v0:
```python
import math

import jax
import jax.numpy as jnp
from jax import lax
from jax.sharding import PartitionSpec as P

HEAD_DIM = 64


EPS = 1e-06
MASKED = -1000000000.0


def layer_norm(values, gain, shift):
    average = jnp.mean(values, axis=-1, keepdims=True)
    centred = values - average
    spread = jnp.mean(centred * centred, axis=-1, keepdims=True)
    return centred * lax.rsqrt(spread + EPS) * gain + shift


def exact_gelu(values):
    return jax.nn.gelu(values, approximate=False)


def gather_params(mat_qkv, mat_out, mat_fc1, mat_fc2, vector_blob):
    return (
        lax.all_gather(mat_qkv, ("dp", "seq"), axis=0, tiled=True),
        lax.all_gather(mat_out, ("dp", "seq"), axis=0, tiled=True),
        lax.all_gather(mat_fc1, ("dp", "seq"), axis=0, tiled=True),
        lax.all_gather(mat_fc2, ("dp", "seq"), axis=0, tiled=True),
        lax.all_gather(vector_blob, ("dp", "seq"), axis=0, tiled=True),
    )


def scatter_grads(mat_qkv, mat_out, mat_fc1, mat_fc2, vector_blob):
    return (
        lax.psum_scatter(mat_qkv, ("dp", "seq"), scatter_dimension=0, tiled=True),
        lax.psum_scatter(mat_out, ("dp", "seq"), scatter_dimension=0, tiled=True),
        lax.psum_scatter(mat_fc1, ("dp", "seq"), scatter_dimension=0, tiled=True),
        lax.psum_scatter(mat_fc2, ("dp", "seq"), scatter_dimension=0, tiled=True),
        lax.psum_scatter(vector_blob, ("dp", "seq"), scatter_dimension=0, tiled=True),
    )


def split_vectors(vector_blob, lengths, groups):
    table = vector_blob.reshape(groups, -1)
    pieces = []
    offset = 0
    for length in lengths:
        pieces.append(table[:, offset : offset + length].reshape(-1))
        offset += length
    return pieces


def pack_terms(vectors, groups):
    return jnp.concatenate([vector.reshape(groups, -1) for vector in vectors], axis=1).reshape(-1)


def head_scores(queries, keys, keep):
    local_len = queries.shape[0]
    full_len = keys.shape[0]
    heads = queries.shape[1] // HEAD_DIM
    q_heads = queries.reshape(local_len, heads, HEAD_DIM)
    k_heads = keys.reshape(full_len, heads, HEAD_DIM)
    scores = jnp.einsum("qhd,khd->hqk", q_heads, k_heads, preferred_element_type=jnp.float32) * (
        1.0 / math.sqrt(HEAD_DIM)
    )
    return (jnp.where(keep[None, None, :], scores, MASKED), q_heads, k_heads)


def attend_forward(item):
    queries, keys, values, keep = item
    local_len = queries.shape[0]
    masked, q_heads, k_heads = head_scores(queries, keys, keep)
    v_heads = values.reshape(keys.shape[0], -1, HEAD_DIM)
    largest = jnp.max(masked, axis=-1, keepdims=True)
    raised = jnp.exp(masked - largest)
    totals = jnp.sum(raised, axis=-1, keepdims=True)
    chance = (raised / totals).astype(jnp.bfloat16)
    mixed = jnp.einsum("hqk,khd->qhd", chance, v_heads, preferred_element_type=jnp.float32)
    return (mixed.reshape(local_len, -1), (largest + jnp.log(totals))[..., 0])


def attend_backward(item):
    queries, keys, values, keep, log_total, grad_mixed = item
    local_len = queries.shape[0]
    full_len = keys.shape[0]
    scale_factor = 1.0 / math.sqrt(HEAD_DIM)
    masked, q_heads, k_heads = head_scores(queries, keys, keep)
    v_heads = values.reshape(full_len, -1, HEAD_DIM)
    chance = jnp.exp(masked - log_total[..., None])
    chance_low = chance.astype(jnp.bfloat16)
    g_heads = grad_mixed.reshape(local_len, -1, HEAD_DIM)
    grad_chance = jnp.einsum("qhd,khd->hqk", g_heads, v_heads, preferred_element_type=jnp.float32)
    inner = jnp.sum(chance * grad_chance, axis=-1, keepdims=True)
    grad_scores = jnp.where(keep[None, None, :], chance * (grad_chance - inner), 0.0).astype(
        jnp.bfloat16
    )
    grad_queries = (
        jnp.einsum("hqk,khd->qhd", grad_scores, k_heads, preferred_element_type=jnp.float32)
        * scale_factor
    )
    grad_keys = (
        jnp.einsum("hqk,qhd->khd", grad_scores, q_heads, preferred_element_type=jnp.float32)
        * scale_factor
    )
    grad_values = jnp.einsum(
        "hqk,qhd->khd", chance_low, g_heads, preferred_element_type=jnp.float32
    )
    return (
        grad_queries.reshape(local_len, -1).astype(jnp.bfloat16),
        grad_keys.reshape(full_len, -1),
        grad_values.reshape(full_len, -1),
    )


def shards(
    tokens,
    cotangent,
    token_mask,
    w_qkv,
    w_out,
    w_fc1,
    w_fc2,
    b_q,
    b_v,
    b_out,
    b_fc1,
    b_fc2,
    ln1_gain,
    ln1_shift,
    ln2_gain,
    ln2_shift,
):
    groups = lax.axis_size("dp") * lax.axis_size("seq")
    slots, local_len, width = tokens.shape
    vector_shards = (b_q, b_v, b_out, b_fc1, b_fc2, ln1_gain, ln1_shift, ln2_gain, ln2_shift)
    lengths = [vector.shape[0] for vector in vector_shards]
    vector_blob = jnp.concatenate(vector_shards)
    gathered = gather_params(w_qkv, w_out, w_fc1, w_fc2, vector_blob)
    full_qkv, full_out, full_fc1, full_fc2 = (gathered[0], gathered[1], gathered[2], gathered[3])
    vectors = [vector.astype(jnp.float32) for vector in split_vectors(gathered[4], lengths, groups)]
    bias_q, bias_v, bias_out, bias_fc1, bias_fc2, gain_one, shift_one, gain_two, shift_two = vectors
    offset = lax.axis_index("seq") * local_len
    keep = token_mask > 0
    local_keep = lax.dynamic_slice_in_dim(token_mask, offset, local_len, 1) > 0
    valid = local_keep.reshape(-1, 1).astype(jnp.float32)
    rows = tokens.reshape(-1, width).astype(jnp.float32)
    normed_one, norm_one_pull = jax.vjp(layer_norm, rows, gain_one, shift_one)
    normed_low = normed_one.astype(jnp.bfloat16)
    qkv_bias = jnp.concatenate([bias_q, jnp.zeros_like(bias_out), bias_v])
    projected = (
        jnp.dot(normed_low, full_qkv, preferred_element_type=jnp.float32) + qkv_bias
    ).astype(jnp.bfloat16)
    queries = projected[:, :width].reshape(slots, local_len, width)
    keys_local = projected[:, width : 2 * width].reshape(slots, local_len, width)
    values_local = projected[:, 2 * width :].reshape(slots, local_len, width)
    keys_full, values_full = (
        lax.all_gather(keys_local, "seq", axis=1, tiled=True),
        lax.all_gather(values_local, "seq", axis=1, tiled=True),
    )
    mixed, log_total = lax.map(attend_forward, (queries, keys_full, values_full, keep))
    attended = mixed.reshape(-1, width).astype(jnp.bfloat16)
    middle = rows + jnp.dot(attended, full_out, preferred_element_type=jnp.float32) + bias_out
    normed_two, norm_two_pull = jax.vjp(layer_norm, middle, gain_two, shift_two)
    second_low = normed_two.astype(jnp.bfloat16)
    hidden = jnp.dot(second_low, full_fc1, preferred_element_type=jnp.float32) + bias_fc1
    activated, gelu_pull = jax.vjp(exact_gelu, hidden)
    activated_low = activated.astype(jnp.bfloat16)
    result = (
        middle + jnp.dot(activated_low, full_fc2, preferred_element_type=jnp.float32) + bias_fc2
    ) * valid
    out_tokens = result.astype(jnp.bfloat16).reshape(slots, local_len, width)
    again = gather_params(w_qkv, w_out, w_fc1, w_fc2, vector_blob)
    back_qkv, back_out, back_fc1, back_fc2 = (again[0], again[1], again[2], again[3])
    grad_y = cotangent.reshape(-1, width).astype(jnp.float32) * valid
    grad_y_low = grad_y.astype(jnp.bfloat16)
    grad_w_fc2 = jnp.einsum(
        "rf,rd->fd", activated_low, grad_y_low, preferred_element_type=jnp.float32
    )
    grad_b_fc2 = jnp.sum(grad_y, axis=0)
    grad_activated = jnp.einsum(
        "rd,fd->rf", grad_y_low, back_fc2, preferred_element_type=jnp.float32
    )
    grad_hidden = gelu_pull(grad_activated)[0].astype(jnp.bfloat16)
    grad_w_fc1 = jnp.einsum(
        "rd,rf->df", second_low, grad_hidden, preferred_element_type=jnp.float32
    )
    grad_b_fc1 = jnp.sum(grad_hidden.astype(jnp.float32), axis=0)
    grad_second = jnp.einsum("rf,df->rd", grad_hidden, back_fc1, preferred_element_type=jnp.float32)
    grad_middle_norm, grad_gain_two, grad_shift_two = norm_two_pull(grad_second)
    grad_middle = grad_y + grad_middle_norm
    grad_branch = grad_middle.astype(jnp.bfloat16)
    grad_w_out = jnp.einsum("re,rd->ed", attended, grad_branch, preferred_element_type=jnp.float32)
    grad_b_out = jnp.sum(grad_branch.astype(jnp.float32), axis=0)
    grad_attended = jnp.einsum(
        "rd,ed->re", grad_branch, back_out, preferred_element_type=jnp.float32
    ).astype(jnp.bfloat16)
    grad_attended = grad_attended.reshape(slots, local_len, width)
    grad_queries, key_terms, value_terms = lax.map(
        attend_backward, (queries, keys_full, values_full, keep, log_total, grad_attended)
    )
    key_sums, value_sums = (
        lax.psum_scatter(
            key_terms.astype(jnp.bfloat16), "seq", scatter_dimension=1, tiled=True
        ).astype(jnp.float32),
        lax.psum_scatter(
            value_terms.astype(jnp.bfloat16), "seq", scatter_dimension=1, tiled=True
        ).astype(jnp.float32),
    )
    grad_qkv = jnp.concatenate(
        [grad_queries, key_sums.astype(jnp.bfloat16), value_sums.astype(jnp.bfloat16)], axis=-1
    ).reshape(-1, 3 * width)
    grad_w_qkv = jnp.einsum("rd,re->de", normed_low, grad_qkv, preferred_element_type=jnp.float32)
    grad_qkv_wide = jnp.sum(grad_qkv.astype(jnp.float32), axis=0)
    grad_b_q = grad_qkv_wide[:width]
    grad_b_v = grad_qkv_wide[2 * width :]
    grad_normed = jnp.einsum("re,de->rd", grad_qkv, back_qkv, preferred_element_type=jnp.float32)
    grad_rows_norm, grad_gain_one, grad_shift_one = norm_one_pull(grad_normed)
    grad_tokens = (grad_middle + grad_rows_norm).reshape(slots, local_len, width)
    vector_terms = pack_terms(
        (
            grad_b_q,
            grad_b_v,
            grad_b_out,
            grad_b_fc1,
            grad_b_fc2,
            grad_gain_one,
            grad_shift_one,
            grad_gain_two,
            grad_shift_two,
        ),
        groups,
    )
    summed = scatter_grads(grad_w_qkv, grad_w_out, grad_w_fc1, grad_w_fc2, vector_terms)
    owned = split_vectors(summed[4], lengths, 1)
    return (
        out_tokens,
        grad_tokens,
        summed[0],
        summed[1],
        summed[2],
        summed[3],
        owned[0],
        owned[1],
        owned[2],
        owned[3],
        owned[4],
        owned[5],
        owned[6],
        owned[7],
        owned[8],
    )


def solution(mesh):
    in_specs = (
        P("dp", "seq", None),
        P("dp", "seq", None),
        P("dp", None),
        P(("dp", "seq"), None),
        P(("dp", "seq"), None),
        P(("dp", "seq"), None),
        P(("dp", "seq"), None),
        P(("dp", "seq")),
        P(("dp", "seq")),
        P(("dp", "seq")),
        P(("dp", "seq")),
        P(("dp", "seq")),
        P(("dp", "seq")),
        P(("dp", "seq")),
        P(("dp", "seq")),
        P(("dp", "seq")),
    )
    out_specs = (
        P("dp", "seq", None),
        P("dp", "seq", None),
        P(("dp", "seq"), None),
        P(("dp", "seq"), None),
        P(("dp", "seq"), None),
        P(("dp", "seq"), None),
        P(("dp", "seq")),
        P(("dp", "seq")),
        P(("dp", "seq")),
        P(("dp", "seq")),
        P(("dp", "seq")),
        P(("dp", "seq")),
        P(("dp", "seq")),
        P(("dp", "seq")),
        P(("dp", "seq")),
    )
    return jax.shard_map(shards, mesh=mesh, in_specs=in_specs, out_specs=out_specs, check_vma=False)
```

profile of v0, /device:TPU:0, one launch (start us, length us, event | category | flops | bytes accessed | tf_op | source)
XLA Modules:
  0.0 1393.9 jit_solution(5962977956944969666)
XLA Ops:
  14.1 43.5 %all-gather = bf16[32,1,384]{2,1,0:T(2,128)(2,1)S(1)} all-gather(bf16[1,1,384]{2,1,0:T(2,128)(2,1)S(1)} %reshape.436), channel_id=1, replica_groups=mesh['dp'=8,'seq'=4] {'dp','seq'}, dimensions={0}, use_global_device_ids=true | all-gather | bytes 25344 | tf_op jit(solution)/shard_map/all_gather | solution.py:32
  64.7 18.5 %all-gather.8.cloned.1.call-done = bf16[1024,3072]{1,0:T(8,128)(2,1)} async-done(((bf16[32,3072]{1,0:T(8,128)(2,1)}), bf16[1024,3072]{1,0:T(8,128)(2,1)}) %all-gather.8.cloned.1.call-update) | async-done | bytes 6291472 | tf_op jit(solution)/shard_map/all_gather | solution.py:28
  83.2 6.4 add_convert_fusion.1
  97.3 25.6 %all-gather.10.cloned.1.call-done = bf16[3,640,1024]{2,1,0:T(8,128)(2,1)} async-done(((bf16[3,160,1024]{2,1,0:T(8,128)(2,1)}), bf16[3,640,1024]{2,1,0:T(8,128)(2,1)}) %all-gather.10.cloned.1.call-update) | async-done | bytes 3932176 | tf_op jit(solution)/shard_map/all_gather | solution.py:161
  123.0 6.4 copy.48
  129.4 28.8 %all-gather.12.cloned.1.call-done = bf16[3,640,1024]{2,1,0:T(8,128)(2,1)} async-done(((bf16[3,160,1024]{2,1,0:T(8,128)(2,1)}), bf16[3,640,1024]{2,1,0:T(8,128)(2,1)}) %all-gather.12.cloned.1.call-update) | async-done | bytes 3932176 | tf_op jit(solution)/shard_map/all_gather | solution.py:160
  158.1 6.3 copy.50
  164.4 26.5 %while.26 = (s32[]{:T(128)}, bf16[3,160,1024]{2,1,0:T(8,128)(2,1)S(1)}, f32[3,16,160]{2,1,0:T(8,128)S(1)}, bf16[3,640,1024]{1,2,0:T(8,128)(2,1)}, pred[3,640]{1,...) while((s32[]{:T(128)}, ...), condition=%wide.region_5.6_spmd, body=%wide.region_2.5_spmd.sunk | while | flops 439088640 | bytes 30250224 | solution.py:163
  190.9 26.4 %all-gather.14.cloned.1.call-done = bf16[1024,1024]{1,0:T(8,128)(2,1)} async-done(((bf16[32,1024]{1,0:T(8,128)(2,1)}), bf16[1024,1024]{1,0:T(8,128)(2,1)}) %all-gather.14.cloned.1.call-update) | async-done | bytes 2097168 | tf_op jit(solution)/shard_map/all_gather | solution.py:29
  221.0 75.3 %all-gather.16.cloned.1.call-done = bf16[1024,4096]{1,0:T(8,128)(2,1)} async-done(((bf16[32,4096]{1,0:T(8,128)(2,1)}), bf16[1024,4096]{1,0:T(8,128)(2,1)}) %all-gather.16.cloned.1.call-update) | async-done | bytes 8388624 | tf_op jit(solution)/shard_map/all_gather | solution.py:30
  296.3 9.9 fusion.88
  306.3 68.9 %all-gather.18.cloned.1.call-done = bf16[4096,1024]{1,0:T(8,128)(2,1)} async-done(((bf16[128,1024]{1,0:T(8,128)(2,1)}), bf16[4096,1024]{1,0:T(8,128)(2,1)}) %all-gather.18.cloned.1.call-update) | async-done | bytes 8388624 | tf_op jit(solution)/shard_map/all_gather | solution.py:31
  375.1 27.1 %convert_reduce_fusion = (f32[4096]{0:T(1024)}, bf16[480,4096]{1,0:T(8,128)(2,1)S(1)}, f32[480,4096]{1,0:T(8,128)}) fusion(f32[480,4096]{1,0:T(8,128)} %fusion.88, f32[4096]{0:T(1024)S(1)} %fusion.83, bf16[480,1024]{1,0:T(8,128)(2,1)S(1)} %copy-done.18, bf16[4096,1024]{1,0:T(8,128)(2,1)} %all-gather.18.cloned.1.call-done), kind=kOutput, calls=%fused_computation.59 | convolution fusion | flops 4173983744 | bytes 29065216 | tf_op jit(solution)/shard_map/rd,fd->rf/dot_general | solution.py:183
  411.9 213.7 %while.27 = (s32[]{:T(128)}, bf16[3,160,1024]{2,1,0:T(8,128)(2,1)}, bf16[3,640,1024]{2,1,0:T(8,128)(2,1)}, bf16[3,640,1024]{2,1,0:T(8,128)(2,1)}, bf16[3,640,102...) while((s32[]{:T(128)}, bf16[3,160,1024]{2,1,0:T(8,128)(2,1)}, ...), condition=%wide.region_12.13_spmd, body=%wide.region_10.12_spmd.sunk | while | flops 1092819200 | bytes 73127184 | solution.py:201
  424.8 22.9 %fusion.168 = bf16[16,64,160]{2,1,0:T(8,128)(2,1)S(1)} fusion(bf16[640,16,64]{0,2,1:T(8,128)(2,1)S(1)} %bitcast.156, f32[16,160,640]{2,1,0:T(8,128)} %fusion.166, f32[16,160,640]{2,1,0:T(8,128)} %fusion.167, f32[16,160]{1,0:T(8,128)S(1)} %dynamic-slice_bitcast_fusion.2, pred[640]{0:T(1024)(128)(4,1)S(1)} %dynamic-slice_reduce_fusion.5), kind=kOutput, calls=%fused_computation.39.clone.1 | convolution fusion | flops 228068480 | bytes 14756480 | tf_op jit(solution)/shard_map/while/body/eval_jaxpr/hqk,khd->qhd/dot_general | solution.py:101
  455.9 23.9 %fusion.170 = bf16[16,64,640]{2,1,0:T(8,128)(2,1)} fusion(bf16[160,16,64]{0,2,1:T(8,128)(2,1)S(1)} %bitcast.161, f32[16,160,640]{2,1,0:T(8,128)} %fusion.166, f32[16,160,640]{2,1,0:T(8,128)} %fusion.167, f32[16,160]{1,0:T(8,128)S(1)} %dynamic-slice_bitcast_fusion.2, pred[640]{0:T(1024)(128)(4,1)S(1)} %dynamic-slice_reduce_fusion.5), kind=kOutput, calls=%fused_computation.37.clone.1 | convolution fusion | flops 229051520 | bytes 14756480 | tf_op jit(solution)/shard_map/while/body/eval_jaxpr/hqk,qhd->khd/dot_general | solution.py:105
  496.0 22.9 %fusion.168 = bf16[16,64,160]{2,1,0:T(8,128)(2,1)S(1)} fusion(bf16[640,16,64]{0,2,1:T(8,128)(2,1)S(1)} %bitcast.156, f32[16,160,640]{2,1,0:T(8,128)} %fusion.166, f32[16,160,640]{2,1,0:T(8,128)} %fusion.167, f32[16,160]{1,0:T(8,128)S(1)} %dynamic-slice_bitcast_fusion.2, pred[640]{0:T(1024)(128)(4,1)S(1)} %dynamic-slice_reduce_fusion.5), kind=kOutput, calls=%fused_computation.39.clone.1 | convolution fusion | flops 228068480 | bytes 14756480 | tf_op jit(solution)/shard_map/while/body/eval_jaxpr/hqk,khd->qhd/dot_general | solution.py:101
  527.1 23.9 %fusion.170 = bf16[16,64,640]{2,1,0:T(8,128)(2,1)} fusion(bf16[160,16,64]{0,2,1:T(8,128)(2,1)S(1)} %bitcast.161, f32[16,160,640]{2,1,0:T(8,128)} %fusion.166, f32[16,160,640]{2,1,0:T(8,128)} %fusion.167, f32[16,160]{1,0:T(8,128)S(1)} %dynamic-slice_bitcast_fusion.2, pred[640]{0:T(1024)(128)(4,1)S(1)} %dynamic-slice_reduce_fusion.5), kind=kOutput, calls=%fused_computation.37.clone.1 | convolution fusion | flops 229051520 | bytes 14756480 | tf_op jit(solution)/shard_map/while/body/eval_jaxpr/hqk,qhd->khd/dot_general | solution.py:105
  567.2 22.9 %fusion.168 = bf16[16,64,160]{2,1,0:T(8,128)(2,1)S(1)} fusion(bf16[640,16,64]{0,2,1:T(8,128)(2,1)S(1)} %bitcast.156, f32[16,160,640]{2,1,0:T(8,128)} %fusion.166, f32[16,160,640]{2,1,0:T(8,128)} %fusion.167, f32[16,160]{1,0:T(8,128)S(1)} %dynamic-slice_bitcast_fusion.2, pred[640]{0:T(1024)(128)(4,1)S(1)} %dynamic-slice_reduce_fusion.5), kind=kOutput, calls=%fused_computation.39.clone.1 | convolution fusion | flops 228068480 | bytes 14756480 | tf_op jit(solution)/shard_map/while/body/eval_jaxpr/hqk,khd->qhd/dot_general | solution.py:101
  598.3 23.9 %fusion.170 = bf16[16,64,640]{2,1,0:T(8,128)(2,1)} fusion(bf16[160,16,64]{0,2,1:T(8,128)(2,1)S(1)} %bitcast.161, f32[16,160,640]{2,1,0:T(8,128)} %fusion.166, f32[16,160,640]{2,1,0:T(8,128)} %fusion.167, f32[16,160]{1,0:T(8,128)S(1)} %dynamic-slice_bitcast_fusion.2, pred[640]{0:T(1024)(128)(4,1)S(1)} %dynamic-slice_reduce_fusion.5), kind=kOutput, calls=%fused_computation.37.clone.1 | convolution fusion | flops 229051520 | bytes 14756480 | tf_op jit(solution)/shard_map/while/body/eval_jaxpr/hqk,qhd->khd/dot_general | solution.py:105
  632.8 34.4 %reduce-scatter.7.cloned.1.call-done = bf16[3,160,1024]{2,1,0:T(8,128)(2,1)} async-done(((bf16[3,640,1024]{2,1,0:T(8,128)(2,1)}), bf16[3,160,1024]{2,1,0:T(8,128)(2,1)}) %reduce-scatter.7.cloned.1.call-update) | async-done | bytes 983056 | tf_op jit(solution)/shard_map/reduce_scatter | solution.py:205
  669.5 43.3 %reduce-scatter.9.cloned.1.call-done = bf16[3,160,1024]{2,1,0:T(8,128)(2,1)} async-done(((bf16[3,640,1024]{2,1,0:T(8,128)(2,1)}), bf16[3,160,1024]{2,1,0:T(8,128)(2,1)}) %reduce-scatter.9.cloned.1.call-update) | async-done | bytes 983056 | tf_op jit(solution)/shard_map/reduce_scatter | solution.py:208
  715.2 8.4 convolution_bitcast_fusion
  725.1 10.4 fusion.87
  736.2 7.5 multiply_convert_fusion
  745.6 8.1 fusion.98
  756.4 9.9 multiply_convert_fusion.1
  778.8 40.5 %all-reduce = f32[12288]{0:T(1024)S(1)} all-reduce(f32[12288]{0:T(1024)S(1)} %reshape.413), channel_id=8, replica_groups=mesh['dp'=8,'seq'=4] {'dp','seq'}, use_global_device_ids=true, to_apply=%region_29.30.clone | all-reduce | flops 12288 | bytes 98304
  823.9 33.0 %reduce-scatter.13.cloned.1.call-done = f32[32,1024]{1,0:T(8,128)} async-done(((f32[1024,1024]{1,0:T(8,128)}), f32[32,1024]{1,0:T(8,128)}) %reduce-scatter.13.cloned.1.call-update) | async-done | bytes 131088 | tf_op jit(solution)/shard_map/reduce_scatter | solution.py:39
  856.9 157.7 %reduce-scatter.11.cloned.1.call-done = f32[32,3072]{1,0:T(8,128)} async-done(((f32[1024,3072]{1,0:T(8,128)}), f32[32,3072]{1,0:T(8,128)}) %reduce-scatter.11.cloned.1.call-update) | async-done | bytes 393232 | tf_op jit(solution)/shard_map/reduce_scatter | solution.py:38
  1014.6 185.1 %reduce-scatter.15.cloned.1.call-done = f32[32,4096]{1,0:T(8,128)} async-done(((f32[1024,4096]{1,0:T(8,128)}), f32[32,4096]{1,0:T(8,128)}) %reduce-scatter.15.cloned.1.call-update) | async-done | bytes 524304 | tf_op jit(solution)/shard_map/reduce_scatter | solution.py:40
  1199.7 187.1 %reduce-scatter.17.cloned.1.call-done = f32[128,1024]{1,0:T(8,128)} async-done(((f32[4096,1024]{1,0:T(8,128)}), f32[128,1024]{1,0:T(8,128)}) %reduce-scatter.17.cloned.1.call-update) | async-done | bytes 524304 | tf_op jit(solution)/shard_map/reduce_scatter | solution.py:41
  (276 shorter events, 169.7 us)
Async XLA Ops:
  7.2 76.0 %all-gather.8.cloned.1.call-start = ((), (), s32[]{:S(2)}) async-start(), calls=%async_computation.6 | async-start | bytes 6488064 | tf_op jit(solution)/shard_map/all_gather | solution.py:28
  7.9 115.0 %all-gather.10.cloned.1.call-start = ((), (), s32[]{:S(2)}) async-start(), calls=%async_computation.7 | async-start | bytes 4915200 | tf_op jit(solution)/shard_map/all_gather | solution.py:161
  60.3 29.3 %copy-start.44 = (f32[1024]{0:T(1024)}, f32[1024]{0:T(1024)S(1)}, u32[]{:S(2)}) copy-start(f32[1024]{0:T(1024)S(1)} %reshape.426) | copy-start | bytes 12292
  62.7 26.9 %copy-start.42 = (f32[480]{0:T(512)}, f32[480]{0:T(512)S(1)}, u32[]{:S(2)}) copy-start(f32[480]{0:T(512)S(1)} %rsqrt.23) | copy-start | bytes 5764
  91.3 66.8 %all-gather.12.cloned.1.call-start = ((), (), s32[]{:S(2)}) async-start(), calls=%async_computation.8 | async-start | bytes 4915200 | tf_op jit(solution)/shard_map/all_gather | solution.py:160
  92.1 125.2 %all-gather.14.cloned.1.call-start = ((), (), s32[]{:S(2)}) async-start(), calls=%async_computation.9 | async-start | bytes 2162688 | tf_op jit(solution)/shard_map/all_gather | solution.py:29
  92.6 203.7 %all-gather.16.cloned.1.call-start = ((), (), s32[]{:S(2)}) async-start(), calls=%async_computation.10 | async-start | bytes 8650752 | tf_op jit(solution)/shard_map/all_gather | solution.py:30
  93.2 281.9 %all-gather.18.cloned.1.call-start = ((), (), s32[]{:S(2)}) async-start(), calls=%async_computation.11 | async-start | bytes 8650752 | tf_op jit(solution)/shard_map/all_gather | solution.py:31
  93.8 573.4 %reduce-scatter.7.cloned.1.call-start = ((), (), s32[]{:S(2)}) async-start(), calls=%async_computation.12 | async-start | bytes 4915200 | tf_op jit(solution)/shard_map/reduce_scatter | solution.py:205
  94.1 202.2 %copy-start.47 = (f32[1024]{0:T(1024)}, f32[1024]{0:T(1024)S(1)}, u32[]{:S(2)}) copy-start(f32[1024]{0:T(1024)S(1)} %reshape.431) | copy-start | bytes 12292
  94.4 35.0 %copy-start.26 = (f32[3,160]{1,0:T(4,128)}, f32[3,160]{1,0:T(4,128)S(1)}, u32[]{:S(2)}) copy-start(f32[3,160]{1,0:T(4,128)S(1)} %fusion.84) | copy-start | bytes 5764
  94.4 34.9 %copy-start.28 = (f32[480]{0:T(512)}, f32[480]{0:T(512)S(1)}, u32[]{:S(2)}) copy-start(f32[480]{0:T(512)S(1)} %reshape.434) | copy-start | bytes 5764
  94.5 280.6 %copy-start.22 = (f32[4096]{0:T(1024)}, f32[4096]{0:T(1024)S(1)}, u32[]{:S(2)}) copy-start(f32[4096]{0:T(1024)S(1)} %fusion.83) | copy-start | bytes 49156
  129.3 35.0 %copy-start.15 = (bf16[3,160,1024]{2,1,0:T(8,128)(2,1)S(1)}, bf16[3,160,1024]{2,1,0:T(8,128)(2,1)}, u32[]{:S(2)}) copy-start(bf16[3,160,1024]{2,1,0:T(8,128)(2,1)} %custom-call.1) | copy-start | bytes 2949124
  164.4 52.9 %copy-start.4 = (bf16[3,160,1024]{2,1,0:T(8,128)(2,1)S(1)}, bf16[3,160,1024]{2,1,0:T(8,128)(2,1)}, u32[]{:S(2)}) copy-start(bf16[3,160,1024]{2,1,0:T(8,128)(2,1)} %param.20) | copy-start | bytes 2949124
  190.9 26.4 %copy-start.16 = (bf16[3,160,1024]{2,1,0:T(8,128)(2,1)}, bf16[3,160,1024]{2,1,0:T(8,128)(2,1)S(1)}, u32[]{:S(2)}) copy-start(bf16[3,160,1024]{2,1,0:T(8,128)(2,1)S(1)} %get-tuple-element.107) | copy-start | bytes 2949124
  220.4 187.1 %copy-start.2 = (f32[480,1024]{1,0:T(8,128)}, f32[480,1024]{1,0:T(8,128)S(1)}, u32[]{:S(2)}) copy-start(f32[480,1024]{1,0:T(8,128)S(1)} %bitcast_add_fusion) | copy-start | bytes 5898244
  221.0 154.1 %copy-start.18 = (bf16[480,1024]{1,0:T(8,128)(2,1)S(1)}, bf16[480,1024]{1,0:T(8,128)(2,1)}, u32[]{:S(2)}) copy-start(bf16[480,1024]{1,0:T(8,128)(2,1)} %fusion.73) | copy-start | bytes 2949124
  375.1 27.1 %copy-start.51 = (bf16[1024,4096]{1,0:T(8,128)(2,1)S(1)}, bf16[1024,4096]{1,0:T(8,128)(2,1)}, u32[]{:S(2)}) copy-start(bf16[1024,4096]{1,0:T(8,128)(2,1)} %all-gather.16.cloned.1.call-done) | copy-start | bytes 25165828
  625.6 87.2 %reduce-scatter.9.cloned.1.call-start = ((), (), s32[]{:S(2)}) async-start(), calls=%async_computation.13 | async-start | bytes 4915200 | tf_op jit(solution)/shard_map/reduce_scatter | solution.py:208
  626.4 230.5 %reduce-scatter.13.cloned.1.call-start = ((), (), s32[]{:S(2)}) async-start(), calls=%async_computation.15 | async-start | bytes 4325376 | tf_op jit(solution)/shard_map/reduce_scatter | solution.py:39
  630.5 84.6 %copy-start.5 = (bf16[3,160,1024]{2,1,0:T(8,128)(2,1)S(1)}, bf16[3,160,1024]{2,1,0:T(8,128)(2,1)}, u32[]{:S(2)}) copy-start(bf16[3,160,1024]{2,1,0:T(8,128)(2,1)} %param.20) | copy-start | bytes 2949124
  630.5 84.6 %copy-start.25 = (f32[3,160]{1,0:T(4,128)S(1)}, f32[3,160]{1,0:T(4,128)}, u32[]{:S(2)}) copy-start(f32[3,160]{1,0:T(4,128)} %copy-done.24) | copy-start | bytes 5764
  630.5 84.6 %copy-start.39 = (f32[1024]{0:T(1024)S(1)}, f32[1024]{0:T(1024)}, u32[]{:S(2)}) copy-start(f32[1024]{0:T(1024)} %copy-done.38) | copy-start | bytes 12292
  630.6 84.6 %copy-start.45 = (f32[1024]{0:T(1024)S(1)}, f32[1024]{0:T(1024)}, u32[]{:S(2)}) copy-start(f32[1024]{0:T(1024)} %copy-done.44) | copy-start | bytes 12292
  630.6 84.6 %copy-start.46 = (f32[3,160]{1,0:T(4,128)S(1)}, f32[3,160]{1,0:T(4,128)}, u32[]{:S(2)}) copy-start(f32[3,160]{1,0:T(4,128)} %get-tuple-element.229) | copy-start | bytes 5764
  630.6 384.0 %reduce-scatter.11.cloned.1.call-start = ((), (), s32[]{:S(2)}) async-start(), calls=%async_computation.14 | async-start | bytes 12976128 | tf_op jit(solution)/shard_map/reduce_scatter | solution.py:38
  723.6 476.1 %reduce-scatter.15.cloned.1.call-start = ((), (), s32[]{:S(2)}) async-start(), calls=%async_computation.16 | async-start | bytes 17301504 | tf_op jit(solution)/shard_map/reduce_scatter | solution.py:40
  735.5 651.3 %reduce-scatter.17.cloned.1.call-start = ((), (), s32[]{:S(2)}) async-start(), calls=%async_computation.17 | async-start | bytes 17301504 | tf_op jit(solution)/shard_map/reduce_scatter | solution.py:41
  774.1 46.5 %copy-start.1 = (f32[480,1024]{1,0:T(8,128)S(1)}, f32[480,1024]{1,0:T(8,128)}, u32[]{:S(2)}) copy-start(f32[480,1024]{1,0:T(8,128)} %copy-done) | copy-start | bytes 5898244
  774.1 46.5 %copy-start.8 = (bf16[3,160,1024]{2,1,0:T(8,128)(2,1)S(1)}, bf16[3,160,1024]{2,1,0:T(8,128)(2,1)}, u32[]{:S(2)}) copy-start(bf16[3,160,1024]{2,1,0:T(8,128)(2,1)} %param.21) | copy-start | bytes 2949124
  774.1 46.5 %copy-start.35 = (f32[480]{0:T(512)S(1)}, f32[480]{0:T(512)}, u32[]{:S(2)}) copy-start(f32[480]{0:T(512)} %copy-done.34) | copy-start | bytes 5764
  (34 other events, 178.8 us)
Sparse Core Ops, SparseCore 0:
  10.9 72.2 all-gather.7
  91.4 31.4 all-gather.9
  125.1 32.9 all-gather.11
  160.9 56.3 all-gather.13
  220.0 76.2 all-gather.15
  299.0 76.0 all-gather.17
  625.7 41.4 reduce-scatter.6
  669.9 42.8 reduce-scatter.8
  715.7 141.1 reduce-scatter.12
  863.3 151.2 reduce-scatter.10
  1017.6 182.0 reduce-scatter.14
  1202.5 184.2 reduce-scatter.16
where the time goes:
time: 1400 us; the launch traced here: 1390 us
  waiting for transfers between devices  888 us (63%)
  matrix products  291 us (21%)
  blocking collectives  84 us (6%)
  local copies, waits for them, and re-layouts  80.9 us (6%)
  other arithmetic  33.8 us (2%)
  between operations  14.9 us (1%)
    reduce_scatter x1, waiting for transfers between devices, scatter_grads(): lax.psum_scatter(mat_fc2, ('dp', 'seq'), scatter_dimension=0, tiled=True)  187 us
    reduce_scatter x1, waiting for transfers between devices, scatter_grads(): lax.psum_scatter(mat_fc1, ('dp', 'seq'), scatter_dimension=0, tiled=True)  185 us
    reduce_scatter x1, waiting for transfers between devices, scatter_grads(): lax.psum_scatter(mat_qkv, ('dp', 'seq'), scatter_dimension=0, tiled=True)  158 us
    all_gather x1, waiting for transfers between devices, gather_params(): lax.all_gather(mat_fc1, ('dp', 'seq'), axis=0, tiled=True)  75.3 us
    dot_general x3, matrix products, attend_backward(): jnp.einsum('hqk,qhd->khd', grad_scores, q_heads, preferred_element_type=j...  71.7 us
    all_gather x1, waiting for transfers between devices, gather_params(): lax.all_gather(mat_fc2, ('dp', 'seq'), axis=0, tiled=True)  68.9 us
    dot_general x3, matrix products, attend_backward(): jnp.einsum('hqk,khd->qhd', grad_scores, k_heads, preferred_element_type=j...  68.6 us
    all_gather x1, blocking collectives, gather_params(): lax.all_gather(vector_blob, ('dp', 'seq'), axis=0, tiled=True)  43.5 us
  transfers between devices with their start and end apart: 12, of which 12 were waited for; matrix products, arithmetic and copies ran while one was open for 10% of the time, Pallas kernels for 0%

commit v1 on v0

v1 whole, which is shorter than its diff:
```python
import math

import jax
import jax.numpy as jnp
from jax import lax
from jax.experimental import pallas as pl
from jax.experimental.pallas import tpu as pltpu
from jax.sharding import PartitionSpec as P

HEAD_DIM = 64
PAIR = 2 * HEAD_DIM
EPS = 1e-06
MASKED = -1000000000.0
SCALE = 1.0 / math.sqrt(HEAD_DIM)
F32 = jnp.float32
BF16 = jnp.bfloat16
QUICK = pl.CostEstimate(flops=0, bytes_accessed=0, transcendentals=0)


def after(values, *others):
    return lax.optimization_barrier((values, others))[0]


class Grid:
    def __init__(self):
        self.dp, self.seq = lax.axis_size("dp"), lax.axis_size("seq")
        self.depth = self.dp // 2
        place, spot = lax.axis_index("dp"), lax.axis_index("seq")
        self.z, self.y = place // 2, place % 2
        self.x, self.core = spot // 2, spot % 2

    def over_core(self, values):
        return lax.ppermute(values, "seq", [(i, i ^ 1) for i in range(self.seq)])

    def over_x(self, values):
        return lax.ppermute(values, "seq", [(i, i ^ 2) for i in range(self.seq)])

    def over_y(self, values):
        return lax.ppermute(values, "dp", [(i, i ^ 1) for i in range(self.dp)])

    def along_z(self, values, step):
        return lax.ppermute(values, "dp", [(i, (i + 2 * step) % self.dp) for i in range(self.dp)])


def pick(values, index, axis):
    return lax.dynamic_index_in_dim(values, index, axis, keepdims=False)


def add(left, right):
    return (left.astype(F32) + right.astype(F32)).astype(left.dtype)


def gather_z(grid, *shards):
    columns = []
    for shard in shards:
        column = [shard]
        for _ in range(1, grid.depth):
            column.append(grid.along_z(column[-1], 1))
        columns.append(column)
    return jnp.stack([jnp.concatenate(parts, axis=1) for parts in zip(*columns)])


def gather_near(grid, column):
    return grid.over_x(column), grid.over_y(column)


def gather_far(grid, by_x, by_y):
    half = grid.depth // 2
    return grid.over_y(by_x[:half]), grid.over_x(by_y[half:])


def assemble(grid, widths, column, near, far):
    parts = []
    half = grid.depth // 2
    for part, first, flip_x, flip_y in (
        (column, 0, 0, 0),
        (near[0], 0, 1, 0),
        (near[1], 0, 0, 1),
        (far[0], 0, 1, 1),
        (far[1], half, 1, 1),
    ):
        parts.append((part, first, flip_x, flip_y, 0))
        parts.append((grid.over_core(part), first, flip_x, flip_y, 1))
    places = [where[1:] for where in parts]
    parts = [part for part, *_ in parts]
    depth, rows, _ = column.shape
    if rows % 16 == 0:
        wholes = assemble_by_copies(depth, places, widths, parts)
    else:
        whole = jnp.zeros((depth, 2, 2, 2) + column.shape[1:], column.dtype)
        for part, (first, flip_x, flip_y, flip_core) in zip(parts, places):
            for k in range(part.shape[0]):
                where = ((grid.z - first - k) % depth, grid.y ^ flip_y, grid.x ^ flip_x, grid.core ^ flip_core)
                whole = lax.dynamic_update_slice(whole, part[k][None, None, None, None], where + (0, 0))
        starts = [sum(widths[:i]) for i in range(len(widths))]
        wholes = [whole[..., start : start + width] for start, width in zip(starts, widths)]
    return [whole.reshape(-1, width) for whole, width in zip(wholes, widths)]


def assemble_by_copies(depth, places, widths, parts):
    rows, wide = parts[0].shape[1:]
    blocks = sum(part.shape[0] for part in parts)
    starts = [sum(widths[:i]) for i in range(len(widths))]

    def kernel(*refs):
        sources, targets = refs[: len(parts)], refs[len(parts) : -3]
        held, came, went = refs[-3:]
        place, spot = lax.axis_index("dp"), lax.axis_index("seq")
        z, y, x, core = place // 2, place % 2, spot // 2, spot % 2
        steps = []
        for source, (first, flip_x, flip_y, flip_core) in zip(sources, places):
            across_y = 1 - y if flip_y else y
            across_x = 1 - x if flip_x else x
            across_core = 1 - core if flip_core else core
            for k in range(source.shape[0]):
                height = lax.rem(z + (2 * depth - first - k), depth)
                slot = len(steps)
                read = pltpu.make_async_copy(source.at[k], held.at[slot], came.at[slot])
                read.start()
                steps.append((read, (height, across_y, across_x, across_core)))
        writes = []
        for slot, (read, where) in enumerate(steps):
            read.wait()
            for i, target in enumerate(targets):
                write = pltpu.make_async_copy(
                    held.at[slot, :, starts[i] : starts[i] + widths[i]],
                    target.at[where],
                    went.at[slot, i],
                )
                write.start()
                writes.append(write)
        for write in writes:
            write.wait()

    shapes = [jax.ShapeDtypeStruct((depth, 2, 2, 2, rows, width), parts[0].dtype) for width in widths]
    return pl.pallas_call(
        kernel,
        in_specs=[pl.BlockSpec(memory_space=pl.ANY)] * len(parts),
        out_specs=[pl.BlockSpec(memory_space=pl.ANY)] * len(widths),
        out_shape=shapes,
        scratch_shapes=[
            pltpu.VMEM((blocks, rows, wide), parts[0].dtype),
            pltpu.SemaphoreType.DMA((blocks,)),
            pltpu.SemaphoreType.DMA((blocks, len(widths))),
        ],
        compiler_params=pltpu.CompilerParams(vmem_limit_bytes=32 * 2**20),
        cost_estimate=pl.CostEstimate(
            flops=0, bytes_accessed=4 * sum(part.size for part in parts), transcendentals=0
        ),
        name="assemble",
    )(*parts)


def reduce_core(grid, terms):
    terms = terms.reshape(grid.depth, 2, 2, 2, -1, terms.shape[-1])
    return add(pick(terms, grid.core, 3), grid.over_core(pick(terms, 1 - grid.core, 3)))


def block_at(total, y, x):
    return pick(pick(total, y, 1), x, 1)


def reduce_far(grid, total, by_x):
    part = grid.depth * by_x // 4
    far = block_at(total, 1 - grid.y, 1 - grid.x)
    return (grid.over_x(far[:part]) if part else None), grid.over_y(far[part:])


def reduce_near(grid, total, far):
    from_x, from_y = far
    to_x = block_at(total, grid.y, 1 - grid.x)
    to_y = block_at(total, 1 - grid.y, grid.x)
    part = 0 if from_x is None else from_x.shape[0]
    to_x = jnp.concatenate([to_x[:part], add(to_x[part:], from_y)])
    if part:
        to_y = jnp.concatenate([add(to_y[:part], from_x), to_y[part:]])
    return grid.over_x(to_x), grid.over_y(to_y)


def reduce_z(grid, total, near):
    own = block_at(total, grid.y, grid.x).astype(F32) + near[0].astype(F32) + near[1].astype(F32)
    low = own.astype(total.dtype)
    result = pick(own, grid.z, 0)
    for step in range(1, grid.depth):
        sent = pick(low, (grid.z + step) % grid.depth, 0)
        result = result + grid.along_z(sent, step).astype(F32)
    return result


def reduce_small(grid, terms):
    total = terms.reshape((grid.depth, 2, 2, 2) + terms.shape[1:])
    total = pick(total, grid.core, 3) + grid.over_core(pick(total, 1 - grid.core, 3))
    total = pick(total, grid.x, 2) + grid.over_x(pick(total, 1 - grid.x, 2))
    total = pick(total, grid.y, 1) + grid.over_y(pick(total, 1 - grid.y, 1))
    result = pick(total, grid.z, 0)
    for step in range(1, grid.depth):
        result = result + grid.along_z(pick(total, (grid.z + step) % grid.depth, 0), step)
    return result


def dot_rows(left, right):
    return lax.dot_general(left, right, (((1,), (1,)), ((), ())), preferred_element_type=F32)


def dot_columns(left, right):
    return lax.dot_general(left, right, (((0,), (0,)), ((), ())), preferred_element_type=F32)


def attend_forward_kernel(keep_ref, q_ref, k_ref, v_ref, out_ref, log_ref):
    keep = keep_ref[0] > 0
    queries = q_ref[0, 0]
    keys = k_ref[:, 0].reshape(-1, PAIR)
    values = v_ref[:, 0].reshape(-1, PAIR)
    outs, logs = [], []
    for head in range(2):
        part = slice(head * HEAD_DIM, (head + 1) * HEAD_DIM)
        scores = dot_rows(queries[:, part] * SCALE, keys[:, part])
        scores = jnp.where(keep, scores, MASKED)
        largest = jnp.max(scores, axis=-1, keepdims=True)
        raised = jnp.exp(scores - largest)
        totals = jnp.sum(raised, axis=-1, keepdims=True)
        mixed = jnp.dot(raised.astype(BF16), values[:, part], preferred_element_type=F32)
        outs.append(mixed / totals)
        logs.append(largest + jnp.log(totals))
    out_ref[0] = jnp.concatenate(outs, axis=1).astype(BF16)
    log_ref[0, 0] = jnp.concatenate(logs, axis=1)


def attend_forward(slot, projected, keep):
    blocks, _, local_len, wide = projected.shape
    width = wide // 3
    pairs = width // PAIR
    full_len = blocks * local_len
    return pl.pallas_call(
        attend_forward_kernel,
        grid=(pairs,),
        in_specs=[
            pl.BlockSpec((1, 1, full_len), lambda p: (slot, 0, 0)),
            pl.BlockSpec((1, 1, local_len, PAIR), lambda p: (0, slot, 0, p)),
            pl.BlockSpec((blocks, 1, local_len, PAIR), lambda p: (0, slot, 0, pairs + p)),
            pl.BlockSpec((blocks, 1, local_len, PAIR), lambda p: (0, slot, 0, 2 * pairs + p)),
        ],
        out_specs=[
            pl.BlockSpec((1, local_len, PAIR), lambda p: (0, 0, p)),
            pl.BlockSpec((1, 1, local_len, 2), lambda p: (0, p, 0, 0)),
        ],
        out_shape=[
            jax.ShapeDtypeStruct((1, local_len, width), BF16),
            jax.ShapeDtypeStruct((1, pairs, local_len, 2), F32),
        ],
        cost_estimate=QUICK,
        compiler_params=pltpu.CompilerParams(vmem_limit_bytes=32 * 2**20),
        name="attend_forward",
    )(keep, projected, projected, projected)


def attend_backward_kernel(keep_ref, q_ref, k_ref, v_ref, log_ref, g_ref, dq_ref, own_ref, send_ref):
    keep = keep_ref[0] > 0
    blocks, _, local_len, _ = k_ref.shape
    queries = q_ref[0, 0]
    keys = k_ref[:, 0].reshape(-1, PAIR)
    values = v_ref[:, 0].reshape(-1, PAIR)
    grads = g_ref[0]
    logs = log_ref[0, 0]
    dqs, dks, dvs = [], [], []
    for head in range(2):
        part = slice(head * HEAD_DIM, (head + 1) * HEAD_DIM)
        scaled = queries[:, part] * SCALE
        scores = jnp.where(keep, dot_rows(scaled, keys[:, part]), MASKED)
        chance = jnp.exp(scores - logs[:, head : head + 1])
        grad_chance = dot_rows(grads[:, part], values[:, part])
        product = chance * grad_chance
        inner = jnp.sum(product, axis=-1, keepdims=True)
        grad_scores = jnp.where(keep, product - chance * inner, 0.0).astype(BF16)
        dqs.append(jnp.dot(grad_scores, keys[:, part], preferred_element_type=F32) * SCALE)
        dks.append(dot_columns(scaled, grad_scores))
        dvs.append(dot_columns(grads[:, part], chance.astype(BF16)))
    dq_ref[0] = jnp.concatenate(dqs, axis=1).astype(BF16)
    for kind, terms in enumerate((dks, dvs)):
        turned = jnp.concatenate(terms, axis=0).T.astype(BF16).reshape(blocks, local_len, PAIR)
        for block in range(blocks):
            target = send_ref if block % 2 else own_ref
            target[block // 2, kind] = turned[block]


def attend_backward(slot, projected, keep, logs, grad_attended):
    blocks, slots, local_len, wide = projected.shape
    width = wide // 3
    pairs = width // PAIR
    full_len = blocks * local_len
    terms = jax.ShapeDtypeStruct((blocks // 2, 2, local_len, width), BF16)
    terms_spec = pl.BlockSpec((blocks // 2, 2, local_len, PAIR), lambda p: (0, 0, 0, p))
    return pl.pallas_call(
        attend_backward_kernel,
        grid=(pairs,),
        in_specs=[
            pl.BlockSpec((1, 1, full_len), lambda p: (slot, 0, 0)),
            pl.BlockSpec((1, 1, local_len, PAIR), lambda p: (0, slot, 0, p)),
            pl.BlockSpec((blocks, 1, local_len, PAIR), lambda p: (0, slot, 0, pairs + p)),
            pl.BlockSpec((blocks, 1, local_len, PAIR), lambda p: (0, slot, 0, 2 * pairs + p)),
            pl.BlockSpec((1, 1, local_len, 2), lambda p: (0, p, 0, 0)),
            pl.BlockSpec((1, local_len, PAIR), lambda p: (slot, 0, p)),
        ],
        out_specs=[pl.BlockSpec((1, local_len, PAIR), lambda p: (0, 0, p)), terms_spec, terms_spec],
        out_shape=[jax.ShapeDtypeStruct((1, local_len, width), BF16), terms, terms],
        cost_estimate=QUICK,
        compiler_params=pltpu.CompilerParams(vmem_limit_bytes=32 * 2**20),
        name="attend_backward",
    )(keep, projected, projected, projected, logs, grad_attended)


def normalise(values):
    average = jnp.mean(values, axis=-1, keepdims=True)
    centred = values - average
    spread = jnp.mean(centred * centred, axis=-1, keepdims=True)
    scale = lax.rsqrt(spread + EPS)
    return centred * scale, scale


def normalise_back(grad, gain, normal, scale):
    inward = grad * gain
    mean_in = jnp.mean(inward, axis=-1, keepdims=True)
    mean_normal = jnp.mean(inward * normal, axis=-1, keepdims=True)
    values = scale * (inward - mean_in - normal * mean_normal)
    return values, jnp.sum(grad * normal, axis=0), jnp.sum(grad, axis=0)


def split_vectors(table, lengths):
    pieces, offset = [], 0
    for length in lengths:
        pieces.append(table[:, offset : offset + length].reshape(-1))
        offset += length
    return pieces


LANES = 128


def fold(vectors, rows):
    groups, count = vectors.shape
    per_row = -(-count // rows)
    vectors = jnp.pad(vectors, ((0, 0), (0, per_row * rows - count)))
    return jnp.pad(vectors.reshape(groups * rows, per_row), ((0, 0), (0, LANES - per_row)))


def unfold(block, rows, count):
    per_row = -(-count // rows)
    return block[:, :per_row].reshape(-1, per_row * rows)[:, :count]


def shards(
    tokens,
    cotangent,
    token_mask,
    w_qkv,
    w_out,
    w_fc1,
    w_fc2,
    b_q,
    b_v,
    b_out,
    b_fc1,
    b_fc2,
    ln1_gain,
    ln1_shift,
    ln2_gain,
    ln2_shift,
):
    grid = Grid()
    groups = grid.dp * grid.seq
    slots, local_len, width = tokens.shape
    count = slots * local_len
    vector_shards = (b_q, b_v, b_out, b_fc1, b_fc2, ln1_gain, ln1_shift, ln2_gain, ln2_shift)
    lengths = [vector.shape[0] for vector in vector_shards]

    total_len = sum(lengths)
    depth_rows = w_qkv.shape[0]

    vectors = fold(jnp.concatenate(vector_shards)[None], depth_rows)
    column_one = gather_z(grid, w_qkv, vectors)
    by_core, by_x = grid.over_core(tokens), grid.over_x(tokens)
    column_one, by_x = lax.optimization_barrier((column_one, by_x))
    near_one = gather_near(grid, column_one)
    column_two = gather_z(grid, after(jnp.concatenate([w_out, w_fc1], axis=1), column_one, by_x))
    near_one = lax.optimization_barrier(near_one)
    far_one = gather_far(grid, *near_one)
    seen = jnp.stack([tokens, by_core, by_x, grid.over_core(by_x)])
    full_qkv, vectors = assemble(grid, (w_qkv.shape[1], LANES), column_one, near_one, far_one)
    column_two = after(column_two, far_one)
    near_two = gather_near(grid, column_two)
    column_three = gather_z(grid, after(w_fc2, column_two))
    near_two = lax.optimization_barrier(near_two)
    far_two = gather_far(grid, *near_two)

    vectors = unfold(vectors, depth_rows, total_len)
    vectors = [v.astype(F32) for v in split_vectors(vectors, lengths)]
    bias_q, bias_v, bias_out, bias_fc1, bias_fc2, gain_one, shift_one, gain_two, shift_two = vectors
    spot = lax.axis_index("seq")
    blocks = grid.seq
    mask_blocks = token_mask.reshape(slots, blocks, local_len)
    keep = jnp.stack([pick(mask_blocks, spot ^ block, 1) for block in range(blocks)], 1)
    valid = (keep[:, 0] > 0).reshape(-1, 1).astype(F32)
    keep = keep.reshape(slots, 1, -1)

    rows = tokens.reshape(-1, width).astype(F32)
    normal_seen, _ = normalise(seen.reshape(-1, width).astype(F32))
    normed_seen = lax.optimization_barrier((normal_seen * gain_one + shift_one).astype(BF16))
    normed_low = normed_seen[:count]
    qkv_bias = jnp.concatenate([bias_q, jnp.zeros_like(bias_out), bias_v])
    projected = (jnp.dot(normed_seen, full_qkv, preferred_element_type=F32) + qkv_bias).astype(BF16)
    projected = projected.reshape(blocks, slots, local_len, 3 * width)

    column_three = after(column_three, far_two, projected)
    near_three = gather_near(grid, column_three)
    full_out, full_fc1 = assemble(grid, (width, w_fc1.shape[1]), column_two, near_two, far_two)
    attended, logs = zip(*[attend_forward(slot, projected, keep) for slot in range(slots)])
    near_three = after(near_three, attended)
    far_three = gather_far(grid, *near_three)
    (full_fc2,) = assemble(grid, (width,), column_three, near_three, far_three)

    attended = jnp.concatenate(attended).reshape(-1, width)
    middle = rows + jnp.dot(attended, full_out, preferred_element_type=F32) + bias_out
    normal_two, scale_two = normalise(middle)
    second_low = (normal_two * gain_two + shift_two).astype(BF16)
    hidden = jnp.dot(second_low, full_fc1, preferred_element_type=F32) + bias_fc1
    below = 0.5 * (1.0 + lax.erf(hidden * math.sqrt(0.5)))
    density = jnp.exp(-0.5 * hidden * hidden) * (1.0 / math.sqrt(2.0 * math.pi))
    activated_low = (hidden * below).astype(BF16)
    slope = (below + hidden * density).astype(BF16)
    activated_low, slope = lax.optimization_barrier((activated_low, slope))

    grad_y_low = cotangent.reshape(-1, width) * valid.astype(BF16)
    grad_y = grad_y_low.astype(F32)
    terms_fc2 = dot_columns(activated_low, grad_y_low).astype(BF16)
    sum_fc2 = reduce_core(grid, terms_fc2)
    grad_y_next, full_fc2 = after((grad_y_low, full_fc2), terms_fc2)
    grad_hidden = (dot_rows(grad_y_next, full_fc2) * slope.astype(F32)).astype(BF16)
    grad_hidden, sum_fc2 = lax.optimization_barrier((grad_hidden, sum_fc2))
    far_fc2 = reduce_far(grid, sum_fc2, 2)
    result = (
        middle + jnp.dot(activated_low, full_fc2, preferred_element_type=F32) + bias_fc2
    ) * valid
    out_tokens = result.astype(BF16).reshape(slots, local_len, width)
    grad_b_fc2 = jnp.sum(grad_y, axis=0)
    terms_fc1 = dot_columns(second_low, grad_hidden).astype(BF16)
    grad_b_fc1 = jnp.sum(grad_hidden.astype(F32), axis=0)
    grad_second = dot_rows(after(grad_hidden, terms_fc1), full_fc1)
    grad_middle, grad_gain_two, grad_shift_two = normalise_back(
        grad_second, gain_two, normal_two, scale_two
    )
    grad_middle = grad_y + grad_middle
    grad_branch = after(grad_middle.astype(BF16), far_fc2)
    near_fc2 = reduce_near(grid, sum_fc2, far_fc2)
    grad_b_out = jnp.sum(grad_branch.astype(F32), axis=0)
    terms_out = dot_columns(attended, grad_branch).astype(BF16)
    sum_two = jnp.concatenate([reduce_core(grid, terms_out), reduce_core(grid, terms_fc1)], axis=-1)
    grad_attended = dot_rows(grad_branch, full_out).astype(BF16).reshape(slots, local_len, width)

    parts, ahead = [], sum_two
    for slot in range(slots):
        grad_attended = after(grad_attended, ahead)
        grad_queries, own, send = attend_backward(slot, projected, keep, logs[slot], grad_attended)
        came = grid.over_core(send)
        across = add(own[1], came[1])
        ahead = (grad_queries, across) if slot == 0 else (grad_queries, across, parts[-1][3])
        if slot == 0:
            near_fc2 = after(near_fc2, grad_queries)
            far_two = reduce_far(grid, after(sum_two, near_fc2), 0)
            grad_w_fc2 = reduce_z(grid, sum_fc2, near_fc2)
            ahead = (grad_queries,)
        else:
            ahead = (grad_queries, parts[-1][4])
        parts.append((grad_queries, own[0], came[0], grid.over_x(across), across))
    near_two = reduce_near(grid, sum_two, far_two)
    grad_two = reduce_z(grid, sum_two, near_two)
    grad_w_out, grad_w_fc1 = grad_two[:, :width], grad_two[:, width:]

    grad_queries = jnp.concatenate([part[0] for part in parts]).reshape(-1, width)
    terms_q = dot_columns(normed_low, grad_queries).astype(BF16)
    sum_q = reduce_core(grid, terms_q)
    far_q = reduce_far(grid, sum_q, 0)
    grad_keys_values = [
        (own.astype(F32) + came.astype(F32) + across.astype(F32)).astype(BF16)
        for _, own, came, across, _ in parts
    ]
    grad_keys, grad_values = [jnp.stack([part[kind] for part in grad_keys_values]) for kind in range(2)]
    grad_kv = jnp.concatenate([grad_keys, grad_values], axis=-1).reshape(-1, 2 * width)
    grad_kv, grad_w_fc2 = lax.optimization_barrier((grad_kv, grad_w_fc2))
    terms_kv = dot_columns(normed_low, grad_kv).astype(BF16)
    sum_kv = reduce_core(grid, terms_kv)
    far_kv = reduce_far(grid, sum_kv, 2)
    grad_qkv = after(jnp.concatenate([grad_queries, grad_kv], axis=-1), terms_kv)
    grad_normed = dot_rows(grad_qkv, full_qkv)
    grad_qkv_wide = jnp.sum(grad_qkv.astype(F32), axis=0)
    grad_b_q = grad_qkv_wide[:width]
    grad_b_v = grad_qkv_wide[2 * width :]
    normal_one, scale_one = normalise(rows)
    grad_rows, grad_gain_one, grad_shift_one = normalise_back(
        grad_normed, gain_one, normal_one, scale_one
    )
    grad_tokens = (grad_middle + grad_rows).reshape(slots, local_len, width)
    terms = (
        grad_b_q,
        grad_b_v,
        grad_b_out,
        grad_b_fc1,
        grad_b_fc2,
        grad_gain_one,
        grad_shift_one,
        grad_gain_two,
        grad_shift_two,
    )
    terms = jnp.concatenate([term.reshape(groups, -1) for term in terms], axis=-1)
    owned = split_vectors(reduce_small(grid, terms[:, None]).reshape(1, -1), lengths)
    near_q = reduce_near(grid, sum_q, far_q)
    near_kv = reduce_near(grid, sum_kv, far_kv)
    grad_w_qkv = jnp.concatenate([reduce_z(grid, sum_q, near_q), reduce_z(grid, sum_kv, near_kv)], axis=-1)
    return (out_tokens, grad_tokens, grad_w_qkv, grad_w_out, grad_w_fc1, grad_w_fc2, *owned)


def solution(mesh):
    spread = P(("dp", "seq"))
    row = P("dp", "seq", None)
    matrix = P(("dp", "seq"), None)
    in_specs = (row, row, P("dp", None)) + (matrix,) * 4 + (spread,) * 9
    out_specs = (row, row) + (matrix,) * 4 + (spread,) * 9
    return jax.shard_map(shards, mesh=mesh, in_specs=in_specs, out_specs=out_specs, check_vma=False)
```

time: 1400 us -> 539 us (0.39)
  waiting for transfers between devices: 888 us -> 175 us
  matrix products: 291 us -> 76.5 us
  blocking collectives: 84 us -> 0 us
  Pallas kernels: 0 us -> 76.9 us
  starting transfers between devices: 0.86 us -> 70.1 us
  other arithmetic: 33.8 us -> 78.7 us
  local copies, waits for them, and re-layouts: 80.9 us -> 52.7 us
    reduce_scatter x6 -> x0, waiting for transfers between devices: 641 us -> none  [the longest x1 187 us: scatter_grads(): lax.psum_scatter(mat_fc2, ('dp', 'seq'), scatter_dimension=0, tiled=True)]
    all_gather x6 -> x0, waiting for transfers between devices: 243 us -> none  [the longest x1 75.3 us: gather_params(): lax.all_gather(mat_fc1, ('dp', 'seq'), axis=0, tiled=True)]
    dot_general x33 -> x13, matrix products: 291 us -> 76.5 us  [the longest x4 22.1 us: dot_rows(): lax.dot_general(left, right, (((1,), (1,)), ((), ())), preferred_element_...]
    ppermute x0 -> x85, waiting for transfers between devices: none -> 175 us  [the longest x27 74.1 us: along_z(): lax.ppermute(values, 'dp', [(i, (i + 2 * step) % self.dp) for i in range(...]
    pallas_call x0 -> x9, Pallas kernels: none -> 76.9 us  [the longest x3 34.8 us: attend_backward(): pl.pallas_call(attend_backward_kernel, grid=(pairs,), in_specs=[pl.BlockS...]
    ppermute x0 -> x85, starting transfers between devices: none -> 70.1 us  [the longest x27 32.5 us: along_z(): lax.ppermute(values, 'dp', [(i, (i + 2 * step) % self.dp) for i in range(...]
    all_gather x1 -> x0, blocking collectives: 43.5 us -> none  [gather_params(): lax.all_gather(vector_blob, ('dp', 'seq'), axis=0, tiled=True)]
    unnamed x1 -> x0, blocking collectives: 40.5 us -> none
  transfers between devices with their start and end apart: 12 -> 85, of which waited for: 12 -> 31; matrix products, arithmetic and copies ran while one was open for 10% -> 31% of each run, Pallas kernels for 0% -> 14%
where the time goes in v1:
time: 539 us; the launch traced here: 533 us
  waiting for transfers between devices  175 us (32%)
  other arithmetic  78.7 us (15%)
  Pallas kernels  76.9 us (14%)
  matrix products  76.5 us (14%)
  starting transfers between devices  70.1 us (13%)
  local copies, waits for them, and re-layouts  52.7 us (10%)
    ppermute x27, waiting for transfers between devices, along_z(): lax.ppermute(values, 'dp', [(i, (i + 2 * step) % self.dp) for i in range(...  74.1 us
    ppermute x15, waiting for transfers between devices, over_y(): return lax.ppermute(values, 'dp', [(i, i ^ 1) for i in range(self.dp)])  61.7 us
    ppermute x17, waiting for transfers between devices, over_x(): return lax.ppermute(values, 'seq', [(i, i ^ 2) for i in range(self.seq)])  39.3 us
    pallas_call x3, Pallas kernels, attend_backward(): pl.pallas_call(attend_backward_kernel, grid=(pairs,), in_specs=[pl.BlockS...  34.8 us
    ppermute x27, starting transfers between devices, along_z(): lax.ppermute(values, 'dp', [(i, (i + 2 * step) % self.dp) for i in range(...  32.5 us
    pallas_call x3, Pallas kernels, attend_forward(): pl.pallas_call(attend_forward_kernel, grid=(pairs,), in_specs=[pl.BlockSp...  24.8 us
    dot_general x4, matrix products, dot_rows(): lax.dot_general(left, right, (((1,), (1,)), ((), ())), preferred_element_...  22.1 us
    convert_element_type x14, other arithmetic, add(): return (left.astype(F32) + right.astype(F32)).astype(left.dtype)  21.5 us
  transfers between devices with their start and end apart: 85, of which 31 were waited for; matrix products, arithmetic and copies ran while one was open for 31% of the time, Pallas kernels for 14%

profile of v1, /device:TPU:0, one launch (start us, length us, event | category | flops | bytes accessed | tf_op | source)
XLA Modules:
  0.0 532.8 jit_solution(4749200512777954005)
XLA Ops:
  0.7 6.1 %concatenate.73 = bf16[384]{0:T(512)(128)(2,1)S(1)} concatenate(bf16[32]{0:T(256)(128)(2,1)} %param.23, bf16[32]{0:T(256)(128)(2,1)} %param.24, bf16[32]{0:T(256)(128)(2,1)} %param.25, bf16[128]{0:T(256)(128)(2,1)} %param.26, bf16[32]{0:T(256)(128)(2,1)} %param.27, bf16[32]{0:T(256)(128)(2,1)} %param.28, bf16[32]{0:T(256)(128)(2,1)} %param.29, bf16[32]{0:T(256)(128)(2,1)} %param.30, ...), dimensions={0} | concatenate | bytes 1536 | tf_op jit(solution)/shard_map/concatenate | solution.py:379
  19.9 7.2 %collective-permute-done.3 = bf16[32,3072]{1,0:T(8,128)(2,1)S(1)} collective-permute-done((bf16[32,3072]{1,0:T(8,128)(2,1)S(1)}, bf16[32,3072]{1,0:T(8,128)(2,1)S(1)}, u32[]{:S(2)}, u32[]{:S(2)}) %collective-permute-start.3) | collective-permute-done | bytes 196640 | tf_op jit(solution)/shard_map/ppermute | solution.py:42
  27.1 7.4 %collective-permute-done.5 = bf16[32,3072]{1,0:T(8,128)(2,1)S(1)} collective-permute-done((bf16[32,3072]{1,0:T(8,128)(2,1)S(1)}, bf16[32,3072]{1,0:T(8,128)(2,1)S(1)}, u32[]{:S(2)}, u32[]{:S(2)}) %collective-permute-start.5) | collective-permute-done | bytes 196640 | tf_op jit(solution)/shard_map/ppermute | solution.py:42
  39.5 5.0 collective-permute-done.18
  46.1 7.4 %collective-permute-done.19 = bf16[32,5120]{1,0:T(8,128)(2,1)} collective-permute-done((bf16[32,5120]{1,0:T(8,128)(2,1)S(1)}, bf16[32,5120]{1,0:T(8,128)(2,1)}, u32[]{:S(2)}, u32[]{:S(2)}) %collective-permute-start.19) | collective-permute-done | bytes 327712 | tf_op jit(solution)/shard_map/ppermute | solution.py:42
  70.4 5.6 %collective-permute-done.14.refs_6_ = bf16[2,32,3200]{2,1,0:T(8,128)(2,1)S(1)} collective-permute-done((bf16[2,32,3200]{2,1,0:T(8,128)(2,1)S(1)}, bf16[2,32,3200]{2,1,0:T(8,128)(2,1)S(1)}, u32[]{:S(2)}, u32[]{:S(2)}) %collective-permute-start.14) | collective-permute-done | bytes 409632 | tf_op jit(solution)/shard_map/ppermute | solution.py:39
  98.7 9.0 %assemble.3 = (bf16[4,2,2,2,32,3072]{5,4,3,2,1,0:T(8,128)(2,1)S(1)}, bf16[4,2,2,2,32,128]{5,4,3,2,1,0:T(8,128)(2,1)S(1)}) custom-call(bf16[4,32,3200]{2,1,0:T(8,128)(2,1)S(1)} %pad_maximum_fusion.8.refs_0_, bf16[4,32,3200]{2,1,0:T(8,128)(2,1)S(1)} %copy-done.4, bf16[4,32,3200]{2,1,0:T(8,128)(2,1)S(1)} %collective-permute-done.10.refs_2_, ...), custom_call_target="tpu_custom_call" | custom-call | bytes 13107200 | tf_op jit(solution)/shard_map/assemble/pallas_call | solution.py:136
  116.9 5.5 %fusion.10 = bf16[1920,1024]{1,0:T(8,128)(2,1)} fusion(f32[4,3,160,1024]{3,2,1,0:T(8,128)} %maximum_convert_fusion, f32[1024]{0:T(1024)S(1)} %reshape.486, f32[1024]{0:T(1024)S(1)} %reshape.485, f32[1920]{0:T(1024)S(1)} %rsqrt.31, f32[1920]{0:T(1024)S(1)} %div.50), kind=kLoop, calls=%fused_computation.19 | loop fusion | flops 9830400 | bytes 11820032 | tf_op jit(solution)/shard_map/convert_element_type | solution.py:407
  123.4 7.5 %collective-permute-done.26.refs_6_ = bf16[2,32,5120]{2,1,0:T(8,128)(2,1)} collective-permute-done((bf16[2,32,5120]{2,1,0:T(8,128)(2,1)S(1)}, bf16[2,32,5120]{2,1,0:T(8,128)(2,1)}, u32[]{:S(2)}, u32[]{:S(2)}) %collective-permute-start.26) | collective-permute-done | bytes 655392 | tf_op jit(solution)/shard_map/ppermute | solution.py:39
  133.4 15.7 %add_convert_fusion = bf16[1920,3072]{1,0:T(8,128)(2,1)S(1)} fusion(bf16[1920,1024]{1,0:T(8,128)(2,1)} %fusion.10, bf16[1024,3072]{1,0:T(8,128)(2,1)} %bitcast.354, f32[3072]{0:T(1024)S(1)} %pad_maximum_fusion.13), kind=kOutput, calls=%fused_computation | convolution fusion | flops 12091392000 | bytes 22032384 | tf_op jit(solution)/shard_map/dot_general | solution.py:410
  149.1 8.3 %attend_forward.5 = (bf16[1,160,1024]{2,1,0:T(8,128)(2,1)S(1)}, f32[1,8,160,2]{3,2,1,0:T(8,128)S(1)}) custom-call(s32[3,1,640]{2,1,0:T(1,128)S(1)} %reshape.453.keep_ref, bf16[4,3,160,3072]{3,2,1,0:T(8,128)(2,1)S(1)} %bitcast.324, bf16[4,3,160,3072]{3,2,1,0:T(8,128)(2,1)S(1)} %bitcast.325, bf16[4,3,160,3072]{3,2,1,0:T(8,128)(2,1)S(1)} %bitcast.326), custom_call_target="tpu_custom_call" | custom-call | tf_op jit(solution)/shard_map/attend_forward/pallas_call | solution.py:234
  158.2 8.3 %attend_forward.4 = (bf16[1,160,1024]{2,1,0:T(8,128)(2,1)S(1)}, f32[1,8,160,2]{3,2,1,0:T(8,128)S(1)}) custom-call(s32[3,1,640]{2,1,0:T(1,128)S(1)} %reshape.453.keep_ref, bf16[4,3,160,3072]{3,2,1,0:T(8,128)(2,1)S(1)} %bitcast.327, bf16[4,3,160,3072]{3,2,1,0:T(8,128)(2,1)S(1)} %bitcast.328, bf16[4,3,160,3072]{3,2,1,0:T(8,128)(2,1)S(1)} %bitcast.329), custom_call_target="tpu_custom_call" | custom-call | tf_op jit(solution)/shard_map/attend_forward/pallas_call | solution.py:234
  167.4 8.3 %attend_forward.3 = (bf16[1,160,1024]{2,1,0:T(8,128)(2,1)S(1)}, f32[1,8,160,2]{3,2,1,0:T(8,128)S(1)}) custom-call(s32[3,1,640]{2,1,0:T(1,128)S(1)} %reshape.453.keep_ref, bf16[4,3,160,3072]{3,2,1,0:T(8,128)(2,1)S(1)} %bitcast.330, bf16[4,3,160,3072]{3,2,1,0:T(8,128)(2,1)S(1)} %bitcast.331, bf16[4,3,160,3072]{3,2,1,0:T(8,128)(2,1)S(1)} %bitcast.332), custom_call_target="tpu_custom_call" | custom-call | tf_op jit(solution)/shard_map/attend_forward/pallas_call | solution.py:234
  190.6 10.9 %fusion.6 = (bf16[480,4096]{1,0:T(8,128)(2,1)}, bf16[480,4096]{1,0:T(8,128)(2,1)S(1)}) fusion(f32[4096]{0:T(1024)S(1)} %fusion.53, bf16[1024,4096]{1,0:T(8,128)(2,1)S(1)} %bitcast.350, f32[1024]{0:T(1024)S(1)} %reshape.491, f32[1024]{0:T(1024)S(1)} %reshape.490, f32[480]{0:T(512)S(1)} %add_rsqrt_fusion.2, f32[480]{0:T(512)S(1)} %broadcast_multiply_fusion.6, ...), kind=kOutput, calls=%fused_computation.14 | convolution fusion | flops 4053073920 | bytes 18251520 | tf_op jit(solution)/shard_map/dot_general | solution.py:425
  230.8 8.2 %multiply_convert_fusion = bf16[480,4096]{1,0:T(8,128)(2,1)} fusion(bf16[480,4096]{1,0:T(8,128)(2,1)} %get-tuple-element.85, bf16[480,1024]{1,0:T(8,128)(2,1)} %bitcast_multiply_fusion, bf16[4096,1024]{1,0:T(8,128)(2,1)S(1)} %bitcast.347), kind=kOutput, calls=%fused_computation.21 | convolution fusion | flops 4032430080 | bytes 17235968 | tf_op jit(solution)/shard_map/dot_general | solution.py:202
  239.1 7.5 %multiply_convert_fusion.2 = bf16[480,1024]{1,0:T(8,128)(2,1)} fusion(f32[480,1024]{1,0:T(8,128)S(1)} %copy-done.22, bf16[480,4096]{1,0:T(8,128)(2,1)} %copy-done.52, bf16[4096,1024]{1,0:T(8,128)(2,1)S(1)} %bitcast.348, f32[480]{0:T(512)S(1)} %reshape.493, f32[1024]{0:T(1024)S(1)} %reshape.494, f32[1024]{0:T(1024)S(1)} %reshape.489), kind=kOutput, calls=%fused_computation.65 | convolution fusion | flops 4028989440 | bytes 15280000 | tf_op jit(solution)/shard_map/dot_general | solution.py:441
  246.6 5.8 %fusion.1 = bf16[4,2,2,128,1024]{4,3,2,1,0:T(8,128)(2,1)S(1)} fusion(bf16[4,2,2,128,1024]{4,3,2,1,0:T(8,128)(2,1)} %collective-permute-done.42, bf16[4,2,2,2,128,1024]{5,4,3,2,1,0:T(8,128)(2,1)} %bitcast.361, s32[]{:T(128)S(6)} %select_n.192), kind=kLoop, calls=%fused_computation.9 | loop fusion | flops 8388608 | bytes 12582916 | tf_op jit(solution)/shard_map/convert_element_type | solution.py:50
  252.5 7.4 %convolution_convert_fusion = bf16[1024,4096]{1,0:T(8,128)(2,1)} fusion(bf16[480,4096]{1,0:T(8,128)(2,1)S(1)} %copy-done.29, f32[1024]{0:T(1024)S(1)} %reshape.491, f32[1024]{0:T(1024)S(1)} %reshape.490, f32[480,1024]{1,0:T(8,128)S(1)} %copy-done.22, f32[480]{0:T(512)S(1)} %add_rsqrt_fusion.2, f32[480]{0:T(512)S(1)} %broadcast_multiply_fusion.6, ...), kind=kOutput, calls=%fused_computation.25 | convolution fusion | flops 4033675264 | bytes 14302976 | tf_op jit(solution)/shard_map/dot_general | solution.py:206
  267.7 5.9 %multiply_reduce_fusion.1 = (f32[1024]{0:T(1024)S(1)}, f32[480]{0:T(512)S(1)}, f32[480]{0:T(512)S(1)}, f32[1024]{0:T(1024)S(1)}, f32[480,1024]{1,0:T(8,128)}) fusion(f32[480]{0:T(512)S(1)} %add_rsqrt_fusion.2, f32[480]{0:T(512)S(1)} %broadcast_multiply_fusion.6, f32[480,1024]{1,0:T(8,128)S(1)} %copy-done.22, f32[1024]{0:T(1024)S(1)} %reshape.489, ...), kind=kOutput, calls=%fused_computation.57 | convolution fusion | flops 4031443968 | bytes 16276992 | tf_op jit(solution)/shard_map/dot_general | solution.py:202
  294.9 5.2 fusion
  303.3 11.6 %attend_backward.3 = (bf16[1,160,1024]{2,1,0:T(8,128)(2,1)S(1)}, bf16[2,2,160,1024]{3,2,1,0:T(8,128)(2,1)S(1)}, bf16[2,2,160,1024]{3,2,1,0:T(8,128)(2,1)S(1)}) custom-call(s32[3,1,640]{2,1,0:T(1,128)S(1)} %reshape.453.keep_ref, bf16[4,3,160,3072]{3,2,1,0:T(8,128)(2,1)S(1)} %bitcast.335, bf16[4,3,160,3072]{3,2,1,0:T(8,128)(2,1)S(1)} %bitcast.336, ...), custom_call_target="tpu_custom_call" | custom-call | tf_op jit(solution)/shard_map/attend_backward/pallas_call | solution.py:293
  315.0 11.6 %attend_backward.4 = (bf16[1,160,1024]{2,1,0:T(8,128)(2,1)S(1)}, bf16[2,2,160,1024]{3,2,1,0:T(8,128)(2,1)S(1)}, bf16[2,2,160,1024]{3,2,1,0:T(8,128)(2,1)S(1)}) custom-call(s32[3,1,640]{2,1,0:T(1,128)S(1)} %reshape.453.keep_ref, bf16[4,3,160,3072]{3,2,1,0:T(8,128)(2,1)S(1)} %bitcast.338, bf16[4,3,160,3072]{3,2,1,0:T(8,128)(2,1)S(1)} %bitcast.339, ...), custom_call_target="tpu_custom_call" | custom-call | tf_op jit(solution)/shard_map/attend_backward/pallas_call | solution.py:293
  342.2 16.3 %collective-permute-done.56 = bf16[128,1024]{1,0:T(8,128)(2,1)S(1)} collective-permute-done((bf16[128,1024]{1,0:T(8,128)(2,1)S(1)}, bf16[128,1024]{1,0:T(8,128)(2,1)S(1)}, u32[]{:S(2)}, u32[]{:S(2)}) %collective-permute-start.56) | collective-permute-done | bytes 262176 | tf_op jit(solution)/shard_map/ppermute | solution.py:42
  362.4 11.6 %attend_backward.5 = (bf16[1,160,1024]{2,1,0:T(8,128)(2,1)S(1)}, bf16[2,2,160,1024]{3,2,1,0:T(8,128)(2,1)S(1)}, bf16[2,2,160,1024]{3,2,1,0:T(8,128)(2,1)S(1)}) custom-call(s32[3,1,640]{2,1,0:T(1,128)S(1)} %reshape.453.keep_ref, bf16[4,3,160,3072]{3,2,1,0:T(8,128)(2,1)S(1)} %bitcast.341, bf16[4,3,160,3072]{3,2,1,0:T(8,128)(2,1)S(1)} %bitcast.342, ...), custom_call_target="tpu_custom_call" | custom-call | tf_op jit(solution)/shard_map/attend_backward/pallas_call | solution.py:293
  377.5 21.5 %collective-permute-done.73 = bf16[4,32,5120]{2,1,0:T(8,128)(2,1)} collective-permute-done((bf16[4,32,5120]{2,1,0:T(8,128)(2,1)}, bf16[4,32,5120]{2,1,0:T(8,128)(2,1)}, u32[]{:S(2)}, u32[]{:S(2)}) %collective-permute-start.73) | collective-permute-done | bytes 1310752 | tf_op jit(solution)/shard_map/ppermute | solution.py:39
  407.6 11.1 %collective-permute-done.59 = bf16[4,32,1024]{2,1,0:T(8,128)(2,1)S(1)} collective-permute-done((bf16[4,32,1024]{2,1,0:T(8,128)(2,1)S(1)}, bf16[4,32,1024]{2,1,0:T(8,128)(2,1)S(1)}, u32[]{:S(2)}, u32[]{:S(2)}) %collective-permute-start.59) | collective-permute-done | bytes 262176 | tf_op jit(solution)/shard_map/ppermute | solution.py:39
  419.4 12.9 %collective-permute-done.74 = bf16[4,32,5120]{2,1,0:T(8,128)(2,1)S(1)} collective-permute-done((bf16[4,32,5120]{2,1,0:T(8,128)(2,1)S(1)}, bf16[4,32,5120]{2,1,0:T(8,128)(2,1)S(1)}, u32[]{:S(2)}, u32[]{:S(2)}) %collective-permute-start.74) | collective-permute-done | bytes 1310752 | tf_op jit(solution)/shard_map/ppermute | solution.py:36
  438.0 13.6 %collective-permute-done.60 = bf16[4,32,1024]{2,1,0:T(8,128)(2,1)S(1)} collective-permute-done((bf16[4,32,1024]{2,1,0:T(8,128)(2,1)S(1)}, bf16[4,32,1024]{2,1,0:T(8,128)(2,1)S(1)}, u32[]{:S(2)}, u32[]{:S(2)}) %collective-permute-start.60) | collective-permute-done | bytes 262176 | tf_op jit(solution)/shard_map/ppermute | solution.py:36
  456.7 10.5 %collective-permute-done.77 = bf16[32,5120]{1,0:T(8,128)(2,1)S(1)} collective-permute-done((bf16[32,5120]{1,0:T(8,128)(2,1)S(1)}, bf16[32,5120]{1,0:T(8,128)(2,1)S(1)}, u32[]{:S(2)}, u32[]{:S(2)}) %collective-permute-start.77) | collective-permute-done | bytes 327712 | tf_op jit(solution)/shard_map/ppermute | solution.py:42
  473.9 6.7 %fusion.65 = (f32[1024]{0:T(1024)S(1)}, f32[1024]{0:T(1024)S(1)}, f32[480]{0:T(512)}, f32[480]{0:T(512)}, f32[480,1024]{1,0:T(8,128)}) fusion(f32[480]{0:T(512)S(1)} %rsqrt.34, f32[480]{0:T(512)S(1)} %div.65, bf16[3,160,1024]{2,1,0:T(8,128)(2,1)} %param.16, f32[480,1024]{1,0:T(8,128)S(1)} %copy-done.33, f32[1024]{0:T(1024)S(1)} %copy-done.48, ...), kind=kOutput, calls=%fused_computation.230 | convolution fusion | flops 3024811008 | bytes 14175744 | tf_op jit(solution)/shard_map/dot_general | solution.py:202
  504.7 6.9 %collective-permute-done.66 = bf16[2,32,2048]{2,1,0:T(8,128)(2,1)S(1)} collective-permute-done((bf16[2,32,2048]{2,1,0:T(8,128)(2,1)S(1)}, bf16[2,32,2048]{2,1,0:T(8,128)(2,1)S(1)}, u32[]{:S(2)}, u32[]{:S(2)}) %collective-permute-start.66) | collective-permute-done | bytes 262176 | tf_op jit(solution)/shard_map/ppermute | solution.py:39
  526.4 5.2 collective-permute-done.71
  (431 shorter events, 238.6 us)
Async XLA Ops:
  36.4 28.3 %collective-permute-start = (bf16[3,160,1024]{2,1,0:T(8,128)(2,1)}, bf16[3,160,1024]{2,1,0:T(8,128)(2,1)}, u32[]{:S(2)}, u32[]{:S(2)}) collective-permute-start(bf16[3,160,1024]{2,1,0:T(8,128)(2,1)} %param.16), channel_id=1, source_target_pairs={{0,1},{1,0},{2,3},{3,2},{4,5},{5,4},{6,7},{7,6},{8,9},{9,8},{10,11... | collective-permute-start | bytes 2949128 | tf_op jit(solution)/shard_map/ppermute | solution.py:33
  58.5 29.2 %collective-permute-start.12 = (bf16[4,32,3200]{2,1,0:T(8,128)(2,1)S(1)}, bf16[4,32,3200]{2,1,0:T(8,128)(2,1)S(1)}, u32[]{:S(2)}, u32[]{:S(2)}) collective-permute-start(bf16[4,32,3200]{2,1,0:T(8,128)(2,1)S(1)} %collective-permute-done.10.refs_2_), channel_id=1, source_target_pairs={{0,1},{1,0},{2,3},{3,2},{4,5},{5,4},{6,7},{7,6},{8,9},{9,8},{10,11... | collective-permute-start | bytes 2457608 | tf_op jit(solution)/shard_map/ppermute | solution.py:33
  62.6 31.4 %collective-permute-start.13 = (bf16[4,32,3200]{2,1,0:T(8,128)(2,1)}, bf16[4,32,3200]{2,1,0:T(8,128)(2,1)S(1)}, u32[]{:S(2)}, u32[]{:S(2)}) collective-permute-start(bf16[4,32,3200]{2,1,0:T(8,128)(2,1)} %collective-permute-done.11.refs_4_), channel_id=1, source_target_pairs={{0,1},{1,0},{2,3},{3,2},{4,5},{5,4},{6,7},{7,6},{8,9},{9,8},{10,11... | collective-permute-start | bytes 2457608 | tf_op jit(solution)/shard_map/ppermute | solution.py:33
  77.3 35.2 %collective-permute-start.22 = (bf16[4,32,5120]{2,1,0:T(8,128)(2,1)S(1)}, bf16[4,32,5120]{2,1,0:T(8,128)(2,1)}, u32[]{:S(2)}, u32[]{:S(2)}) collective-permute-start(bf16[4,32,5120]{2,1,0:T(8,128)(2,1)S(1)} %pad_maximum_fusion.2.refs_0_), channel_id=1, source_target_pairs={{0,2},{1,3},{2,0},{3,1},{4,6},{5,7},{6,4},{7,5},{8,10},{9,11},{10,... | collective-permute-start | bytes 3932168 | tf_op jit(solution)/shard_map/ppermute | solution.py:36
  78.8 33.7 %collective-permute-start.23 = (bf16[4,32,5120]{2,1,0:T(8,128)(2,1)S(1)}, bf16[4,32,5120]{2,1,0:T(8,128)(2,1)}, u32[]{:S(2)}, u32[]{:S(2)}) collective-permute-start(bf16[4,32,5120]{2,1,0:T(8,128)(2,1)S(1)} %pad_maximum_fusion.2.refs_0_), channel_id=1, source_target_pairs={{0,4},{4,0},{8,12},{12,8},{16,20},{20,16},{24,28},{28,24},{1,5},{5... | collective-permute-start | bytes 3932168 | tf_op jit(solution)/shard_map/ppermute | solution.py:39
  95.1 83.6 %collective-permute-start.21 = (bf16[4,32,5120]{2,1,0:T(8,128)(2,1)S(1)}, bf16[4,32,5120]{2,1,0:T(8,128)(2,1)}, u32[]{:S(2)}, u32[]{:S(2)}) collective-permute-start(bf16[4,32,5120]{2,1,0:T(8,128)(2,1)S(1)} %pad_maximum_fusion.2.refs_0_), channel_id=1, source_target_pairs={{0,1},{1,0},{2,3},{3,2},{4,5},{5,4},{6,7},{7,6},{8,9},{9,8},{10,11... | collective-permute-start | bytes 3932168 | tf_op jit(solution)/shard_map/ppermute | solution.py:33
  122.6 56.8 %collective-permute-start.24 = (bf16[4,32,5120]{2,1,0:T(8,128)(2,1)}, bf16[4,32,5120]{2,1,0:T(8,128)(2,1)}, u32[]{:S(2)}, u32[]{:S(2)}) collective-permute-start(bf16[4,32,5120]{2,1,0:T(8,128)(2,1)} %collective-permute-done.22.refs_2_), channel_id=1, source_target_pairs={{0,1},{1,0},{2,3},{3,2},{4,5},{5,4},{6,7},{7,6},{8,9},{9,8},{10,11... | collective-permute-start | bytes 3932168 | tf_op jit(solution)/shard_map/ppermute | solution.py:33
  123.4 56.4 %collective-permute-start.25 = (bf16[4,32,5120]{2,1,0:T(8,128)(2,1)}, bf16[4,32,5120]{2,1,0:T(8,128)(2,1)}, u32[]{:S(2)}, u32[]{:S(2)}) collective-permute-start(bf16[4,32,5120]{2,1,0:T(8,128)(2,1)} %collective-permute-done.23.refs_4_), channel_id=1, source_target_pairs={{0,1},{1,0},{2,3},{3,2},{4,5},{5,4},{6,7},{7,6},{8,9},{9,8},{10,11... | collective-permute-start | bytes 3932168 | tf_op jit(solution)/shard_map/ppermute | solution.py:33
  130.9 49.5 %collective-permute-start.27 = (bf16[2,32,5120]{2,1,0:T(8,128)(2,1)}, bf16[2,32,5120]{2,1,0:T(8,128)(2,1)}, u32[]{:S(2)}, u32[]{:S(2)}) collective-permute-start(bf16[2,32,5120]{2,1,0:T(8,128)(2,1)} %collective-permute-done.26.refs_6_), channel_id=1, source_target_pairs={{0,1},{1,0},{2,3},{3,2},{4,5},{5,4},{6,7},{7,6},{8,9},{9,8},{10,11... | collective-permute-start | bytes 1966088 | tf_op jit(solution)/shard_map/ppermute | solution.py:33
  133.4 47.1 %collective-permute-start.29 = (bf16[2,32,5120]{2,1,0:T(8,128)(2,1)}, bf16[2,32,5120]{2,1,0:T(8,128)(2,1)}, u32[]{:S(2)}, u32[]{:S(2)}) collective-permute-start(bf16[2,32,5120]{2,1,0:T(8,128)(2,1)} %collective-permute-done.28.refs_8_), channel_id=1, source_target_pairs={{0,1},{1,0},{2,3},{3,2},{4,5},{5,4},{6,7},{7,6},{8,9},{9,8},{10,11... | collective-permute-start | bytes 1966088 | tf_op jit(solution)/shard_map/ppermute | solution.py:33
  178.8 35.6 %collective-permute-start.33 = (bf16[4,128,1024]{2,1,0:T(8,128)(2,1)S(1)}, bf16[4,128,1024]{2,1,0:T(8,128)(2,1)S(1)}, u32[]{:S(2)}, u32[]{:S(2)}) collective-permute-start(bf16[4,128,1024]{2,1,0:T(8,128)(2,1)S(1)} %pad_maximum_fusion.3.refs_0_), channel_id=1, source_target_pairs={{0,1},{1,0},{2,3},{3,2},{4,5},{5,4},{6,7},{7,6},{8,9},{9,8},{10,11... | collective-permute-start | bytes 3145736 | tf_op jit(solution)/shard_map/ppermute | solution.py:33
  179.4 27.0 %collective-permute-start.34 = (bf16[4,128,1024]{2,1,0:T(8,128)(2,1)S(1)}, bf16[4,128,1024]{2,1,0:T(8,128)(2,1)S(1)}, u32[]{:S(2)}, u32[]{:S(2)}) collective-permute-start(bf16[4,128,1024]{2,1,0:T(8,128)(2,1)S(1)} %pad_maximum_fusion.3.refs_0_), channel_id=1, source_target_pairs={{0,2},{1,3},{2,0},{3,1},{4,6},{5,7},{6,4},{7,5},{8,10},{9,11},{10,... | collective-permute-start | bytes 3145736 | tf_op jit(solution)/shard_map/ppermute | solution.py:36
  179.9 26.5 %collective-permute-start.35 = (bf16[4,128,1024]{2,1,0:T(8,128)(2,1)S(1)}, bf16[4,128,1024]{2,1,0:T(8,128)(2,1)}, u32[]{:S(2)}, u32[]{:S(2)}) collective-permute-start(bf16[4,128,1024]{2,1,0:T(8,128)(2,1)S(1)} %pad_maximum_fusion.3.refs_0_), channel_id=1, source_target_pairs={{0,4},{4,0},{8,12},{12,8},{16,20},{20,16},{24,28},{28,24},{1,5},{5... | collective-permute-start | bytes 3145736 | tf_op jit(solution)/shard_map/ppermute | solution.py:39
  213.8 32.8 %collective-permute-start.42 = (bf16[4,2,2,128,1024]{4,3,2,1,0:T(8,128)(2,1)}, bf16[4,2,2,128,1024]{4,3,2,1,0:T(8,128)(2,1)}, u32[]{:S(2)}, u32[]{:S(2)}) collective-permute-start(bf16[4,2,2,128,1024]{4,3,2,1,0:T(8,128)(2,1)} %dynamic-slice_bitcast_fusion.1), channel_id=1, source_target_pairs={{0,1},{1,0},{2,3},{3,2},{4,5},{5,4},{6,7},{7,6},{8,9},{9,8},{10,11... | collective-permute-start | bytes 12582920 | tf_op jit(solution)/shard_map/ppermute | solution.py:33
  267.7 27.1 %collective-permute-start.46 = (bf16[4,2,2,32,4096]{4,3,2,1,0:T(8,128)(2,1)}, bf16[4,2,2,32,4096]{4,3,2,1,0:T(8,128)(2,1)}, u32[]{:S(2)}, u32[]{:S(2)}) collective-permute-start(bf16[4,2,2,32,4096]{4,3,2,1,0:T(8,128)(2,1)} %dynamic-slice_bitcast_fusion), channel_id=1, source_target_pairs={{0,1},{1,0},{2,3},{3,2},{4,5},{5,4},{6,7},{7,6},{8,9},{9,8},{10,11... | collective-permute-start | bytes 12582920 | tf_op jit(solution)/shard_map/ppermute | solution.py:33
  287.0 41.3 %collective-permute-start.53 = (bf16[4,128,1024]{2,1,0:T(8,128)(2,1)}, bf16[4,128,1024]{2,1,0:T(8,128)(2,1)}, u32[]{:S(2)}, u32[]{:S(2)}) collective-permute-start(bf16[4,128,1024]{2,1,0:T(8,128)(2,1)} %pad_maximum_fusion.4), channel_id=1, source_target_pairs={{0,2},{1,3},{2,0},{3,1},{4,6},{5,7},{6,4},{7,5},{8,10},{9,11},{10,... | collective-permute-start | bytes 3145736 | tf_op jit(solution)/shard_map/ppermute | solution.py:36
  289.9 38.4 %collective-permute-start.54 = (bf16[4,128,1024]{2,1,0:T(8,128)(2,1)}, bf16[4,128,1024]{2,1,0:T(8,128)(2,1)}, u32[]{:S(2)}, u32[]{:S(2)}) collective-permute-start(bf16[4,128,1024]{2,1,0:T(8,128)(2,1)} %pad_maximum_fusion.5), channel_id=1, source_target_pairs={{0,4},{4,0},{8,12},{12,8},{16,20},{20,16},{24,28},{28,24},{1,5},{5... | collective-permute-start | bytes 3145736 | tf_op jit(solution)/shard_map/ppermute | solution.py:39
  314.9 45.0 %collective-permute-start.47 = (bf16[2,2,160,1024]{3,2,1,0:T(8,128)(2,1)S(1)}, bf16[2,2,160,1024]{3,2,1,0:T(8,128)(2,1)S(1)}, u32[]{:S(2)}, u32[]{:S(2)}) collective-permute-start(bf16[2,2,160,1024]{3,2,1,0:T(8,128)(2,1)S(1)} %get-tuple-element.98), channel_id=1, source_target_pairs={{0,1},{1,0},{2,3},{3,2},{4,5},{5,4},{6,7},{7,6},{8,9},{9,8},{10,11... | collective-permute-start | bytes 3932168 | tf_op jit(solution)/shard_map/ppermute | solution.py:33
  326.6 47.5 %collective-permute-start.49 = (bf16[2,2,160,1024]{3,2,1,0:T(8,128)(2,1)S(1)}, bf16[2,2,160,1024]{3,2,1,0:T(8,128)(2,1)S(1)}, u32[]{:S(2)}, u32[]{:S(2)}) collective-permute-start(bf16[2,2,160,1024]{3,2,1,0:T(8,128)(2,1)S(1)} %get-tuple-element.102), channel_id=1, source_target_pairs={{0,1},{1,0},{2,3},{3,2},{4,5},{5,4},{6,7},{7,6},{8,9},{9,8},{10,11... | collective-permute-start | bytes 3932168 | tf_op jit(solution)/shard_map/ppermute | solution.py:33
  341.7 77.8 %collective-permute-start.75 = (bf16[4,32,5120]{2,1,0:T(8,128)(2,1)}, bf16[4,32,5120]{2,1,0:T(8,128)(2,1)S(1)}, u32[]{:S(2)}, u32[]{:S(2)}) collective-permute-start(bf16[4,32,5120]{2,1,0:T(8,128)(2,1)} %fusion.25), channel_id=1, source_target_pairs={{0,4},{4,0},{8,12},{12,8},{16,20},{20,16},{24,28},{28,24},{1,5},{5... | collective-permute-start | bytes 3932168 | tf_op jit(solution)/shard_map/ppermute | solution.py:39
  358.5 40.5 %collective-permute-start.73 = (bf16[4,32,5120]{2,1,0:T(8,128)(2,1)}, bf16[4,32,5120]{2,1,0:T(8,128)(2,1)}, u32[]{:S(2)}, u32[]{:S(2)}) collective-permute-start(bf16[4,32,5120]{2,1,0:T(8,128)(2,1)} %dynamic-slice_bitcast_fusion.3), channel_id=1, source_target_pairs={{0,4},{4,0},{8,12},{12,8},{16,20},{20,16},{24,28},{28,24},{1,5},{5... | collective-permute-start | bytes 3932168 | tf_op jit(solution)/shard_map/ppermute | solution.py:39
  361.0 41.5 %collective-permute-start.48 = (bf16[2,160,1024]{2,1,0:T(8,128)(2,1)}, bf16[2,160,1024]{2,1,0:T(8,128)(2,1)}, u32[]{:S(2)}, u32[]{:S(2)}) collective-permute-start(bf16[2,160,1024]{2,1,0:T(8,128)(2,1)} %fusion.34), channel_id=1, source_target_pairs={{0,2},{1,3},{2,0},{3,1},{4,6},{5,7},{6,4},{7,5},{8,10},{9,11},{10,... | collective-permute-start | bytes 1966088 | tf_op jit(solution)/shard_map/ppermute | solution.py:36
  374.0 32.6 %collective-permute-start.51 = (bf16[2,2,160,1024]{3,2,1,0:T(8,128)(2,1)S(1)}, bf16[2,2,160,1024]{3,2,1,0:T(8,128)(2,1)S(1)}, u32[]{:S(2)}, u32[]{:S(2)}) collective-permute-start(bf16[2,2,160,1024]{3,2,1,0:T(8,128)(2,1)S(1)} %get-tuple-element.104), channel_id=1, source_target_pairs={{0,1},{1,0},{2,3},{3,2},{4,5},{5,4},{6,7},{7,6},{8,9},{9,8},{10,11... | collective-permute-start | bytes 3932168 | tf_op jit(solution)/shard_map/ppermute | solution.py:33
  374.4 26.3 %collective-permute-start.50 = (bf16[2,160,1024]{2,1,0:T(8,128)(2,1)S(1)}, bf16[2,160,1024]{2,1,0:T(8,128)(2,1)S(1)}, u32[]{:S(2)}, u32[]{:S(2)}) collective-permute-start(bf16[2,160,1024]{2,1,0:T(8,128)(2,1)S(1)} %fusion.35), channel_id=1, source_target_pairs={{0,2},{1,3},{2,0},{3,1},{4,6},{5,7},{6,4},{7,5},{8,10},{9,11},{10,... | collective-permute-start | bytes 1966088 | tf_op jit(solution)/shard_map/ppermute | solution.py:36
  400.7 31.6 %collective-permute-start.74 = (bf16[4,32,5120]{2,1,0:T(8,128)(2,1)S(1)}, bf16[4,32,5120]{2,1,0:T(8,128)(2,1)S(1)}, u32[]{:S(2)}, u32[]{:S(2)}) collective-permute-start(bf16[4,32,5120]{2,1,0:T(8,128)(2,1)S(1)} %fusion.12), channel_id=1, source_target_pairs={{0,2},{1,3},{2,0},{3,1},{4,6},{5,7},{6,4},{7,5},{8,10},{9,11},{10,... | collective-permute-start | bytes 3932168 | tf_op jit(solution)/shard_map/ppermute | solution.py:36
  404.5 32.9 %collective-permute-start.61 = (bf16[4,32,1024]{2,1,0:T(8,128)(2,1)S(1)}, bf16[4,32,1024]{2,1,0:T(8,128)(2,1)S(1)}, u32[]{:S(2)}, u32[]{:S(2)}) collective-permute-start(bf16[4,32,1024]{2,1,0:T(8,128)(2,1)S(1)} %get-tuple-element.144), channel_id=1, source_target_pairs={{0,4},{4,0},{8,12},{12,8},{16,20},{20,16},{24,28},{28,24},{1,5},{5... | collective-permute-start | bytes 786440 | tf_op jit(solution)/shard_map/ppermute | solution.py:39
  406.8 60.5 %collective-permute-start.52 = (bf16[2,160,1024]{2,1,0:T(8,128)(2,1)S(1)}, bf16[2,160,1024]{2,1,0:T(8,128)(2,1)S(1)}, u32[]{:S(2)}, u32[]{:S(2)}) collective-permute-start(bf16[2,160,1024]{2,1,0:T(8,128)(2,1)S(1)} %fusion.36), channel_id=1, source_target_pairs={{0,2},{1,3},{2,0},{3,1},{4,6},{5,7},{6,4},{7,5},{8,10},{9,11},{10,... | collective-permute-start | bytes 1966088 | tf_op jit(solution)/shard_map/ppermute | solution.py:36
  418.7 32.9 %collective-permute-start.60 = (bf16[4,32,1024]{2,1,0:T(8,128)(2,1)S(1)}, bf16[4,32,1024]{2,1,0:T(8,128)(2,1)S(1)}, u32[]{:S(2)}, u32[]{:S(2)}) collective-permute-start(bf16[4,32,1024]{2,1,0:T(8,128)(2,1)S(1)} %fusion.41), channel_id=1, source_target_pairs={{0,2},{1,3},{2,0},{3,1},{4,6},{5,7},{6,4},{7,5},{8,10},{9,11},{10,... | collective-permute-start | bytes 786440 | tf_op jit(solution)/shard_map/ppermute | solution.py:36
  437.4 29.8 %collective-permute-start.77 = (bf16[32,5120]{1,0:T(8,128)(2,1)S(1)}, bf16[32,5120]{1,0:T(8,128)(2,1)S(1)}, u32[]{:S(2)}, u32[]{:S(2)}) collective-permute-start(bf16[32,5120]{1,0:T(8,128)(2,1)S(1)} %get-tuple-element.142), channel_id=1, source_target_pairs={{0,16},{4,20},{8,24},{12,28},{16,0},{20,4},{24,8},{28,12},{1,17},{... | collective-permute-start | bytes 983048 | tf_op jit(solution)/shard_map/ppermute | solution.py:42
  437.4 29.8 %collective-permute-start.76 = (bf16[32,5120]{1,0:T(8,128)(2,1)S(1)}, bf16[32,5120]{1,0:T(8,128)(2,1)S(1)}, u32[]{:S(2)}, u32[]{:S(2)}) collective-permute-start(bf16[32,5120]{1,0:T(8,128)(2,1)S(1)} %get-tuple-element.140), channel_id=1, source_target_pairs={{0,8},{4,12},{8,16},{12,20},{16,24},{20,28},{24,0},{28,4},{1,9},{5... | collective-permute-start | bytes 983048 | tf_op jit(solution)/shard_map/ppermute | solution.py:42
  452.4 29.9 %collective-permute-start.64 = (bf16[32,1024]{1,0:T(8,128)(2,1)}, bf16[32,1024]{1,0:T(8,128)(2,1)S(1)}, u32[]{:S(2)}, u32[]{:S(2)}) collective-permute-start(bf16[32,1024]{1,0:T(8,128)(2,1)} %get-tuple-element.158), channel_id=1, source_target_pairs={{0,24},{4,28},{8,0},{12,4},{16,8},{20,12},{24,16},{28,20},{1,25},{... | collective-permute-start | bytes 196616 | tf_op jit(solution)/shard_map/ppermute | solution.py:42
  456.7 25.7 %collective-permute-start.63 = (bf16[32,1024]{1,0:T(8,128)(2,1)}, bf16[32,1024]{1,0:T(8,128)(2,1)}, u32[]{:S(2)}, u32[]{:S(2)}) collective-permute-start(bf16[32,1024]{1,0:T(8,128)(2,1)} %get-tuple-element.159), channel_id=1, source_target_pairs={{0,16},{4,20},{8,24},{12,28},{16,0},{20,4},{24,8},{28,12},{1,17},{... | collective-permute-start | bytes 196616 | tf_op jit(solution)/shard_map/ppermute | solution.py:42
  (113 other events, 1127.6 us)

commit v2 on v1

--- a/solution.py
+++ b/solution.py
@@ -69,18 +69,22 @@
     return grid.over_y(by_x[:half]), grid.over_x(by_y[half:])
 
 
-def assemble(grid, widths, column, near, far):
+def swap(grid, *parts):
+    return [grid.over_core(part) for part in parts]
+
+
+def assemble(grid, widths, column, near, far, swapped):
     parts = []
     half = grid.depth // 2
-    for part, first, flip_x, flip_y in (
-        (column, 0, 0, 0),
-        (near[0], 0, 1, 0),
-        (near[1], 0, 0, 1),
-        (far[0], 0, 1, 1),
-        (far[1], half, 1, 1),
+    for part, other, first, flip_x, flip_y in zip(
+        (column, *near, *far),
+        (*swapped, *swap(grid, *far)),
+        (0, 0, 0, 0, half),
+        (0, 1, 0, 1, 1),
+        (0, 0, 1, 1, 1),
     ):
         parts.append((part, first, flip_x, flip_y, 0))
-        parts.append((grid.over_core(part), first, flip_x, flip_y, 1))
+        parts.append((other, first, flip_x, flip_y, 1))
     places = [where[1:] for where in parts]
     parts = [part for part, *_ in parts]
     depth, rows, _ = column.shape
@@ -385,7 +389,9 @@
     near_one = lax.optimization_barrier(near_one)
     far_one = gather_far(grid, *near_one)
     seen = jnp.stack([tokens, by_core, by_x, grid.over_core(by_x)])
-    full_qkv, vectors = assemble(grid, (w_qkv.shape[1], LANES), column_one, near_one, far_one)
+    full_qkv, vectors = assemble(
+        grid, (w_qkv.shape[1], LANES), column_one, near_one, far_one, swap(grid, column_one, *near_one)
+    )
     column_two = after(column_two, far_one)
     near_two = gather_near(grid, column_two)
     column_three = gather_z(grid, after(w_fc2, column_two))
@@ -410,15 +416,19 @@
     projected = (jnp.dot(normed_seen, full_qkv, preferred_element_type=F32) + qkv_bias).astype(BF16)
     projected = projected.reshape(blocks, slots, local_len, 3 * width)
 
-    column_three = after(column_three, far_two, projected)
+    swapped_two = swap(grid, column_two, *near_two)
+    projected, column_three, far_two, swapped_two = lax.optimization_barrier(
+        (projected, column_three, far_two, swapped_two)
+    )
     near_three = gather_near(grid, column_three)
-    full_out, full_fc1 = assemble(grid, (width, w_fc1.shape[1]), column_two, near_two, far_two)
+    full_out, full_fc1 = assemble(
+        grid, (width, w_fc1.shape[1]), column_two, near_two, far_two, swapped_two
+    )
     attended, logs = zip(*[attend_forward(slot, projected, keep) for slot in range(slots)])
-    near_three = after(near_three, attended)
+    attended = jnp.concatenate(attended).reshape(-1, width)
+    attended, near_three = lax.optimization_barrier((attended, near_three))
     far_three = gather_far(grid, *near_three)
-    (full_fc2,) = assemble(grid, (width,), column_three, near_three, far_three)
-
-    attended = jnp.concatenate(attended).reshape(-1, width)
+    swapped_three = swap(grid, column_three, *near_three)
     middle = rows + jnp.dot(attended, full_out, preferred_element_type=F32) + bias_out
     normal_two, scale_two = normalise(middle)
     second_low = (normal_two * gain_two + shift_two).astype(BF16)
@@ -427,7 +437,10 @@
     density = jnp.exp(-0.5 * hidden * hidden) * (1.0 / math.sqrt(2.0 * math.pi))
     activated_low = (hidden * below).astype(BF16)
     slope = (below + hidden * density).astype(BF16)
-    activated_low, slope = lax.optimization_barrier((activated_low, slope))
+    activated_low, slope, far_three, swapped_three = lax.optimization_barrier(
+        (activated_low, slope, far_three, swapped_three)
+    )
+    (full_fc2,) = assemble(grid, (width,), column_three, near_three, far_three, swapped_three)
 
     grad_y_low = cotangent.reshape(-1, width) * valid.astype(BF16)
     grad_y = grad_y_low.astype(F32)
@@ -437,10 +450,6 @@
     grad_hidden = (dot_rows(grad_y_next, full_fc2) * slope.astype(F32)).astype(BF16)
     grad_hidden, sum_fc2 = lax.optimization_barrier((grad_hidden, sum_fc2))
     far_fc2 = reduce_far(grid, sum_fc2, 2)
-    result = (
-        middle + jnp.dot(activated_low, full_fc2, preferred_element_type=F32) + bias_fc2
-    ) * valid
-    out_tokens = result.astype(BF16).reshape(slots, local_len, width)
     grad_b_fc2 = jnp.sum(grad_y, axis=0)
     terms_fc1 = dot_columns(second_low, grad_hidden).astype(BF16)
     grad_b_fc1 = jnp.sum(grad_hidden.astype(F32), axis=0)
@@ -460,6 +469,8 @@
     for slot in range(slots):
         grad_attended = after(grad_attended, ahead)
         grad_queries, own, send = attend_backward(slot, projected, keep, logs[slot], grad_attended)
+        if slot:
+            send = after(send, parts[-1][3])
         came = grid.over_core(send)
         across = add(own[1], came[1])
         ahead = (grad_queries, across) if slot == 0 else (grad_queries, across, parts[-1][3])
@@ -471,6 +482,11 @@
         else:
             ahead = (grad_queries, parts[-1][4])
         parts.append((grad_queries, own[0], came[0], grid.over_x(across), across))
+    activated_late = after(activated_low, parts[-1][4])
+    result = (
+        middle + jnp.dot(activated_late, full_fc2, preferred_element_type=F32) + bias_fc2
+    ) * valid
+    out_tokens = result.astype(BF16).reshape(slots, local_len, width)
     near_two = reduce_near(grid, sum_two, far_two)
     grad_two = reduce_z(grid, sum_two, near_two)
     grad_w_out, grad_w_fc1 = grad_two[:, :width], grad_two[:, width:]

time: 539 us -> 542 us (level)
  waiting for transfers between devices: 175 us -> 155 us
  local copies, waits for them, and re-layouts: 52.7 us -> 66.4 us
  matrix products: 76.5 us -> 82.2 us
    ppermute x15, waiting for transfers between devices: 61.7 us -> 25.9 us  [over_y(): return lax.ppermute(values, 'dp', [(i, i ^ 1) for i in range(self.dp)])]
    ppermute x17, waiting for transfers between devices: 39.3 us -> 56.5 us  [over_x(): return lax.ppermute(values, 'seq', [(i, i ^ 2) for i in range(self.seq)])]
    unnamed x124 -> x160, local copies, waits for them, and re-layouts: 18.1 us -> 29.8 us
    convert_element_type x0 -> x1, other arithmetic: none -> 5.57 us  [shards(): (dot_rows(grad_y_next, full_fc2) * slope.astype(F32)).astype(BF16)]
  transfers between devices with their start and end apart: 85 -> 85, of which waited for: 31 -> 29; matrix products, arithmetic and copies ran while one was open for 31% -> 31% of each run, Pallas kernels for 14% -> 14%
where the time goes in v2:
time: 542 us; the launch traced here: 536 us
  waiting for transfers between devices  155 us (29%)
  other arithmetic  83.6 us (15%)
  matrix products  82.2 us (15%)
  Pallas kernels  75.5 us (14%)
  starting transfers between devices  70.2 us (13%)
  local copies, waits for them, and re-layouts  66.4 us (12%)
    ppermute x27, waiting for transfers between devices, along_z(): lax.ppermute(values, 'dp', [(i, (i + 2 * step) % self.dp) for i in range(...  72.5 us
    ppermute x17, waiting for transfers between devices, over_x(): return lax.ppermute(values, 'seq', [(i, i ^ 2) for i in range(self.seq)])  56.5 us
    pallas_call x3, Pallas kernels, attend_backward(): pl.pallas_call(attend_backward_kernel, grid=(pairs,), in_specs=[pl.BlockS...  34.8 us
    ppermute x27, starting transfers between devices, along_z(): lax.ppermute(values, 'dp', [(i, (i + 2 * step) % self.dp) for i in range(...  30 us
    unnamed x160, local copies, waits for them, and re-layouts  29.8 us
    ppermute x15, waiting for transfers between devices, over_y(): return lax.ppermute(values, 'dp', [(i, i ^ 1) for i in range(self.dp)])  25.9 us
    pallas_call x3, Pallas kernels, attend_forward(): pl.pallas_call(attend_forward_kernel, grid=(pairs,), in_specs=[pl.BlockSp...  24.8 us
    dot_general x5, matrix products, dot_columns(): lax.dot_general(left, right, (((0,), (0,)), ((), ())), preferred_element_...  22 us
  transfers between devices with their start and end apart: 85, of which 29 were waited for; matrix products, arithmetic and copies ran while one was open for 31% of the time, Pallas kernels for 14%

profile of v2, /device:TPU:0, one launch (start us, length us, event | category | flops | bytes accessed | tf_op | source)
XLA Modules:
  0.0 535.6 jit_solution(105087391059112711)
XLA Ops:
  0.7 6.1 %concatenate.73 = bf16[384]{0:T(512)(128)(2,1)S(1)} concatenate(bf16[32]{0:T(256)(128)(2,1)} %param.23, bf16[32]{0:T(256)(128)(2,1)} %param.24, bf16[32]{0:T(256)(128)(2,1)} %param.25, bf16[128]{0:T(256)(128)(2,1)} %param.26, bf16[32]{0:T(256)(128)(2,1)} %param.27, bf16[32]{0:T(256)(128)(2,1)} %param.28, bf16[32]{0:T(256)(128)(2,1)} %param.29, bf16[32]{0:T(256)(128)(2,1)} %param.30, ...), dimensions={0} | concatenate | bytes 1536 | tf_op jit(solution)/shard_map/concatenate | solution.py:383
  19.9 7.2 %collective-permute-done.3 = bf16[32,3072]{1,0:T(8,128)(2,1)S(1)} collective-permute-done((bf16[32,3072]{1,0:T(8,128)(2,1)S(1)}, bf16[32,3072]{1,0:T(8,128)(2,1)S(1)}, u32[]{:S(2)}, u32[]{:S(2)}) %collective-permute-start.3) | collective-permute-done | bytes 196640 | tf_op jit(solution)/shard_map/ppermute | solution.py:42
  27.1 7.4 %collective-permute-done.5 = bf16[32,3072]{1,0:T(8,128)(2,1)S(1)} collective-permute-done((bf16[32,3072]{1,0:T(8,128)(2,1)S(1)}, bf16[32,3072]{1,0:T(8,128)(2,1)S(1)}, u32[]{:S(2)}, u32[]{:S(2)}) %collective-permute-start.5) | collective-permute-done | bytes 196640 | tf_op jit(solution)/shard_map/ppermute | solution.py:42
  39.4 5.2 collective-permute-done.18
  45.1 8.4 %collective-permute-done.19 = bf16[32,5120]{1,0:T(8,128)(2,1)S(1)} collective-permute-done((bf16[32,5120]{1,0:T(8,128)(2,1)S(1)}, bf16[32,5120]{1,0:T(8,128)(2,1)S(1)}, u32[]{:S(2)}, u32[]{:S(2)}) %collective-permute-start.19) | collective-permute-done | bytes 327712 | tf_op jit(solution)/shard_map/ppermute | solution.py:42
  57.1 5.2 collective-permute-done.20
  70.1 5.6 %collective-permute-done.16.refs_8_ = bf16[2,32,3200]{2,1,0:T(8,128)(2,1)S(1)} collective-permute-done((bf16[2,32,3200]{2,1,0:T(8,128)(2,1)S(1)}, bf16[2,32,3200]{2,1,0:T(8,128)(2,1)S(1)}, u32[]{:S(2)}, u32[]{:S(2)}) %collective-permute-start.16) | collective-permute-done | bytes 409632 | tf_op jit(solution)/shard_map/ppermute | solution.py:36
  86.5 5.4 %collective-permute-done.21 = bf16[128,1024]{1,0:T(8,128)(2,1)} collective-permute-done((bf16[128,1024]{1,0:T(8,128)(2,1)S(1)}, bf16[128,1024]{1,0:T(8,128)(2,1)}, u32[]{:S(2)}, u32[]{:S(2)}) %collective-permute-start.21) | collective-permute-done | bytes 262176 | tf_op jit(solution)/shard_map/ppermute | solution.py:42
  99.9 8.4 %assemble.3 = (bf16[4,2,2,2,32,3072]{5,4,3,2,1,0:T(8,128)(2,1)S(1)}, bf16[4,2,2,2,32,128]{5,4,3,2,1,0:T(8,128)(2,1)S(1)}) custom-call(bf16[4,32,3200]{2,1,0:T(8,128)(2,1)S(1)} %pad_maximum_fusion.8.refs_0_, bf16[4,32,3200]{2,1,0:T(8,128)(2,1)S(1)} %copy-done.13, bf16[4,32,3200]{2,1,0:T(8,128)(2,1)} %collective-permute-done.10.refs_2_, ...), custom_call_target="tpu_custom_call" | custom-call | bytes 13107200 | tf_op jit(solution)/shard_map/assemble/pallas_call | solution.py:140
  113.3 5.3 fusion.10
  128.1 18.3 %add_convert_fusion = bf16[1920,3072]{1,0:T(8,128)(2,1)} fusion(bf16[1920,1024]{1,0:T(8,128)(2,1)} %fusion.10, bf16[1024,3072]{1,0:T(8,128)(2,1)} %bitcast.354, f32[3072]{0:T(1024)S(1)} %pad_maximum_fusion.13), kind=kOutput, calls=%fused_computation | convolution fusion | flops 12091392000 | bytes 22032384 | tf_op jit(solution)/shard_map/dot_general | solution.py:416
  160.7 8.3 %attend_forward.5 = (bf16[1,160,1024]{2,1,0:T(8,128)(2,1)S(1)}, f32[1,8,160,2]{3,2,1,0:T(8,128)S(1)}) custom-call(s32[3,1,640]{2,1,0:T(1,128)S(1)} %reshape.453.keep_ref, bf16[4,3,160,3072]{3,2,1,0:T(8,128)(2,1)S(1)} %bitcast.324, bf16[4,3,160,3072]{3,2,1,0:T(8,128)(2,1)S(1)} %bitcast.325, bf16[4,3,160,3072]{3,2,1,0:T(8,128)(2,1)S(1)} %bitcast.326), custom_call_target="tpu_custom_call" | custom-call | tf_op jit(solution)/shard_map/attend_forward/pallas_call | solution.py:238
  169.9 8.3 %attend_forward.4 = (bf16[1,160,1024]{2,1,0:T(8,128)(2,1)S(1)}, f32[1,8,160,2]{3,2,1,0:T(8,128)S(1)}) custom-call(s32[3,1,640]{2,1,0:T(1,128)S(1)} %reshape.453.keep_ref, bf16[4,3,160,3072]{3,2,1,0:T(8,128)(2,1)S(1)} %bitcast.327, bf16[4,3,160,3072]{3,2,1,0:T(8,128)(2,1)S(1)} %bitcast.328, bf16[4,3,160,3072]{3,2,1,0:T(8,128)(2,1)S(1)} %bitcast.329), custom_call_target="tpu_custom_call" | custom-call | tf_op jit(solution)/shard_map/attend_forward/pallas_call | solution.py:238
  179.0 8.3 %attend_forward.3 = (bf16[1,160,1024]{2,1,0:T(8,128)(2,1)S(1)}, f32[1,8,160,2]{3,2,1,0:T(8,128)S(1)}) custom-call(s32[3,1,640]{2,1,0:T(1,128)S(1)} %reshape.453.keep_ref, bf16[4,3,160,3072]{3,2,1,0:T(8,128)(2,1)S(1)} %bitcast.330, bf16[4,3,160,3072]{3,2,1,0:T(8,128)(2,1)S(1)} %bitcast.331, bf16[4,3,160,3072]{3,2,1,0:T(8,128)(2,1)S(1)} %bitcast.332), custom_call_target="tpu_custom_call" | custom-call | tf_op jit(solution)/shard_map/attend_forward/pallas_call | solution.py:238
  201.3 10.4 %fusion.6 = (bf16[480,4096]{1,0:T(8,128)(2,1)}, bf16[480,4096]{1,0:T(8,128)(2,1)S(1)}) fusion(f32[4096]{0:T(1024)S(1)} %fusion.53, bf16[1024,4096]{1,0:T(8,128)(2,1)S(1)} %bitcast.350, f32[1024]{0:T(1024)S(1)} %reshape.491, f32[1024]{0:T(1024)S(1)} %reshape.490, f32[480]{0:T(512)S(1)} %add_rsqrt_fusion.2, f32[480]{0:T(512)S(1)} %broadcast_multiply_fusion.6, ...), kind=kOutput, calls=%fused_computation.14 | convolution fusion | flops 4053073920 | bytes 18251520 | tf_op jit(solution)/shard_map/dot_general | solution.py:435
  236.1 6.4 %fusion.79 = f32[480,4096]{1,0:T(8,128)} fusion(bf16[480,1024]{1,0:T(8,128)(2,1)S(1)} %copy-done.48, bf16[4096,1024]{1,0:T(8,128)(2,1)S(1)} %bitcast.347), kind=kOutput, calls=%fused_computation.240 | convolution fusion | flops 4026531840 | bytes 17235968 | tf_op jit(solution)/shard_map/dot_general | solution.py:206
  242.5 5.6 %multiply_convert_fusion = bf16[480,4096]{1,0:T(8,128)(2,1)S(1)} fusion(f32[480,4096]{1,0:T(8,128)} %fusion.79, bf16[480,4096]{1,0:T(8,128)(2,1)} %get-tuple-element.113), kind=kLoop, calls=%fused_computation.21 | loop fusion | flops 5898240 | bytes 15728640 | tf_op jit(solution)/shard_map/convert_element_type | solution.py:450
  248.1 7.0 %fusion.1 = bf16[4,2,2,128,1024]{4,3,2,1,0:T(8,128)(2,1)S(1)} fusion(bf16[4,2,2,128,1024]{4,3,2,1,0:T(8,128)(2,1)} %collective-permute-done.42, bf16[4,2,2,2,128,1024]{5,4,3,2,1,0:T(8,128)(2,1)} %bitcast.361, s32[]{:T(128)S(6)} %select_n.192), kind=kLoop, calls=%fused_computation.9 | loop fusion | flops 8388608 | bytes 12582916 | tf_op jit(solution)/shard_map/convert_element_type | solution.py:50
  260.8 7.3 %convolution_convert_fusion = bf16[1024,4096]{1,0:T(8,128)(2,1)} fusion(bf16[480,4096]{1,0:T(8,128)(2,1)S(1)} %multiply_convert_fusion, f32[1024]{0:T(1024)S(1)} %reshape.491, f32[1024]{0:T(1024)S(1)} %reshape.490, f32[480,1024]{1,0:T(8,128)S(1)} %copy-done.35, f32[480]{0:T(512)S(1)} %add_rsqrt_fusion.2, f32[480]{0:T(512)S(1)} %broadcast_multiply_fusion.6, ...), kind=kOutput, calls=%fused_computation.25 | convolution fusion | flops 4033675264 | bytes 14302976 | tf_op jit(solution)/shard_map/dot_general | solution.py:210
  272.8 5.9 %multiply_reduce_fusion.1 = (f32[1024]{0:T(1024)S(1)}, f32[480]{0:T(512)S(1)}, f32[480]{0:T(512)S(1)}, f32[1024]{0:T(1024)S(1)}, f32[480,1024]{1,0:T(8,128)}) fusion(f32[480]{0:T(512)S(1)} %add_rsqrt_fusion.2, f32[480]{0:T(512)S(1)} %broadcast_multiply_fusion.6, f32[480,1024]{1,0:T(8,128)S(1)} %copy-done.35, f32[1024]{0:T(1024)S(1)} %reshape.489, ...), kind=kOutput, calls=%fused_computation.57 | convolution fusion | flops 4031443968 | bytes 16276992 | tf_op jit(solution)/shard_map/dot_general | solution.py:206
  311.9 11.6 %attend_backward.3 = (bf16[1,160,1024]{2,1,0:T(8,128)(2,1)S(1)}, bf16[2,2,160,1024]{3,2,1,0:T(8,128)(2,1)S(1)}, bf16[2,2,160,1024]{3,2,1,0:T(8,128)(2,1)S(1)}) custom-call(s32[3,1,640]{2,1,0:T(1,128)S(1)} %reshape.453.keep_ref, bf16[4,3,160,3072]{3,2,1,0:T(8,128)(2,1)S(1)} %bitcast.335, bf16[4,3,160,3072]{3,2,1,0:T(8,128)(2,1)S(1)} %bitcast.336, ...), custom_call_target="tpu_custom_call" | custom-call | tf_op jit(solution)/shard_map/attend_backward/pallas_call | solution.py:297
  334.9 11.6 %attend_backward.4 = (bf16[1,160,1024]{2,1,0:T(8,128)(2,1)S(1)}, bf16[2,2,160,1024]{3,2,1,0:T(8,128)(2,1)S(1)}, bf16[2,2,160,1024]{3,2,1,0:T(8,128)(2,1)S(1)}) custom-call(s32[3,1,640]{2,1,0:T(1,128)S(1)} %reshape.453.keep_ref, bf16[4,3,160,3072]{3,2,1,0:T(8,128)(2,1)S(1)} %bitcast.338, bf16[4,3,160,3072]{3,2,1,0:T(8,128)(2,1)S(1)} %bitcast.339, ...), custom_call_target="tpu_custom_call" | custom-call | tf_op jit(solution)/shard_map/attend_backward/pallas_call | solution.py:297
  348.7 10.0 %collective-permute-done.56 = bf16[128,1024]{1,0:T(8,128)(2,1)S(1)} collective-permute-done((bf16[128,1024]{1,0:T(8,128)(2,1)S(1)}, bf16[128,1024]{1,0:T(8,128)(2,1)S(1)}, u32[]{:S(2)}, u32[]{:S(2)}) %collective-permute-start.56) | collective-permute-done | bytes 262176 | tf_op jit(solution)/shard_map/ppermute | solution.py:42
  360.6 11.6 %attend_backward.5 = (bf16[1,160,1024]{2,1,0:T(8,128)(2,1)S(1)}, bf16[2,2,160,1024]{3,2,1,0:T(8,128)(2,1)S(1)}, bf16[2,2,160,1024]{3,2,1,0:T(8,128)(2,1)S(1)}) custom-call(s32[3,1,640]{2,1,0:T(1,128)S(1)} %reshape.453.keep_ref, bf16[4,3,160,3072]{3,2,1,0:T(8,128)(2,1)S(1)} %bitcast.341, bf16[4,3,160,3072]{3,2,1,0:T(8,128)(2,1)S(1)} %bitcast.342, ...), custom_call_target="tpu_custom_call" | custom-call | tf_op jit(solution)/shard_map/attend_backward/pallas_call | solution.py:297
  381.2 9.2 %collective-permute-done.59 = bf16[4,32,1024]{2,1,0:T(8,128)(2,1)S(1)} collective-permute-done((bf16[4,32,1024]{2,1,0:T(8,128)(2,1)S(1)}, bf16[4,32,1024]{2,1,0:T(8,128)(2,1)S(1)}, u32[]{:S(2)}, u32[]{:S(2)}) %collective-permute-start.59) | collective-permute-done | bytes 262176 | tf_op jit(solution)/shard_map/ppermute | solution.py:39
  392.9 16.0 %collective-permute-done.74 = bf16[4,32,5120]{2,1,0:T(8,128)(2,1)S(1)} collective-permute-done((bf16[4,32,5120]{2,1,0:T(8,128)(2,1)S(1)}, bf16[4,32,5120]{2,1,0:T(8,128)(2,1)S(1)}, u32[]{:S(2)}, u32[]{:S(2)}) %collective-permute-start.74) | collective-permute-done | bytes 1310752 | tf_op jit(solution)/shard_map/ppermute | solution.py:36
  413.4 14.2 %collective-permute-done.50 = bf16[2,160,1024]{2,1,0:T(8,128)(2,1)S(1)} collective-permute-done((bf16[2,160,1024]{2,1,0:T(8,128)(2,1)S(1)}, bf16[2,160,1024]{2,1,0:T(8,128)(2,1)S(1)}, u32[]{:S(2)}, u32[]{:S(2)}) %collective-permute-start.50) | collective-permute-done | bytes 655392 | tf_op jit(solution)/shard_map/ppermute | solution.py:36
  432.8 14.1 %collective-permute-done.77 = bf16[32,5120]{1,0:T(8,128)(2,1)S(1)} collective-permute-done((bf16[32,5120]{1,0:T(8,128)(2,1)S(1)}, bf16[32,5120]{1,0:T(8,128)(2,1)S(1)}, u32[]{:S(2)}, u32[]{:S(2)}) %collective-permute-start.77) | collective-permute-done | bytes 327712 | tf_op jit(solution)/shard_map/ppermute | solution.py:42
  451.6 12.4 %collective-permute-done.52 = bf16[2,160,1024]{2,1,0:T(8,128)(2,1)S(1)} collective-permute-done((bf16[2,160,1024]{2,1,0:T(8,128)(2,1)S(1)}, bf16[2,160,1024]{2,1,0:T(8,128)(2,1)S(1)}, u32[]{:S(2)}, u32[]{:S(2)}) %collective-permute-start.52) | collective-permute-done | bytes 655392 | tf_op jit(solution)/shard_map/ppermute | solution.py:36
  464.8 6.0 %convolution_convert_fusion.2 = bf16[1024,2048]{1,0:T(8,128)(2,1)} fusion(bf16[480,2048]{1,0:T(8,128)(2,1)S(1)} %bitcast.364, bf16[1920,1024]{1,0:T(8,128)(2,1)} %fusion.10), kind=kOutput, calls=%fused_computation.36 | convolution fusion | flops 2015363072 | bytes 7143424 | tf_op jit(solution)/shard_map/dot_general | solution.py:210
  481.1 10.0 %multiply_convert_fusion.2 = bf16[480,1024]{1,0:T(8,128)(2,1)} fusion(f32[480,1024]{1,0:T(8,128)S(1)} %copy-done.36, bf16[480,4096]{1,0:T(8,128)(2,1)} %copy-done.70, bf16[4096,1024]{1,0:T(8,128)(2,1)} %bitcast.348, f32[480]{0:T(512)S(1)} %copy-done.68, f32[1024]{0:T(1024)S(1)} %copy-done.69, f32[1024]{0:T(1024)S(1)} %reshape.489), kind=kOutput, calls=%fused_computation.63 | convolution fusion | flops 4028989440 | bytes 15280000 | tf_op jit(solution)/shard_map/dot_general | solution.py:487
  507.4 6.4 %collective-permute-done.66 = bf16[2,32,2048]{2,1,0:T(8,128)(2,1)S(1)} collective-permute-done((bf16[2,32,2048]{2,1,0:T(8,128)(2,1)S(1)}, bf16[2,32,2048]{2,1,0:T(8,128)(2,1)S(1)}, u32[]{:S(2)}, u32[]{:S(2)}) %collective-permute-start.66) | collective-permute-done | bytes 262176 | tf_op jit(solution)/shard_map/ppermute | solution.py:39
  (468 shorter events, 250.0 us)
Async XLA Ops:
  11.5 23.3 %collective-permute-start.7 = (bf16[3,160,1024]{2,1,0:T(8,128)(2,1)}, bf16[3,160,1024]{2,1,0:T(8,128)(2,1)}, u32[]{:S(2)}, u32[]{:S(2)}) collective-permute-start(bf16[3,160,1024]{2,1,0:T(8,128)(2,1)} %param.16), channel_id=1, source_target_pairs={{0,2},{1,3},{2,0},{3,1},{4,6},{5,7},{6,4},{7,5},{8,10},{9,11},{10,... | collective-permute-start | bytes 2949128 | tf_op jit(solution)/shard_map/ppermute | solution.py:36
  44.6 21.4 %collective-permute-start.8 = (bf16[3,160,1024]{2,1,0:T(8,128)(2,1)}, bf16[3,160,1024]{2,1,0:T(8,128)(2,1)}, u32[]{:S(2)}, u32[]{:S(2)}) collective-permute-start(bf16[3,160,1024]{2,1,0:T(8,128)(2,1)} %collective-permute-done.7), channel_id=1, source_target_pairs={{0,1},{1,0},{2,3},{3,2},{4,5},{5,4},{6,7},{7,6},{8,9},{9,8},{10,11... | collective-permute-start | bytes 2949128 | tf_op jit(solution)/shard_map/ppermute | solution.py:33
  54.6 25.9 %collective-permute-start.9 = (bf16[4,32,3200]{2,1,0:T(8,128)(2,1)S(1)}, bf16[4,32,3200]{2,1,0:T(8,128)(2,1)S(1)}, u32[]{:S(2)}, u32[]{:S(2)}) collective-permute-start(bf16[4,32,3200]{2,1,0:T(8,128)(2,1)S(1)} %pad_maximum_fusion.8.refs_0_), channel_id=1, source_target_pairs={{0,1},{1,0},{2,3},{3,2},{4,5},{5,4},{6,7},{7,6},{8,9},{9,8},{10,11... | collective-permute-start | bytes 2457608 | tf_op jit(solution)/shard_map/ppermute | solution.py:33
  57.0 38.7 %collective-permute-start.12 = (bf16[4,32,3200]{2,1,0:T(8,128)(2,1)}, bf16[4,32,3200]{2,1,0:T(8,128)(2,1)}, u32[]{:S(2)}, u32[]{:S(2)}) collective-permute-start(bf16[4,32,3200]{2,1,0:T(8,128)(2,1)} %collective-permute-done.10.refs_2_), channel_id=1, source_target_pairs={{0,1},{1,0},{2,3},{3,2},{4,5},{5,4},{6,7},{7,6},{8,9},{9,8},{10,11... | collective-permute-start | bytes 2457608 | tf_op jit(solution)/shard_map/ppermute | solution.py:33
  62.3 33.4 %collective-permute-start.13 = (bf16[4,32,3200]{2,1,0:T(8,128)(2,1)S(1)}, bf16[4,32,3200]{2,1,0:T(8,128)(2,1)}, u32[]{:S(2)}, u32[]{:S(2)}) collective-permute-start(bf16[4,32,3200]{2,1,0:T(8,128)(2,1)S(1)} %collective-permute-done.11.refs_4_), channel_id=1, source_target_pairs={{0,1},{1,0},{2,3},{3,2},{4,5},{5,4},{6,7},{7,6},{8,9},{9,8},{10,11... | collective-permute-start | bytes 2457608 | tf_op jit(solution)/shard_map/ppermute | solution.py:33
  91.9 30.3 %collective-permute-start.25 = (bf16[4,32,5120]{2,1,0:T(8,128)(2,1)S(1)}, bf16[4,32,5120]{2,1,0:T(8,128)(2,1)}, u32[]{:S(2)}, u32[]{:S(2)}) collective-permute-start(bf16[4,32,5120]{2,1,0:T(8,128)(2,1)S(1)} %pad_maximum_fusion.2.refs_0_), channel_id=1, source_target_pairs={{0,4},{4,0},{8,12},{12,8},{16,20},{20,16},{24,28},{28,24},{1,5},{5... | collective-permute-start | bytes 3932168 | tf_op jit(solution)/shard_map/ppermute | solution.py:39
  94.2 30.0 %collective-permute-start.24 = (bf16[4,32,5120]{2,1,0:T(8,128)(2,1)S(1)}, bf16[4,32,5120]{2,1,0:T(8,128)(2,1)}, u32[]{:S(2)}, u32[]{:S(2)}) collective-permute-start(bf16[4,32,5120]{2,1,0:T(8,128)(2,1)S(1)} %pad_maximum_fusion.2.refs_0_), channel_id=1, source_target_pairs={{0,2},{1,3},{2,0},{3,1},{4,6},{5,7},{6,4},{7,5},{8,10},{9,11},{10,... | collective-permute-start | bytes 3932168 | tf_op jit(solution)/shard_map/ppermute | solution.py:36
  95.7 52.0 %collective-permute-start.28 = (bf16[4,32,5120]{2,1,0:T(8,128)(2,1)S(1)}, bf16[4,32,5120]{2,1,0:T(8,128)(2,1)}, u32[]{:S(2)}, u32[]{:S(2)}) collective-permute-start(bf16[4,32,5120]{2,1,0:T(8,128)(2,1)S(1)} %pad_maximum_fusion.2.refs_0_), channel_id=1, source_target_pairs={{0,1},{1,0},{2,3},{3,2},{4,5},{5,4},{6,7},{7,6},{8,9},{9,8},{10,11... | collective-permute-start | bytes 3932168 | tf_op jit(solution)/shard_map/ppermute | solution.py:33
  125.4 22.3 %collective-permute-start.29 = (bf16[4,32,5120]{2,1,0:T(8,128)(2,1)}, bf16[4,32,5120]{2,1,0:T(8,128)(2,1)S(1)}, u32[]{:S(2)}, u32[]{:S(2)}) collective-permute-start(bf16[4,32,5120]{2,1,0:T(8,128)(2,1)} %collective-permute-done.24.refs_2_), channel_id=1, source_target_pairs={{0,1},{1,0},{2,3},{3,2},{4,5},{5,4},{6,7},{7,6},{8,9},{9,8},{10,11... | collective-permute-start | bytes 3932168 | tf_op jit(solution)/shard_map/ppermute | solution.py:33
  126.6 22.2 %collective-permute-start.30 = (bf16[4,32,5120]{2,1,0:T(8,128)(2,1)}, bf16[4,32,5120]{2,1,0:T(8,128)(2,1)S(1)}, u32[]{:S(2)}, u32[]{:S(2)}) collective-permute-start(bf16[4,32,5120]{2,1,0:T(8,128)(2,1)} %collective-permute-done.25.refs_4_), channel_id=1, source_target_pairs={{0,1},{1,0},{2,3},{3,2},{4,5},{5,4},{6,7},{7,6},{8,9},{9,8},{10,11... | collective-permute-start | bytes 3932168 | tf_op jit(solution)/shard_map/ppermute | solution.py:33
  149.8 44.8 %collective-permute-start.32 = (bf16[4,128,1024]{2,1,0:T(8,128)(2,1)S(1)}, bf16[4,128,1024]{2,1,0:T(8,128)(2,1)S(1)}, u32[]{:S(2)}, u32[]{:S(2)}) collective-permute-start(bf16[4,128,1024]{2,1,0:T(8,128)(2,1)S(1)} %pad_maximum_fusion.3.refs_0_), channel_id=1, source_target_pairs={{0,4},{4,0},{8,12},{12,8},{16,20},{20,16},{24,28},{28,24},{1,5},{5... | collective-permute-start | bytes 3145736 | tf_op jit(solution)/shard_map/ppermute | solution.py:39
  151.4 43.3 %collective-permute-start.31 = (bf16[4,128,1024]{2,1,0:T(8,128)(2,1)S(1)}, bf16[4,128,1024]{2,1,0:T(8,128)(2,1)}, u32[]{:S(2)}, u32[]{:S(2)}) collective-permute-start(bf16[4,128,1024]{2,1,0:T(8,128)(2,1)S(1)} %pad_maximum_fusion.3.refs_0_), channel_id=1, source_target_pairs={{0,2},{1,3},{2,0},{3,1},{4,6},{5,7},{6,4},{7,5},{8,10},{9,11},{10,... | collective-permute-start | bytes 3145736 | tf_op jit(solution)/shard_map/ppermute | solution.py:36
  153.0 35.3 %collective-permute-start.33 = (bf16[2,32,5120]{2,1,0:T(8,128)(2,1)}, bf16[2,32,5120]{2,1,0:T(8,128)(2,1)}, u32[]{:S(2)}, u32[]{:S(2)}) collective-permute-start(bf16[2,32,5120]{2,1,0:T(8,128)(2,1)} %collective-permute-done.26.refs_6_), channel_id=1, source_target_pairs={{0,1},{1,0},{2,3},{3,2},{4,5},{5,4},{6,7},{7,6},{8,9},{9,8},{10,11... | collective-permute-start | bytes 1966088 | tf_op jit(solution)/shard_map/ppermute | solution.py:33
  153.1 35.2 %collective-permute-start.34 = (bf16[2,32,5120]{2,1,0:T(8,128)(2,1)}, bf16[2,32,5120]{2,1,0:T(8,128)(2,1)}, u32[]{:S(2)}, u32[]{:S(2)}) collective-permute-start(bf16[2,32,5120]{2,1,0:T(8,128)(2,1)} %collective-permute-done.27.refs_8_), channel_id=1, source_target_pairs={{0,1},{1,0},{2,3},{3,2},{4,5},{5,4},{6,7},{7,6},{8,9},{9,8},{10,11... | collective-permute-start | bytes 1966088 | tf_op jit(solution)/shard_map/ppermute | solution.py:33
  188.1 23.7 %collective-permute-start.37 = (bf16[4,128,1024]{2,1,0:T(8,128)(2,1)S(1)}, bf16[4,128,1024]{2,1,0:T(8,128)(2,1)S(1)}, u32[]{:S(2)}, u32[]{:S(2)}) collective-permute-start(bf16[4,128,1024]{2,1,0:T(8,128)(2,1)S(1)} %pad_maximum_fusion.3.refs_0_), channel_id=1, source_target_pairs={{0,1},{1,0},{2,3},{3,2},{4,5},{5,4},{6,7},{7,6},{8,9},{9,8},{10,11... | collective-permute-start | bytes 3145736 | tf_op jit(solution)/shard_map/ppermute | solution.py:33
  221.2 26.8 %collective-permute-start.42 = (bf16[4,2,2,128,1024]{4,3,2,1,0:T(8,128)(2,1)}, bf16[4,2,2,128,1024]{4,3,2,1,0:T(8,128)(2,1)}, u32[]{:S(2)}, u32[]{:S(2)}) collective-permute-start(bf16[4,2,2,128,1024]{4,3,2,1,0:T(8,128)(2,1)} %dynamic-slice_bitcast_fusion.1), channel_id=1, source_target_pairs={{0,1},{1,0},{2,3},{3,2},{4,5},{5,4},{6,7},{7,6},{8,9},{9,8},{10,11... | collective-permute-start | bytes 12582920 | tf_op jit(solution)/shard_map/ppermute | solution.py:33
  258.3 30.1 %collective-permute-start.43 = (bf16[2,128,1024]{2,1,0:T(8,128)(2,1)}, bf16[2,128,1024]{2,1,0:T(8,128)(2,1)}, u32[]{:S(2)}, u32[]{:S(2)}) collective-permute-start(bf16[2,128,1024]{2,1,0:T(8,128)(2,1)} %get-tuple-element.164), channel_id=1, source_target_pairs={{0,2},{1,3},{2,0},{3,1},{4,6},{5,7},{6,4},{7,5},{8,10},{9,11},{10,... | collective-permute-start | bytes 1572872 | tf_op jit(solution)/shard_map/ppermute | solution.py:36
  259.3 29.1 %collective-permute-start.44 = (bf16[2,128,1024]{2,1,0:T(8,128)(2,1)}, bf16[2,128,1024]{2,1,0:T(8,128)(2,1)}, u32[]{:S(2)}, u32[]{:S(2)}) collective-permute-start(bf16[2,128,1024]{2,1,0:T(8,128)(2,1)} %get-tuple-element.165), channel_id=1, source_target_pairs={{0,4},{4,0},{8,12},{12,8},{16,20},{20,16},{24,28},{28,24},{1,5},{5... | collective-permute-start | bytes 1572872 | tf_op jit(solution)/shard_map/ppermute | solution.py:39
  272.8 29.0 %collective-permute-start.46 = (bf16[4,2,2,32,4096]{4,3,2,1,0:T(8,128)(2,1)}, bf16[4,2,2,32,4096]{4,3,2,1,0:T(8,128)(2,1)}, u32[]{:S(2)}, u32[]{:S(2)}) collective-permute-start(bf16[4,2,2,32,4096]{4,3,2,1,0:T(8,128)(2,1)} %dynamic-slice_bitcast_fusion), channel_id=1, source_target_pairs={{0,1},{1,0},{2,3},{3,2},{4,5},{5,4},{6,7},{7,6},{8,9},{9,8},{10,11... | collective-permute-start | bytes 12582920 | tf_op jit(solution)/shard_map/ppermute | solution.py:33
  293.8 29.8 %collective-permute-start.53 = (bf16[4,128,1024]{2,1,0:T(8,128)(2,1)}, bf16[4,128,1024]{2,1,0:T(8,128)(2,1)}, u32[]{:S(2)}, u32[]{:S(2)}) collective-permute-start(bf16[4,128,1024]{2,1,0:T(8,128)(2,1)} %pad_maximum_fusion.4), channel_id=1, source_target_pairs={{0,2},{1,3},{2,0},{3,1},{4,6},{5,7},{6,4},{7,5},{8,10},{9,11},{10,... | collective-permute-start | bytes 3145736 | tf_op jit(solution)/shard_map/ppermute | solution.py:36
  296.8 26.8 %collective-permute-start.54 = (bf16[4,128,1024]{2,1,0:T(8,128)(2,1)}, bf16[4,128,1024]{2,1,0:T(8,128)(2,1)}, u32[]{:S(2)}, u32[]{:S(2)}) collective-permute-start(bf16[4,128,1024]{2,1,0:T(8,128)(2,1)} %pad_maximum_fusion.5), channel_id=1, source_target_pairs={{0,4},{4,0},{8,12},{12,8},{16,20},{20,16},{24,28},{28,24},{1,5},{5... | collective-permute-start | bytes 3145736 | tf_op jit(solution)/shard_map/ppermute | solution.py:39
  323.6 23.0 %collective-permute-start.47 = (bf16[2,2,160,1024]{3,2,1,0:T(8,128)(2,1)S(1)}, bf16[2,2,160,1024]{3,2,1,0:T(8,128)(2,1)S(1)}, u32[]{:S(2)}, u32[]{:S(2)}) collective-permute-start(bf16[2,2,160,1024]{3,2,1,0:T(8,128)(2,1)S(1)} %get-tuple-element.125), channel_id=1, source_target_pairs={{0,1},{1,0},{2,3},{3,2},{4,5},{5,4},{6,7},{7,6},{8,9},{9,8},{10,11... | collective-permute-start | bytes 3932168 | tf_op jit(solution)/shard_map/ppermute | solution.py:33
  325.0 50.5 %collective-permute-start.73 = (bf16[4,32,5120]{2,1,0:T(8,128)(2,1)S(1)}, bf16[4,32,5120]{2,1,0:T(8,128)(2,1)}, u32[]{:S(2)}, u32[]{:S(2)}) collective-permute-start(bf16[4,32,5120]{2,1,0:T(8,128)(2,1)S(1)} %dynamic-slice_bitcast_fusion.3), channel_id=1, source_target_pairs={{0,4},{4,0},{8,12},{12,8},{16,20},{20,16},{24,28},{28,24},{1,5},{5... | collective-permute-start | bytes 3932168 | tf_op jit(solution)/shard_map/ppermute | solution.py:39
  330.1 62.8 %collective-permute-start.75 = (bf16[4,32,5120]{2,1,0:T(8,128)(2,1)}, bf16[4,32,5120]{2,1,0:T(8,128)(2,1)S(1)}, u32[]{:S(2)}, u32[]{:S(2)}) collective-permute-start(bf16[4,32,5120]{2,1,0:T(8,128)(2,1)} %fusion.25), channel_id=1, source_target_pairs={{0,4},{4,0},{8,12},{12,8},{16,20},{20,16},{24,28},{28,24},{1,5},{5... | collective-permute-start | bytes 3932168 | tf_op jit(solution)/shard_map/ppermute | solution.py:39
  347.7 27.3 %collective-permute-start.48 = (bf16[2,160,1024]{2,1,0:T(8,128)(2,1)}, bf16[2,160,1024]{2,1,0:T(8,128)(2,1)S(1)}, u32[]{:S(2)}, u32[]{:S(2)}) collective-permute-start(bf16[2,160,1024]{2,1,0:T(8,128)(2,1)} %fusion.34), channel_id=1, source_target_pairs={{0,2},{1,3},{2,0},{3,1},{4,6},{5,7},{6,4},{7,5},{8,10},{9,11},{10,... | collective-permute-start | bytes 1966088 | tf_op jit(solution)/shard_map/ppermute | solution.py:36
  377.1 31.7 %collective-permute-start.74 = (bf16[4,32,5120]{2,1,0:T(8,128)(2,1)S(1)}, bf16[4,32,5120]{2,1,0:T(8,128)(2,1)S(1)}, u32[]{:S(2)}, u32[]{:S(2)}) collective-permute-start(bf16[4,32,5120]{2,1,0:T(8,128)(2,1)S(1)} %fusion.12), channel_id=1, source_target_pairs={{0,2},{1,3},{2,0},{3,1},{4,6},{5,7},{6,4},{7,5},{8,10},{9,11},{10,... | collective-permute-start | bytes 3932168 | tf_op jit(solution)/shard_map/ppermute | solution.py:36
  380.6 47.0 %collective-permute-start.61 = (bf16[4,32,1024]{2,1,0:T(8,128)(2,1)S(1)}, bf16[4,32,1024]{2,1,0:T(8,128)(2,1)S(1)}, u32[]{:S(2)}, u32[]{:S(2)}) collective-permute-start(bf16[4,32,1024]{2,1,0:T(8,128)(2,1)S(1)} %get-tuple-element.174), channel_id=1, source_target_pairs={{0,4},{4,0},{8,12},{12,8},{16,20},{20,16},{24,28},{28,24},{1,5},{5... | collective-permute-start | bytes 786440 | tf_op jit(solution)/shard_map/ppermute | solution.py:39
  390.5 37.2 %collective-permute-start.60 = (bf16[4,32,1024]{2,1,0:T(8,128)(2,1)S(1)}, bf16[4,32,1024]{2,1,0:T(8,128)(2,1)S(1)}, u32[]{:S(2)}, u32[]{:S(2)}) collective-permute-start(bf16[4,32,1024]{2,1,0:T(8,128)(2,1)S(1)} %fusion.41), channel_id=1, source_target_pairs={{0,2},{1,3},{2,0},{3,1},{4,6},{5,7},{6,4},{7,5},{8,10},{9,11},{10,... | collective-permute-start | bytes 786440 | tf_op jit(solution)/shard_map/ppermute | solution.py:36
  391.8 35.8 %collective-permute-start.50 = (bf16[2,160,1024]{2,1,0:T(8,128)(2,1)S(1)}, bf16[2,160,1024]{2,1,0:T(8,128)(2,1)S(1)}, u32[]{:S(2)}, u32[]{:S(2)}) collective-permute-start(bf16[2,160,1024]{2,1,0:T(8,128)(2,1)S(1)} %fusion.35), channel_id=1, source_target_pairs={{0,2},{1,3},{2,0},{3,1},{4,6},{5,7},{6,4},{7,5},{8,10},{9,11},{10,... | collective-permute-start | bytes 1966088 | tf_op jit(solution)/shard_map/ppermute | solution.py:36
  409.5 21.2 %collective-permute-start.76 = (bf16[32,5120]{1,0:T(8,128)(2,1)S(1)}, bf16[32,5120]{1,0:T(8,128)(2,1)S(1)}, u32[]{:S(2)}, u32[]{:S(2)}) collective-permute-start(bf16[32,5120]{1,0:T(8,128)(2,1)S(1)} %get-tuple-element.170), channel_id=1, source_target_pairs={{0,8},{4,12},{8,16},{12,20},{16,24},{20,28},{24,0},{28,4},{1,9},{5... | collective-permute-start | bytes 983048 | tf_op jit(solution)/shard_map/ppermute | solution.py:42
  409.6 22.1 %collective-permute-start.78 = (bf16[32,5120]{1,0:T(8,128)(2,1)S(1)}, bf16[32,5120]{1,0:T(8,128)(2,1)S(1)}, u32[]{:S(2)}, u32[]{:S(2)}) collective-permute-start(bf16[32,5120]{1,0:T(8,128)(2,1)S(1)} %get-tuple-element.171), channel_id=1, source_target_pairs={{0,24},{4,28},{8,0},{12,4},{16,8},{20,12},{24,16},{28,20},{1,25},{... | collective-permute-start | bytes 983048 | tf_op jit(solution)/shard_map/ppermute | solution.py:42
  427.8 20.6 %collective-permute-start.62 = (bf16[32,1024]{1,0:T(8,128)(2,1)S(1)}, bf16[32,1024]{1,0:T(8,128)(2,1)S(1)}, u32[]{:S(2)}, u32[]{:S(2)}) collective-permute-start(bf16[32,1024]{1,0:T(8,128)(2,1)S(1)} %get-tuple-element.187), channel_id=1, source_target_pairs={{0,8},{4,12},{8,16},{12,20},{16,24},{20,28},{24,0},{28,4},{1,9},{5... | collective-permute-start | bytes 196616 | tf_op jit(solution)/shard_map/ppermute | solution.py:42
  (131 other events, 1196.9 us)

commit v3 on v1

--- a/solution.py
+++ b/solution.py
@@ -384,7 +384,7 @@
     column_two = gather_z(grid, after(jnp.concatenate([w_out, w_fc1], axis=1), column_one, by_x))
     near_one = lax.optimization_barrier(near_one)
     far_one = gather_far(grid, *near_one)
-    seen = jnp.stack([tokens, by_core, by_x, grid.over_core(by_x)])
+    seen = lax.optimization_barrier(jnp.stack([tokens, by_core, by_x, grid.over_core(by_x)]))
     full_qkv, vectors = assemble(grid, (w_qkv.shape[1], LANES), column_one, near_one, far_one)
     column_two = after(column_two, far_one)
     near_two = gather_near(grid, column_two)

time: 539 us -> 543 us (level)
  waiting for transfers between devices: 175 us -> 166 us
    ppermute x15, waiting for transfers between devices: 61.7 us -> 55.4 us  [over_y(): return lax.ppermute(values, 'dp', [(i, i ^ 1) for i in range(self.dp)])]
    ppermute x17, waiting for transfers between devices: 39.3 us -> 33.9 us  [over_x(): return lax.ppermute(values, 'seq', [(i, i ^ 2) for i in range(self.seq)])]
    unnamed x124 -> x134, local copies, waits for them, and re-layouts: 18.1 us -> 17.4 us
  transfers between devices with their start and end apart: 85 -> 85, of which waited for: 31 -> 30; matrix products, arithmetic and copies ran while one was open for 31% -> 32% of each run, Pallas kernels for 14% -> 15%
where the time goes in v3:
time: 543 us; the launch traced here: 536 us
  waiting for transfers between devices  166 us (31%)
  other arithmetic  83.2 us (15%)
  matrix products  80.8 us (15%)
  Pallas kernels  78.1 us (14%)
  starting transfers between devices  74.4 us (14%)
  local copies, waits for them, and re-layouts  50.9 us (9%)
    ppermute x27, waiting for transfers between devices, along_z(): lax.ppermute(values, 'dp', [(i, (i + 2 * step) % self.dp) for i in range(...  76.2 us
    ppermute x15, waiting for transfers between devices, over_y(): return lax.ppermute(values, 'dp', [(i, i ^ 1) for i in range(self.dp)])  55.4 us
    pallas_call x3, Pallas kernels, attend_backward(): pl.pallas_call(attend_backward_kernel, grid=(pairs,), in_specs=[pl.BlockS...  34.8 us
    ppermute x17, waiting for transfers between devices, over_x(): return lax.ppermute(values, 'seq', [(i, i ^ 2) for i in range(self.seq)])  33.9 us
    ppermute x27, starting transfers between devices, along_z(): lax.ppermute(values, 'dp', [(i, (i + 2 * step) % self.dp) for i in range(...  32.8 us
    pallas_call x3, Pallas kernels, attend_forward(): pl.pallas_call(attend_forward_kernel, grid=(pairs,), in_specs=[pl.BlockSp...  24.8 us
    convert_element_type x14, other arithmetic, add(): return (left.astype(F32) + right.astype(F32)).astype(left.dtype)  24 us
    dot_general x4, matrix products, dot_rows(): lax.dot_general(left, right, (((1,), (1,)), ((), ())), preferred_element_...  23 us
  transfers between devices with their start and end apart: 85, of which 30 were waited for; matrix products, arithmetic and copies ran while one was open for 32% of the time, Pallas kernels for 15%

profile of v3, /device:TPU:0, one launch (start us, length us, event | category | flops | bytes accessed | tf_op | source)
XLA Modules:
  0.0 535.6 jit_solution(17754750265871372181)
XLA Ops:
  0.7 6.1 %concatenate.73 = bf16[384]{0:T(512)(128)(2,1)S(1)} concatenate(bf16[32]{0:T(256)(128)(2,1)} %param.23, bf16[32]{0:T(256)(128)(2,1)} %param.24, bf16[32]{0:T(256)(128)(2,1)} %param.25, bf16[128]{0:T(256)(128)(2,1)} %param.26, bf16[32]{0:T(256)(128)(2,1)} %param.27, bf16[32]{0:T(256)(128)(2,1)} %param.28, bf16[32]{0:T(256)(128)(2,1)} %param.29, bf16[32]{0:T(256)(128)(2,1)} %param.30, ...), dimensions={0} | concatenate | bytes 1536 | tf_op jit(solution)/shard_map/concatenate | solution.py:379
  19.9 7.2 %collective-permute-done.3 = bf16[32,3072]{1,0:T(8,128)(2,1)S(1)} collective-permute-done((bf16[32,3072]{1,0:T(8,128)(2,1)S(1)}, bf16[32,3072]{1,0:T(8,128)(2,1)S(1)}, u32[]{:S(2)}, u32[]{:S(2)}) %collective-permute-start.3) | collective-permute-done | bytes 196640 | tf_op jit(solution)/shard_map/ppermute | solution.py:42
  27.1 7.4 %collective-permute-done.5 = bf16[32,3072]{1,0:T(8,128)(2,1)S(1)} collective-permute-done((bf16[32,3072]{1,0:T(8,128)(2,1)S(1)}, bf16[32,3072]{1,0:T(8,128)(2,1)S(1)}, u32[]{:S(2)}, u32[]{:S(2)}) %collective-permute-start.5) | collective-permute-done | bytes 196640 | tf_op jit(solution)/shard_map/ppermute | solution.py:42
  46.1 7.4 %collective-permute-done.19 = bf16[32,5120]{1,0:T(8,128)(2,1)} collective-permute-done((bf16[32,5120]{1,0:T(8,128)(2,1)S(1)}, bf16[32,5120]{1,0:T(8,128)(2,1)}, u32[]{:S(2)}, u32[]{:S(2)}) %collective-permute-start.19) | collective-permute-done | bytes 327712 | tf_op jit(solution)/shard_map/ppermute | solution.py:42
  77.3 5.5 %collective-permute-done.30 = bf16[128,1024]{1,0:T(8,128)(2,1)} collective-permute-done((bf16[128,1024]{1,0:T(8,128)(2,1)S(1)}, bf16[128,1024]{1,0:T(8,128)(2,1)}, u32[]{:S(2)}, u32[]{:S(2)}) %collective-permute-start.30) | collective-permute-done | bytes 262176 | tf_op jit(solution)/shard_map/ppermute | solution.py:42
  93.4 10.0 %assemble.3 = (bf16[4,2,2,2,32,3072]{5,4,3,2,1,0:T(8,128)(2,1)S(1)}, bf16[4,2,2,2,32,128]{5,4,3,2,1,0:T(8,128)(2,1)S(1)}) custom-call(bf16[4,32,3200]{2,1,0:T(8,128)(2,1)S(1)} %pad_maximum_fusion.9.refs_0_, bf16[4,32,3200]{2,1,0:T(8,128)(2,1)S(1)} %copy-done.7, bf16[4,32,3200]{2,1,0:T(8,128)(2,1)S(1)} %collective-permute-done.10.refs_2_, ...), custom_call_target="tpu_custom_call" | custom-call | bytes 13107200 | tf_op jit(solution)/shard_map/assemble/pallas_call | solution.py:136
  119.3 7.5 %collective-permute-done.26.refs_6_ = bf16[2,32,5120]{2,1,0:T(8,128)(2,1)} collective-permute-done((bf16[2,32,5120]{2,1,0:T(8,128)(2,1)S(1)}, bf16[2,32,5120]{2,1,0:T(8,128)(2,1)}, u32[]{:S(2)}, u32[]{:S(2)}) %collective-permute-start.26) | collective-permute-done | bytes 655392 | tf_op jit(solution)/shard_map/ppermute | solution.py:39
  128.2 15.7 %add_convert_fusion = bf16[1920,3072]{1,0:T(8,128)(2,1)S(1)} fusion(bf16[1920,1024]{1,0:T(8,128)(2,1)} %fusion.10, bf16[1024,3072]{1,0:T(8,128)(2,1)} %bitcast.354, f32[3072]{0:T(1024)S(1)} %pad_maximum_fusion.14), kind=kOutput, calls=%fused_computation | convolution fusion | flops 12091392000 | bytes 22032384 | tf_op jit(solution)/shard_map/dot_general | solution.py:410
  143.9 8.3 %attend_forward.5 = (bf16[1,160,1024]{2,1,0:T(8,128)(2,1)S(1)}, f32[1,8,160,2]{3,2,1,0:T(8,128)S(1)}) custom-call(s32[3,1,640]{2,1,0:T(1,128)S(1)} %reshape.453.keep_ref, bf16[4,3,160,3072]{3,2,1,0:T(8,128)(2,1)S(1)} %bitcast.324, bf16[4,3,160,3072]{3,2,1,0:T(8,128)(2,1)S(1)} %bitcast.325, bf16[4,3,160,3072]{3,2,1,0:T(8,128)(2,1)S(1)} %bitcast.326), custom_call_target="tpu_custom_call" | custom-call | tf_op jit(solution)/shard_map/attend_forward/pallas_call | solution.py:234
  153.1 8.3 %attend_forward.4 = (bf16[1,160,1024]{2,1,0:T(8,128)(2,1)S(1)}, f32[1,8,160,2]{3,2,1,0:T(8,128)S(1)}) custom-call(s32[3,1,640]{2,1,0:T(1,128)S(1)} %reshape.453.keep_ref, bf16[4,3,160,3072]{3,2,1,0:T(8,128)(2,1)S(1)} %bitcast.327, bf16[4,3,160,3072]{3,2,1,0:T(8,128)(2,1)S(1)} %bitcast.328, bf16[4,3,160,3072]{3,2,1,0:T(8,128)(2,1)S(1)} %bitcast.329), custom_call_target="tpu_custom_call" | custom-call | tf_op jit(solution)/shard_map/attend_forward/pallas_call | solution.py:234
  162.2 8.3 %attend_forward.3 = (bf16[1,160,1024]{2,1,0:T(8,128)(2,1)S(1)}, f32[1,8,160,2]{3,2,1,0:T(8,128)S(1)}) custom-call(s32[3,1,640]{2,1,0:T(1,128)S(1)} %reshape.453.keep_ref, bf16[4,3,160,3072]{3,2,1,0:T(8,128)(2,1)S(1)} %bitcast.330, bf16[4,3,160,3072]{3,2,1,0:T(8,128)(2,1)S(1)} %bitcast.331, bf16[4,3,160,3072]{3,2,1,0:T(8,128)(2,1)S(1)} %bitcast.332), custom_call_target="tpu_custom_call" | custom-call | tf_op jit(solution)/shard_map/attend_forward/pallas_call | solution.py:234
  185.6 12.2 %fusion.6 = (bf16[480,4096]{1,0:T(8,128)(2,1)}, bf16[480,4096]{1,0:T(8,128)(2,1)}) fusion(f32[4096]{0:T(1024)S(1)} %fusion.53, bf16[1024,4096]{1,0:T(8,128)(2,1)S(1)} %bitcast.350, f32[1024]{0:T(1024)S(1)} %reshape.491, f32[1024]{0:T(1024)S(1)} %reshape.490, f32[480]{0:T(512)S(1)} %add_rsqrt_fusion.2, f32[480]{0:T(512)S(1)} %broadcast_multiply_fusion.6, ...), kind=kOutput, calls=%fused_computation.14 | convolution fusion | flops 4053073920 | bytes 18251520 | tf_op jit(solution)/shard_map/dot_general | solution.py:425
  197.8 7.0 %convolution_convert_fusion.1 = bf16[4096,1024]{1,0:T(8,128)(2,1)S(1)} fusion(bf16[480,4096]{1,0:T(8,128)(2,1)} %get-tuple-element.78, bf16[480,1024]{1,0:T(8,128)(2,1)S(1)} %copy-done.45), kind=kOutput, calls=%fused_computation.26 | convolution fusion | flops 4030726144 | bytes 13303808 | tf_op jit(solution)/shard_map/dot_general | solution.py:206
  228.3 7.9 %multiply_convert_fusion = bf16[480,4096]{1,0:T(8,128)(2,1)} fusion(bf16[480,4096]{1,0:T(8,128)(2,1)} %get-tuple-element.85, bf16[480,1024]{1,0:T(8,128)(2,1)S(1)} %copy-done.46, bf16[4096,1024]{1,0:T(8,128)(2,1)S(1)} %bitcast.347), kind=kOutput, calls=%fused_computation.21 | convolution fusion | flops 4032430080 | bytes 17235968 | tf_op jit(solution)/shard_map/dot_general | solution.py:202
  236.2 7.3 %multiply_convert_fusion.2 = bf16[480,1024]{1,0:T(8,128)(2,1)} fusion(f32[480,1024]{1,0:T(8,128)S(1)} %copy-done.26, bf16[480,4096]{1,0:T(8,128)(2,1)} %get-tuple-element.78, bf16[4096,1024]{1,0:T(8,128)(2,1)S(1)} %bitcast.348, f32[480]{0:T(512)S(1)} %reshape.493, f32[1024]{0:T(1024)S(1)} %reshape.494, f32[1024]{0:T(1024)S(1)} %reshape.489), kind=kOutput, calls=%fused_computation.66 | convolution fusion | flops 4028989440 | bytes 15280000 | tf_op jit(solution)/shard_map/dot_general | solution.py:441
  243.5 5.8 %fusion.1 = bf16[4,2,2,128,1024]{4,3,2,1,0:T(8,128)(2,1)S(1)} fusion(bf16[4,2,2,128,1024]{4,3,2,1,0:T(8,128)(2,1)} %collective-permute-done.42, bf16[4,2,2,2,128,1024]{5,4,3,2,1,0:T(8,128)(2,1)} %bitcast.361, s32[]{:T(128)S(6)} %select_n.192), kind=kLoop, calls=%fused_computation.9 | loop fusion | flops 8388608 | bytes 12582916 | tf_op jit(solution)/shard_map/convert_element_type | solution.py:50
  249.4 7.4 %convolution_convert_fusion = bf16[1024,4096]{1,0:T(8,128)(2,1)} fusion(bf16[480,4096]{1,0:T(8,128)(2,1)S(1)} %copy-done.32, f32[1024]{0:T(1024)S(1)} %reshape.491, f32[1024]{0:T(1024)S(1)} %reshape.490, f32[480,1024]{1,0:T(8,128)S(1)} %copy-done.26, f32[480]{0:T(512)S(1)} %add_rsqrt_fusion.2, f32[480]{0:T(512)S(1)} %broadcast_multiply_fusion.6, ...), kind=kOutput, calls=%fused_computation.25 | convolution fusion | flops 4033675264 | bytes 14302976 | tf_op jit(solution)/shard_map/dot_general | solution.py:206
  265.2 5.9 %multiply_reduce_fusion.1 = (f32[1024]{0:T(1024)S(1)}, f32[480]{0:T(512)S(1)}, f32[480]{0:T(512)S(1)}, f32[1024]{0:T(1024)S(1)}, f32[480,1024]{1,0:T(8,128)}) fusion(f32[480]{0:T(512)S(1)} %add_rsqrt_fusion.2, f32[480]{0:T(512)S(1)} %broadcast_multiply_fusion.6, f32[480,1024]{1,0:T(8,128)S(1)} %copy-done.26, f32[1024]{0:T(1024)S(1)} %reshape.489, ...), kind=kOutput, calls=%fused_computation.58 | convolution fusion | flops 4031443968 | bytes 16276992 | tf_op jit(solution)/shard_map/dot_general | solution.py:202
  292.9 7.4 %fusion = bf16[4,2,2,32,4096]{4,3,2,1,0:T(8,128)(2,1)} fusion(bf16[4,2,2,32,4096]{4,3,2,1,0:T(8,128)(2,1)} %collective-permute-done.46, bf16[4,2,2,2,32,4096]{5,4,3,2,1,0:T(8,128)(2,1)} %bitcast.363, s32[]{:T(128)S(6)} %select_n.192), kind=kLoop, calls=%fused_computation.7 | loop fusion | flops 8388608 | bytes 12582916 | tf_op jit(solution)/shard_map/convert_element_type | solution.py:50
  300.3 5.3 pad_maximum_fusion
  305.6 11.6 %attend_backward.3 = (bf16[1,160,1024]{2,1,0:T(8,128)(2,1)S(1)}, bf16[2,2,160,1024]{3,2,1,0:T(8,128)(2,1)S(1)}, bf16[2,2,160,1024]{3,2,1,0:T(8,128)(2,1)S(1)}) custom-call(s32[3,1,640]{2,1,0:T(1,128)S(1)} %reshape.453.keep_ref, bf16[4,3,160,3072]{3,2,1,0:T(8,128)(2,1)S(1)} %bitcast.335, bf16[4,3,160,3072]{3,2,1,0:T(8,128)(2,1)S(1)} %bitcast.336, ...), custom_call_target="tpu_custom_call" | custom-call | tf_op jit(solution)/shard_map/attend_backward/pallas_call | solution.py:293
  317.3 11.6 %attend_backward.4 = (bf16[1,160,1024]{2,1,0:T(8,128)(2,1)S(1)}, bf16[2,2,160,1024]{3,2,1,0:T(8,128)(2,1)S(1)}, bf16[2,2,160,1024]{3,2,1,0:T(8,128)(2,1)S(1)}) custom-call(s32[3,1,640]{2,1,0:T(1,128)S(1)} %reshape.453.keep_ref, bf16[4,3,160,3072]{3,2,1,0:T(8,128)(2,1)S(1)} %bitcast.338, bf16[4,3,160,3072]{3,2,1,0:T(8,128)(2,1)S(1)} %bitcast.339, ...), custom_call_target="tpu_custom_call" | custom-call | tf_op jit(solution)/shard_map/attend_backward/pallas_call | solution.py:293
  345.4 15.4 %collective-permute-done.56 = bf16[128,1024]{1,0:T(8,128)(2,1)S(1)} collective-permute-done((bf16[128,1024]{1,0:T(8,128)(2,1)S(1)}, bf16[128,1024]{1,0:T(8,128)(2,1)S(1)}, u32[]{:S(2)}, u32[]{:S(2)}) %collective-permute-start.56) | collective-permute-done | bytes 262176 | tf_op jit(solution)/shard_map/ppermute | solution.py:42
  364.5 11.6 %attend_backward.5 = (bf16[1,160,1024]{2,1,0:T(8,128)(2,1)S(1)}, bf16[2,2,160,1024]{3,2,1,0:T(8,128)(2,1)S(1)}, bf16[2,2,160,1024]{3,2,1,0:T(8,128)(2,1)S(1)}) custom-call(s32[3,1,640]{2,1,0:T(1,128)S(1)} %reshape.453.keep_ref, bf16[4,3,160,3072]{3,2,1,0:T(8,128)(2,1)S(1)} %bitcast.341, bf16[4,3,160,3072]{3,2,1,0:T(8,128)(2,1)S(1)} %bitcast.342, ...), custom_call_target="tpu_custom_call" | custom-call | tf_op jit(solution)/shard_map/attend_backward/pallas_call | solution.py:293
  380.4 21.0 %collective-permute-done.73 = bf16[4,32,5120]{2,1,0:T(8,128)(2,1)} collective-permute-done((bf16[4,32,5120]{2,1,0:T(8,128)(2,1)}, bf16[4,32,5120]{2,1,0:T(8,128)(2,1)}, u32[]{:S(2)}, u32[]{:S(2)}) %collective-permute-start.73) | collective-permute-done | bytes 1310752 | tf_op jit(solution)/shard_map/ppermute | solution.py:39
  409.9 10.5 %collective-permute-done.59 = bf16[4,32,1024]{2,1,0:T(8,128)(2,1)S(1)} collective-permute-done((bf16[4,32,1024]{2,1,0:T(8,128)(2,1)S(1)}, bf16[4,32,1024]{2,1,0:T(8,128)(2,1)S(1)}, u32[]{:S(2)}, u32[]{:S(2)}) %collective-permute-start.59) | collective-permute-done | bytes 262176 | tf_op jit(solution)/shard_map/ppermute | solution.py:39
  422.9 11.8 %collective-permute-done.74 = bf16[4,32,5120]{2,1,0:T(8,128)(2,1)S(1)} collective-permute-done((bf16[4,32,5120]{2,1,0:T(8,128)(2,1)S(1)}, bf16[4,32,5120]{2,1,0:T(8,128)(2,1)S(1)}, u32[]{:S(2)}, u32[]{:S(2)}) %collective-permute-start.74) | collective-permute-done | bytes 1310752 | tf_op jit(solution)/shard_map/ppermute | solution.py:36
  441.7 12.3 %collective-permute-done.60 = bf16[4,32,1024]{2,1,0:T(8,128)(2,1)S(1)} collective-permute-done((bf16[4,32,1024]{2,1,0:T(8,128)(2,1)S(1)}, bf16[4,32,1024]{2,1,0:T(8,128)(2,1)S(1)}, u32[]{:S(2)}, u32[]{:S(2)}) %collective-permute-start.60) | collective-permute-done | bytes 262176 | tf_op jit(solution)/shard_map/ppermute | solution.py:36
  459.1 11.8 %collective-permute-done.77 = bf16[32,5120]{1,0:T(8,128)(2,1)S(1)} collective-permute-done((bf16[32,5120]{1,0:T(8,128)(2,1)S(1)}, bf16[32,5120]{1,0:T(8,128)(2,1)S(1)}, u32[]{:S(2)}, u32[]{:S(2)}) %collective-permute-start.77) | collective-permute-done | bytes 327712 | tf_op jit(solution)/shard_map/ppermute | solution.py:42
  477.6 6.7 %fusion.64 = (f32[1024]{0:T(1024)S(1)}, f32[1024]{0:T(1024)S(1)}, f32[480]{0:T(512)}, f32[480]{0:T(512)}, f32[480,1024]{1,0:T(8,128)}) fusion(f32[480]{0:T(512)S(1)} %rsqrt.34, f32[480]{0:T(512)S(1)} %div.65, bf16[3,160,1024]{2,1,0:T(8,128)(2,1)} %param.16, f32[480,1024]{1,0:T(8,128)S(1)} %copy-done.37, f32[1024]{0:T(1024)S(1)} %copy-done.54, ...), kind=kOutput, calls=%fused_computation.230 | convolution fusion | flops 3024811008 | bytes 14175744 | tf_op jit(solution)/shard_map/dot_general | solution.py:202
  507.6 6.9 %collective-permute-done.66 = bf16[2,32,2048]{2,1,0:T(8,128)(2,1)S(1)} collective-permute-done((bf16[2,32,2048]{2,1,0:T(8,128)(2,1)S(1)}, bf16[2,32,2048]{2,1,0:T(8,128)(2,1)S(1)}, u32[]{:S(2)}, u32[]{:S(2)}) %collective-permute-start.66) | collective-permute-done | bytes 262176 | tf_op jit(solution)/shard_map/ppermute | solution.py:39
  529.2 5.2 collective-permute-done.71
  (441 shorter events, 238.7 us)
Async XLA Ops:
  36.4 29.2 %collective-permute-start = (bf16[3,160,1024]{2,1,0:T(8,128)(2,1)}, bf16[3,160,1024]{2,1,0:T(8,128)(2,1)}, u32[]{:S(2)}, u32[]{:S(2)}) collective-permute-start(bf16[3,160,1024]{2,1,0:T(8,128)(2,1)} %param.16), channel_id=1, source_target_pairs={{0,1},{1,0},{2,3},{3,2},{4,5},{5,4},{6,7},{7,6},{8,9},{9,8},{10,11... | collective-permute-start | bytes 2949128 | tf_op jit(solution)/shard_map/ppermute | solution.py:33
  70.7 37.6 %collective-permute-start.22 = (bf16[4,32,5120]{2,1,0:T(8,128)(2,1)S(1)}, bf16[4,32,5120]{2,1,0:T(8,128)(2,1)}, u32[]{:S(2)}, u32[]{:S(2)}) collective-permute-start(bf16[4,32,5120]{2,1,0:T(8,128)(2,1)S(1)} %pad_maximum_fusion.3.refs_0_), channel_id=1, source_target_pairs={{0,2},{1,3},{2,0},{3,1},{4,6},{5,7},{6,4},{7,5},{8,10},{9,11},{10,... | collective-permute-start | bytes 3932168 | tf_op jit(solution)/shard_map/ppermute | solution.py:36
  72.2 36.1 %collective-permute-start.23 = (bf16[4,32,5120]{2,1,0:T(8,128)(2,1)S(1)}, bf16[4,32,5120]{2,1,0:T(8,128)(2,1)}, u32[]{:S(2)}, u32[]{:S(2)}) collective-permute-start(bf16[4,32,5120]{2,1,0:T(8,128)(2,1)S(1)} %pad_maximum_fusion.3.refs_0_), channel_id=1, source_target_pairs={{0,4},{4,0},{8,12},{12,8},{16,20},{20,16},{24,28},{28,24},{1,5},{5... | collective-permute-start | bytes 3932168 | tf_op jit(solution)/shard_map/ppermute | solution.py:39
  88.7 84.7 %collective-permute-start.21 = (bf16[4,32,5120]{2,1,0:T(8,128)(2,1)S(1)}, bf16[4,32,5120]{2,1,0:T(8,128)(2,1)}, u32[]{:S(2)}, u32[]{:S(2)}) collective-permute-start(bf16[4,32,5120]{2,1,0:T(8,128)(2,1)S(1)} %pad_maximum_fusion.3.refs_0_), channel_id=1, source_target_pairs={{0,1},{1,0},{2,3},{3,2},{4,5},{5,4},{6,7},{7,6},{8,9},{9,8},{10,11... | collective-permute-start | bytes 3932168 | tf_op jit(solution)/shard_map/ppermute | solution.py:33
  117.0 57.0 %collective-permute-start.24 = (bf16[4,32,5120]{2,1,0:T(8,128)(2,1)}, bf16[4,32,5120]{2,1,0:T(8,128)(2,1)}, u32[]{:S(2)}, u32[]{:S(2)}) collective-permute-start(bf16[4,32,5120]{2,1,0:T(8,128)(2,1)} %collective-permute-done.22.refs_2_), channel_id=1, source_target_pairs={{0,1},{1,0},{2,3},{3,2},{4,5},{5,4},{6,7},{7,6},{8,9},{9,8},{10,11... | collective-permute-start | bytes 3932168 | tf_op jit(solution)/shard_map/ppermute | solution.py:33
  119.3 55.9 %collective-permute-start.25 = (bf16[4,32,5120]{2,1,0:T(8,128)(2,1)}, bf16[4,32,5120]{2,1,0:T(8,128)(2,1)}, u32[]{:S(2)}, u32[]{:S(2)}) collective-permute-start(bf16[4,32,5120]{2,1,0:T(8,128)(2,1)} %collective-permute-done.23.refs_4_), channel_id=1, source_target_pairs={{0,1},{1,0},{2,3},{3,2},{4,5},{5,4},{6,7},{7,6},{8,9},{9,8},{10,11... | collective-permute-start | bytes 3932168 | tf_op jit(solution)/shard_map/ppermute | solution.py:33
  126.7 49.9 %collective-permute-start.27 = (bf16[2,32,5120]{2,1,0:T(8,128)(2,1)}, bf16[2,32,5120]{2,1,0:T(8,128)(2,1)}, u32[]{:S(2)}, u32[]{:S(2)}) collective-permute-start(bf16[2,32,5120]{2,1,0:T(8,128)(2,1)} %collective-permute-done.26.refs_6_), channel_id=1, source_target_pairs={{0,1},{1,0},{2,3},{3,2},{4,5},{5,4},{6,7},{7,6},{8,9},{9,8},{10,11... | collective-permute-start | bytes 1966088 | tf_op jit(solution)/shard_map/ppermute | solution.py:33
  128.2 48.5 %collective-permute-start.29 = (bf16[2,32,5120]{2,1,0:T(8,128)(2,1)}, bf16[2,32,5120]{2,1,0:T(8,128)(2,1)}, u32[]{:S(2)}, u32[]{:S(2)}) collective-permute-start(bf16[2,32,5120]{2,1,0:T(8,128)(2,1)} %collective-permute-done.28.refs_8_), channel_id=1, source_target_pairs={{0,1},{1,0},{2,3},{3,2},{4,5},{5,4},{6,7},{7,6},{8,9},{9,8},{10,11... | collective-permute-start | bytes 1966088 | tf_op jit(solution)/shard_map/ppermute | solution.py:33
  173.5 37.5 %collective-permute-start.33 = (bf16[4,128,1024]{2,1,0:T(8,128)(2,1)S(1)}, bf16[4,128,1024]{2,1,0:T(8,128)(2,1)S(1)}, u32[]{:S(2)}, u32[]{:S(2)}) collective-permute-start(bf16[4,128,1024]{2,1,0:T(8,128)(2,1)S(1)} %pad_maximum_fusion.4.refs_0_), channel_id=1, source_target_pairs={{0,1},{1,0},{2,3},{3,2},{4,5},{5,4},{6,7},{7,6},{8,9},{9,8},{10,11... | collective-permute-start | bytes 3145736 | tf_op jit(solution)/shard_map/ppermute | solution.py:33
  174.0 30.7 %collective-permute-start.34 = (bf16[4,128,1024]{2,1,0:T(8,128)(2,1)S(1)}, bf16[4,128,1024]{2,1,0:T(8,128)(2,1)S(1)}, u32[]{:S(2)}, u32[]{:S(2)}) collective-permute-start(bf16[4,128,1024]{2,1,0:T(8,128)(2,1)S(1)} %pad_maximum_fusion.4.refs_0_), channel_id=1, source_target_pairs={{0,2},{1,3},{2,0},{3,1},{4,6},{5,7},{6,4},{7,5},{8,10},{9,11},{10,... | collective-permute-start | bytes 3145736 | tf_op jit(solution)/shard_map/ppermute | solution.py:36
  175.1 29.7 %collective-permute-start.35 = (bf16[4,128,1024]{2,1,0:T(8,128)(2,1)S(1)}, bf16[4,128,1024]{2,1,0:T(8,128)(2,1)}, u32[]{:S(2)}, u32[]{:S(2)}) collective-permute-start(bf16[4,128,1024]{2,1,0:T(8,128)(2,1)S(1)} %pad_maximum_fusion.4.refs_0_), channel_id=1, source_target_pairs={{0,4},{4,0},{8,12},{12,8},{16,20},{20,16},{24,28},{28,24},{1,5},{5... | collective-permute-start | bytes 3145736 | tf_op jit(solution)/shard_map/ppermute | solution.py:39
  210.4 33.1 %collective-permute-start.42 = (bf16[4,2,2,128,1024]{4,3,2,1,0:T(8,128)(2,1)}, bf16[4,2,2,128,1024]{4,3,2,1,0:T(8,128)(2,1)}, u32[]{:S(2)}, u32[]{:S(2)}) collective-permute-start(bf16[4,2,2,128,1024]{4,3,2,1,0:T(8,128)(2,1)} %dynamic-slice_bitcast_fusion.1), channel_id=1, source_target_pairs={{0,1},{1,0},{2,3},{3,2},{4,5},{5,4},{6,7},{7,6},{8,9},{9,8},{10,11... | collective-permute-start | bytes 12582920 | tf_op jit(solution)/shard_map/ppermute | solution.py:33
  265.2 27.7 %collective-permute-start.46 = (bf16[4,2,2,32,4096]{4,3,2,1,0:T(8,128)(2,1)}, bf16[4,2,2,32,4096]{4,3,2,1,0:T(8,128)(2,1)}, u32[]{:S(2)}, u32[]{:S(2)}) collective-permute-start(bf16[4,2,2,32,4096]{4,3,2,1,0:T(8,128)(2,1)} %dynamic-slice_bitcast_fusion), channel_id=1, source_target_pairs={{0,1},{1,0},{2,3},{3,2},{4,5},{5,4},{6,7},{7,6},{8,9},{9,8},{10,11... | collective-permute-start | bytes 12582920 | tf_op jit(solution)/shard_map/ppermute | solution.py:33
  284.5 46.1 %collective-permute-start.53 = (bf16[4,128,1024]{2,1,0:T(8,128)(2,1)}, bf16[4,128,1024]{2,1,0:T(8,128)(2,1)}, u32[]{:S(2)}, u32[]{:S(2)}) collective-permute-start(bf16[4,128,1024]{2,1,0:T(8,128)(2,1)} %pad_maximum_fusion.5), channel_id=1, source_target_pairs={{0,2},{1,3},{2,0},{3,1},{4,6},{5,7},{6,4},{7,5},{8,10},{9,11},{10,... | collective-permute-start | bytes 3145736 | tf_op jit(solution)/shard_map/ppermute | solution.py:36
  287.9 42.7 %collective-permute-start.54 = (bf16[4,128,1024]{2,1,0:T(8,128)(2,1)}, bf16[4,128,1024]{2,1,0:T(8,128)(2,1)}, u32[]{:S(2)}, u32[]{:S(2)}) collective-permute-start(bf16[4,128,1024]{2,1,0:T(8,128)(2,1)} %pad_maximum_fusion.6), channel_id=1, source_target_pairs={{0,4},{4,0},{8,12},{12,8},{16,20},{20,16},{24,28},{28,24},{1,5},{5... | collective-permute-start | bytes 3145736 | tf_op jit(solution)/shard_map/ppermute | solution.py:39
  317.2 46.0 %collective-permute-start.47 = (bf16[2,2,160,1024]{3,2,1,0:T(8,128)(2,1)S(1)}, bf16[2,2,160,1024]{3,2,1,0:T(8,128)(2,1)S(1)}, u32[]{:S(2)}, u32[]{:S(2)}) collective-permute-start(bf16[2,2,160,1024]{3,2,1,0:T(8,128)(2,1)S(1)} %get-tuple-element.98), channel_id=1, source_target_pairs={{0,1},{1,0},{2,3},{3,2},{4,5},{5,4},{6,7},{7,6},{8,9},{9,8},{10,11... | collective-permute-start | bytes 3932168 | tf_op jit(solution)/shard_map/ppermute | solution.py:33
  328.9 47.3 %collective-permute-start.49 = (bf16[2,2,160,1024]{3,2,1,0:T(8,128)(2,1)S(1)}, bf16[2,2,160,1024]{3,2,1,0:T(8,128)(2,1)}, u32[]{:S(2)}, u32[]{:S(2)}) collective-permute-start(bf16[2,2,160,1024]{3,2,1,0:T(8,128)(2,1)S(1)} %get-tuple-element.102), channel_id=1, source_target_pairs={{0,1},{1,0},{2,3},{3,2},{4,5},{5,4},{6,7},{7,6},{8,9},{9,8},{10,11... | collective-permute-start | bytes 3932168 | tf_op jit(solution)/shard_map/ppermute | solution.py:33
  337.3 23.6 %collective-permute-start.56 = (bf16[128,1024]{1,0:T(8,128)(2,1)S(1)}, bf16[128,1024]{1,0:T(8,128)(2,1)S(1)}, u32[]{:S(2)}, u32[]{:S(2)}) collective-permute-start(bf16[128,1024]{1,0:T(8,128)(2,1)S(1)} %get-tuple-element.147), channel_id=1, source_target_pairs={{0,16},{4,20},{8,24},{12,28},{16,0},{20,4},{24,8},{28,12},{1,17},{... | collective-permute-start | bytes 786440 | tf_op jit(solution)/shard_map/ppermute | solution.py:42
  337.6 24.7 %collective-permute-start.55 = (bf16[128,1024]{1,0:T(8,128)(2,1)S(1)}, bf16[128,1024]{1,0:T(8,128)(2,1)S(1)}, u32[]{:S(2)}, u32[]{:S(2)}) collective-permute-start(bf16[128,1024]{1,0:T(8,128)(2,1)S(1)} %get-tuple-element.145), channel_id=1, source_target_pairs={{0,8},{4,12},{8,16},{12,20},{16,24},{20,28},{24,0},{28,4},{1,9},{5... | collective-permute-start | bytes 786440 | tf_op jit(solution)/shard_map/ppermute | solution.py:42
  344.0 77.8 %collective-permute-start.75 = (bf16[4,32,5120]{2,1,0:T(8,128)(2,1)}, bf16[4,32,5120]{2,1,0:T(8,128)(2,1)S(1)}, u32[]{:S(2)}, u32[]{:S(2)}) collective-permute-start(bf16[4,32,5120]{2,1,0:T(8,128)(2,1)} %fusion.25), channel_id=1, source_target_pairs={{0,4},{4,0},{8,12},{12,8},{16,20},{20,16},{24,28},{28,24},{1,5},{5... | collective-permute-start | bytes 3932168 | tf_op jit(solution)/shard_map/ppermute | solution.py:39
  360.9 40.5 %collective-permute-start.73 = (bf16[4,32,5120]{2,1,0:T(8,128)(2,1)}, bf16[4,32,5120]{2,1,0:T(8,128)(2,1)}, u32[]{:S(2)}, u32[]{:S(2)}) collective-permute-start(bf16[4,32,5120]{2,1,0:T(8,128)(2,1)} %dynamic-slice_bitcast_fusion.3), channel_id=1, source_target_pairs={{0,4},{4,0},{8,12},{12,8},{16,20},{20,16},{24,28},{28,24},{1,5},{5... | collective-permute-start | bytes 3932168 | tf_op jit(solution)/shard_map/ppermute | solution.py:39
  363.5 41.9 %collective-permute-start.48 = (bf16[2,160,1024]{2,1,0:T(8,128)(2,1)S(1)}, bf16[2,160,1024]{2,1,0:T(8,128)(2,1)S(1)}, u32[]{:S(2)}, u32[]{:S(2)}) collective-permute-start(bf16[2,160,1024]{2,1,0:T(8,128)(2,1)S(1)} %fusion.34), channel_id=1, source_target_pairs={{0,2},{1,3},{2,0},{3,1},{4,6},{5,7},{6,4},{7,5},{8,10},{9,11},{10,... | collective-permute-start | bytes 1966088 | tf_op jit(solution)/shard_map/ppermute | solution.py:36
  376.1 32.3 %collective-permute-start.51 = (bf16[2,2,160,1024]{3,2,1,0:T(8,128)(2,1)S(1)}, bf16[2,2,160,1024]{3,2,1,0:T(8,128)(2,1)S(1)}, u32[]{:S(2)}, u32[]{:S(2)}) collective-permute-start(bf16[2,2,160,1024]{3,2,1,0:T(8,128)(2,1)S(1)} %get-tuple-element.104), channel_id=1, source_target_pairs={{0,1},{1,0},{2,3},{3,2},{4,5},{5,4},{6,7},{7,6},{8,9},{9,8},{10,11... | collective-permute-start | bytes 3932168 | tf_op jit(solution)/shard_map/ppermute | solution.py:33
  377.7 25.4 %collective-permute-start.50 = (bf16[2,160,1024]{2,1,0:T(8,128)(2,1)S(1)}, bf16[2,160,1024]{2,1,0:T(8,128)(2,1)S(1)}, u32[]{:S(2)}, u32[]{:S(2)}) collective-permute-start(bf16[2,160,1024]{2,1,0:T(8,128)(2,1)S(1)} %fusion.35), channel_id=1, source_target_pairs={{0,2},{1,3},{2,0},{3,1},{4,6},{5,7},{6,4},{7,5},{8,10},{9,11},{10,... | collective-permute-start | bytes 1966088 | tf_op jit(solution)/shard_map/ppermute | solution.py:36
  403.0 31.6 %collective-permute-start.74 = (bf16[4,32,5120]{2,1,0:T(8,128)(2,1)S(1)}, bf16[4,32,5120]{2,1,0:T(8,128)(2,1)S(1)}, u32[]{:S(2)}, u32[]{:S(2)}) collective-permute-start(bf16[4,32,5120]{2,1,0:T(8,128)(2,1)S(1)} %fusion.12), channel_id=1, source_target_pairs={{0,2},{1,3},{2,0},{3,1},{4,6},{5,7},{6,4},{7,5},{8,10},{9,11},{10,... | collective-permute-start | bytes 3932168 | tf_op jit(solution)/shard_map/ppermute | solution.py:36
  406.3 34.7 %collective-permute-start.61 = (bf16[4,32,1024]{2,1,0:T(8,128)(2,1)S(1)}, bf16[4,32,1024]{2,1,0:T(8,128)(2,1)S(1)}, u32[]{:S(2)}, u32[]{:S(2)}) collective-permute-start(bf16[4,32,1024]{2,1,0:T(8,128)(2,1)S(1)} %get-tuple-element.144), channel_id=1, source_target_pairs={{0,4},{4,0},{8,12},{12,8},{16,20},{20,16},{24,28},{28,24},{1,5},{5... | collective-permute-start | bytes 786440 | tf_op jit(solution)/shard_map/ppermute | solution.py:39
  408.7 62.6 %collective-permute-start.52 = (bf16[2,160,1024]{2,1,0:T(8,128)(2,1)S(1)}, bf16[2,160,1024]{2,1,0:T(8,128)(2,1)S(1)}, u32[]{:S(2)}, u32[]{:S(2)}) collective-permute-start(bf16[2,160,1024]{2,1,0:T(8,128)(2,1)S(1)} %fusion.36), channel_id=1, source_target_pairs={{0,2},{1,3},{2,0},{3,1},{4,6},{5,7},{6,4},{7,5},{8,10},{9,11},{10,... | collective-permute-start | bytes 1966088 | tf_op jit(solution)/shard_map/ppermute | solution.py:36
  420.5 33.4 %collective-permute-start.60 = (bf16[4,32,1024]{2,1,0:T(8,128)(2,1)S(1)}, bf16[4,32,1024]{2,1,0:T(8,128)(2,1)S(1)}, u32[]{:S(2)}, u32[]{:S(2)}) collective-permute-start(bf16[4,32,1024]{2,1,0:T(8,128)(2,1)S(1)} %fusion.41), channel_id=1, source_target_pairs={{0,2},{1,3},{2,0},{3,1},{4,6},{5,7},{6,4},{7,5},{8,10},{9,11},{10,... | collective-permute-start | bytes 786440 | tf_op jit(solution)/shard_map/ppermute | solution.py:36
  441.0 29.8 %collective-permute-start.77 = (bf16[32,5120]{1,0:T(8,128)(2,1)S(1)}, bf16[32,5120]{1,0:T(8,128)(2,1)S(1)}, u32[]{:S(2)}, u32[]{:S(2)}) collective-permute-start(bf16[32,5120]{1,0:T(8,128)(2,1)S(1)} %get-tuple-element.142), channel_id=1, source_target_pairs={{0,16},{4,20},{8,24},{12,28},{16,0},{20,4},{24,8},{28,12},{1,17},{... | collective-permute-start | bytes 983048 | tf_op jit(solution)/shard_map/ppermute | solution.py:42
  441.0 30.1 %collective-permute-start.76 = (bf16[32,5120]{1,0:T(8,128)(2,1)S(1)}, bf16[32,5120]{1,0:T(8,128)(2,1)S(1)}, u32[]{:S(2)}, u32[]{:S(2)}) collective-permute-start(bf16[32,5120]{1,0:T(8,128)(2,1)S(1)} %get-tuple-element.140), channel_id=1, source_target_pairs={{0,8},{4,12},{8,16},{12,20},{16,24},{20,28},{24,0},{28,4},{1,9},{5... | collective-permute-start | bytes 983048 | tf_op jit(solution)/shard_map/ppermute | solution.py:42
  454.8 31.2 %collective-permute-start.64 = (bf16[32,1024]{1,0:T(8,128)(2,1)}, bf16[32,1024]{1,0:T(8,128)(2,1)S(1)}, u32[]{:S(2)}, u32[]{:S(2)}) collective-permute-start(bf16[32,1024]{1,0:T(8,128)(2,1)} %get-tuple-element.158), channel_id=1, source_target_pairs={{0,24},{4,28},{8,0},{12,4},{16,8},{20,12},{24,16},{28,20},{1,25},{... | collective-permute-start | bytes 196616 | tf_op jit(solution)/shard_map/ppermute | solution.py:42
  459.1 26.9 %collective-permute-start.63 = (bf16[32,1024]{1,0:T(8,128)(2,1)}, bf16[32,1024]{1,0:T(8,128)(2,1)}, u32[]{:S(2)}, u32[]{:S(2)}) collective-permute-start(bf16[32,1024]{1,0:T(8,128)(2,1)} %get-tuple-element.159), channel_id=1, source_target_pairs={{0,16},{4,20},{8,24},{12,28},{16,0},{20,4},{24,8},{28,12},{1,17},{... | collective-permute-start | bytes 196616 | tf_op jit(solution)/shard_map/ppermute | solution.py:42
  (118 other events, 1357.7 us)
